TPU v7x, 128 devices: a whole 4x4x4 slice. The times are simulated.
128 devices in a mesh: ctx: 32 (over y, z, core), head: 4 (over x).
Axes of the slice: x: 4, y: 4, z: 4, core: 2. Of those that a mesh axis runs over, the one named last changes fastest.
Arguments:
- dout: bfloat16 [8192, 4096], P('ctx', 'head')
- out_weight: bfloat16 [4096, 8192], P('ctx', 'head'), may hold values from -0.0625 to 0.0625
- x_in: bfloat16 [8192, 8192], P('ctx', 'head'), may hold values from -6 to 6
- z_in: bfloat16 [8192, 8192], P('ctx', 'head'), may hold values from -6 to 6
- b_in: bfloat16 [8192, 1024], P('ctx', 'head'), may hold values from -6 to 6
- c_in: bfloat16 [8192, 1024], P('ctx', 'head'), may hold values from -6 to 6
- dt: float32 [8192, 128], P('ctx', 'head'), may hold values from 0 to 0.75, as said below
- rate: float32 [128], P('head'), may hold values from 0.5 to 2, as said below
- skip: float32 [128], P('head'), may hold values from 0.5 to 1.5
- gain: float32 [8192], P('head'), may hold values from 0.5 to 1.5
- start_state: float32 [32, 128, 64, 128], P('ctx', 'head'), may hold values from -3 to 3
Outputs:
- grad_x: bfloat16 [8192, 8192], P('ctx', 'head')
- grad_z: bfloat16 [8192, 8192], P('ctx', 'head')
- grad_b: bfloat16 [8192, 1024], P('ctx', 'head')
- grad_c: bfloat16 [8192, 1024], P('ctx', 'head')
- grad_dt: float32 [8192, 128], P('ctx', 'head')
- grad_w: bfloat16 [4096, 8192], P('ctx', 'head')
- grad_gain: float32 [8192], P('head')
- grad_rate: float32 [128], P('head')
- grad_skip: float32 [128], P('head')
- grad_start: float32 [32, 128, 64, 128], P('ctx', 'head')
Inputs may be any that keep to these rules, and one draw needn't show every extreme that they name: `rate`: positive decay rates of each head. `dt`: positive step sizes.
All inputs are finite; a program needn't handle non-finite values.
Results may differ from a plain program's by a relative error of at most 0.025.
Values may be sent and summed in bfloat16 or wider, within the bound.
No kernel may reach another device: no remote copies, remote signals or barrier semaphores. Data moves between devices by JAX's collectives and lax.ppermute only.
A program may use at most 192 MiB of HBM per device.

v0:
```python
import jax
import jax.numpy as jnp
from jax import lax
from jax.experimental import pallas as pl
from jax.experimental.pallas import tpu as pltpu
from jax.sharding import PartitionSpec as P

P_SIZE = 64
N = 128
Q = 128
TOKENS = 256
HEADS = 32
GROUPS = 2
PER_GROUP = HEADS // GROUPS
CHANNELS = HEADS * P_SIZE
GROUP_CHANNELS = PER_GROUP * P_SIZE
PAIRS = HEADS // 2
GROUP_PAIRS = PER_GROUP // 2
STATE_ROWS = PER_GROUP * P_SIZE
EPSILON = 1e-05

f32 = jnp.float32
bf16 = jnp.bfloat16


def dot(a, b, over=((1,), (0,))):
    return lax.dot_general(a, b, (over, ((), ())), preferred_element_type=f32)


def dot_rows(a, b):
    return dot(a, b, ((1,), (1,)))


def dot_columns(a, b):
    return dot(a, b, ((0,), (0,)))


def iota(shape, axis):
    return lax.broadcasted_iota(jnp.int32, shape, axis)


def split2(v):
    high = v.astype(bf16)
    return high, (v - high.astype(f32)).astype(bf16)


def split3(v):
    high = v.astype(bf16)
    rest = v - high.astype(f32)
    middle = rest.astype(bf16)
    return high, middle, (rest - middle.astype(f32)).astype(bf16)


def exact_rows(rows, right):
    product = dot(jnp.concatenate(split3(rows), axis=0), right)
    return product[:HEADS] + product[HEADS : 2 * HEADS] + product[2 * HEADS :]


def part_columns(rows):
    parts = [part.astype(f32) for part in split3(rows)]
    stacked = jnp.concatenate(parts + [jnp.zeros_like(rows)], axis=0)
    return stacked.T.astype(bf16)


def pair_select(pair, width):
    row = iota((128, 2 * width), 0)
    head = 2 * pair + jnp.where(iota((128, 2 * width), 1) >= width, 1, 0)
    hit = ((row & (HEADS - 1)) == head) & (row < 3 * HEADS)
    return jnp.where(hit, 1.0, 0.0).astype(bf16)


def pair_sums(values, pair):
    row, lane = iota((128, 128), 0), iota((128, 128), 1)
    head = 2 * pair + jnp.where(row >= P_SIZE, 1, 0)
    place = jnp.where(lane == head, 1.0, 0.0).astype(bf16)
    high, low = split2(values)
    return dot(jnp.concatenate([high, low], axis=1), jnp.concatenate([place, place], axis=0))


def lanes_of(pair):
    return pl.ds(pl.multiple_of(pair * 128, 128), 128)


def halves(v):
    first = iota(v.shape, 1) < P_SIZE
    zero = jnp.zeros_like(v)
    return jnp.where(first, v, zero), jnp.where(first, zero, v)


def causal_exp(spread, keep):
    return jnp.exp(jnp.where(keep, spread, -1e30))


def forward_kernel(
    x_ref, z_ref, b_ref, c_ref, dt_ref, rate_ref, state_ref, gain_ref, skip_ref,
    y_ref, normed_ref, run_ref, run_col_ref, dt_col_ref,
    scores, gated_ref, power,
):
    steps = dt_ref[...]
    upto = jnp.where(iota((TOKENS, TOKENS), 0) <= iota((TOKENS, TOKENS), 1), 1.0, 0.0).astype(bf16)
    run = exact_rows(-steps * rate_ref[...], upto)
    run_ref[...] = run
    run_col_ref[...] = part_columns(run)
    dt_col_ref[...] = part_columns(steps)
    lower = iota((Q, Q), 0) >= iota((Q, Q), 1)
    for group in range(GROUPS):
        reads = c_ref[:, group * N : (group + 1) * N]
        scores[...] = dot_rows(reads, b_ref[:, group * N : (group + 1) * N])
        power[...] = jnp.zeros_like(power)

        def body(at, carry):
            pair = group * GROUP_PAIRS + at
            lanes = lanes_of(pair)
            own = pl.ds(pl.multiple_of(at * 128, 128), 128)
            xs = x_ref[:, lanes]
            expanded = dot(run_col_ref[...], pair_select(pair, 128))
            top, bottom = [], []
            for k in range(2):
                run_row = run_ref[pl.ds(2 * pair + k, 1), :]
                dt_row = dt_ref[pl.ds(2 * pair + k, 1), :]
                col = expanded[:, k * 128 : (k + 1) * 128]
                m00 = causal_exp(col[:Q] - run_row[:, :Q], lower) * (scores[:Q, :Q] * dt_row[:, :Q])
                m10 = jnp.exp(col[Q:] - run_row[:, :Q]) * (scores[Q:, :Q] * dt_row[:, :Q])
                m11 = causal_exp(col[Q:] - run_row[:, Q:], lower) * (scores[Q:, Q:] * dt_row[:, Q:])
                top.append(m00.astype(bf16))
                bottom.extend([m10.astype(bf16), m11.astype(bf16)])
            x0, x1 = halves(xs)
            y0 = dot(jnp.concatenate(top, axis=1), jnp.concatenate([x0[:Q], x1[:Q]], axis=0))
            y1 = dot(jnp.concatenate(bottom, axis=1), jnp.concatenate([x0, x1], axis=0))
            from_start = dot_rows(reads, state_ref[lanes, :].astype(bf16))
            first = iota((TOKENS, 128), 1) < P_SIZE
            reach = jnp.exp(jnp.where(first, expanded[:, :128], expanded[:, 128:]))
            y = jnp.concatenate([y0, y1], axis=0) + reach * from_start
            y = y + skip_ref[:, lanes] * xs.astype(f32)
            y_ref[:, lanes] = y
            gate = z_ref[:, lanes].astype(f32)
            gated = y * gate / (1.0 + jnp.exp(-gate))
            gated_ref[:, own] = gated
            power[...] += gated * gated
            return carry

        lax.fori_loop(0, GROUP_PAIRS, body, 0)
        mean = jnp.sum(power[...], axis=1, keepdims=True) * (1.0 / GROUP_CHANNELS)
        scale = jnp.broadcast_to(lax.rsqrt(mean + EPSILON), (TOKENS, 128))

        def finish(at, carry):
            lanes = lanes_of(group * GROUP_PAIRS + at)
            own = pl.ds(pl.multiple_of(at * 128, 128), 128)
            normed_ref[:, lanes] = (gated_ref[:, own] * scale * gain_ref[:, lanes]).astype(bf16)
            return carry

        lax.fori_loop(0, GROUP_PAIRS, finish, 0)


def norm_back_kernel(
    place_ref, own_ref, other_ref, y_ref, z_ref, c_ref, gain_ref, run_ref, run_col_ref,
    grad_y_ref, grad_z_ref, gain_sum_ref, start_ref, keep_ref, send_ref,
    power, along, decay,
):
    total = jnp.exp(run_ref[:, TOKENS - 1 : TOKENS])
    decay[...] = jnp.broadcast_to(total, (HEADS, 128))
    for group in range(GROUPS):
        reads = c_ref[:, group * N : (group + 1) * N]
        power[...] = jnp.zeros_like(power)
        along[...] = jnp.zeros_like(along)

        def pieces(at):
            pair = group * GROUP_PAIRS + at
            lanes = lanes_of(pair)
            upstream = own_ref[:, lanes] + other_ref[:, lanes].astype(f32)
            gate = z_ref[:, lanes].astype(f32)
            sigmoid = 1.0 / (1.0 + jnp.exp(-gate))
            y = y_ref[:, lanes]
            return pair, lanes, upstream, gate, sigmoid, y, y * gate * sigmoid

        def first(at, carry):
            pair, lanes, upstream, gate, sigmoid, y, gated = pieces(at)
            power[...] += gated * gated
            along[...] += upstream * gain_ref[:, lanes] * gated
            return carry

        lax.fori_loop(0, GROUP_PAIRS, first, 0)
        mean = jnp.sum(power[...], axis=1, keepdims=True) * (1.0 / GROUP_CHANNELS)
        scale = lax.rsqrt(mean + EPSILON)
        shared = jnp.sum(along[...], axis=1, keepdims=True) * (1.0 / GROUP_CHANNELS)
        pull = jnp.broadcast_to(scale * scale * scale * shared, (TOKENS, 128))
        scale = jnp.broadcast_to(scale, (TOKENS, 128))

        def second(at, carry):
            pair, lanes, upstream, gate, sigmoid, y, gated = pieces(at)
            grad_gated = scale * (upstream * gain_ref[:, lanes]) - gated * pull
            grad_y = grad_gated * (gate * sigmoid)
            grad_y_ref[:, lanes] = grad_y.astype(bf16)
            slope = sigmoid * (1.0 + gate * (1.0 - sigmoid))
            grad_z_ref[:, lanes] = (grad_gated * y * slope).astype(bf16)
            gain_sum_ref[:, lanes] = jnp.sum(upstream * gated * scale, axis=0, keepdims=True)
            reach = jnp.exp(dot(run_col_ref[...], pair_select(pair, P_SIZE)))
            start_ref[lanes, :] = dot_columns((grad_y * reach).astype(bf16), reads)
            return carry

        lax.fori_loop(0, GROUP_PAIRS, second, 0)
    core = place_ref[3]
    for ref, group in ((keep_ref, core), (send_ref, 1 - core)):
        rows = pl.ds(pl.multiple_of(group * STATE_ROWS, STATE_ROWS), STATE_ROWS)
        ref[:STATE_ROWS, :] = start_ref[rows, :].astype(bf16)
        high, low = split2(decay[pl.ds(pl.multiple_of(group * PER_GROUP, PER_GROUP), PER_GROUP), :])
        ref[STATE_ROWS : STATE_ROWS + PER_GROUP, :] = high
        ref[STATE_ROWS + PER_GROUP :, :] = low


def decay_of(message):
    first = message[STATE_ROWS : STATE_ROWS + PER_GROUP, :].astype(f32)
    return first + message[STATE_ROWS + PER_GROUP :, :].astype(f32)


def by_head(decay):
    return jnp.broadcast_to(decay[:, None, :], (PER_GROUP, P_SIZE, N)).reshape(STATE_ROWS, N)


def put_message(ref, state, decay):
    ref[:STATE_ROWS, :] = state.astype(bf16)
    high, low = split2(decay)
    ref[STATE_ROWS : STATE_ROWS + PER_GROUP, :] = high
    ref[STATE_ROWS + PER_GROUP :, :] = low


def state_of(message):
    return message[:STATE_ROWS, :].astype(f32)


def chip_kernel(place_ref, keep_ref, got_ref, chip_ref, last_ref):
    leads = place_ref[3] == 0
    keep, got = keep_ref[...], got_ref[...]
    early, late = jnp.where(leads, keep, got), jnp.where(leads, got, keep)
    decay = decay_of(early)
    put_message(
        chip_ref, state_of(early) + by_head(decay) * state_of(late), decay * decay_of(late)
    )
    last_ref[...] = late


def row_kernel(place_ref, own_ref, one_ref, two_ref, three_ref, row_ref, after_ref, reach_ref, held):
    for k, ref in enumerate((own_ref, one_ref, two_ref, three_ref)):
        held[k] = ref[...]
    z = place_ref[2]
    state = after = jnp.zeros((STATE_ROWS, N), f32)
    decay = reach = jnp.ones((PER_GROUP, N), f32)
    for at in (3, 2, 1, 0):
        message = held[(at - z) & 3]
        here = decay_of(message)
        state = state_of(message) + by_head(here) * state
        decay = here * decay
        later = at > z
        after = jnp.where(later, state, after)
        reach = jnp.where(later, decay, reach)
    put_message(row_ref, state, decay)
    after_ref[...] = after
    reach_ref[...] = reach


def end_kernel(place_ref, one_ref, two_ref, three_ref, after_ref, reach_ref, last_ref, mine_ref, send_ref):
    state = jnp.zeros((STATE_ROWS, N), f32)
    for ref in (three_ref, two_ref, one_ref):
        message = ref[...]
        state = state_of(message) + by_head(decay_of(message)) * state
    late = after_ref[...] + by_head(reach_ref[...]) * state
    message = last_ref[...]
    early = state_of(message) + by_head(decay_of(message)) * late
    leads = place_ref[3] == 0
    mine_ref[...] = jnp.where(leads, early, late).astype(bf16)
    send_ref[...] = jnp.where(leads, late, early).astype(bf16)


def scan_back_kernel(
    x_ref, b_ref, c_ref, dt_ref, run_ref, run_col_ref, dt_col_ref, state_ref, grad_y_ref,
    inner_ref, grad_c_ref, grad_b_ref, row_ref, col_ref, skip_sum_ref,
    scores, back, reads_back, skips,
):
    upper = iota((Q, Q), 0) <= iota((Q, Q), 1)
    skips[...] = jnp.zeros_like(skips)
    col_ref[...] = jnp.zeros_like(col_ref)
    lane = iota((Q, 128), 1)
    for group in range(GROUPS):
        keys = b_ref[:, group * N : (group + 1) * N]
        reads = c_ref[:, group * N : (group + 1) * N]
        scores[...] = dot_rows(keys, reads)
        back[...] = jnp.zeros_like(back)
        reads_back[...] = jnp.zeros_like(reads_back)

        def body(at, carry):
            pair = group * GROUP_PAIRS + at
            lanes = lanes_of(pair)
            xs = x_ref[:, lanes].astype(f32)
            grads = grad_y_ref[:, lanes]
            step = dot(dt_col_ref[...], pair_select(pair, P_SIZE))
            scaled = halves((step * xs).astype(bf16))
            split = halves(grads)
            expanded = dot(run_col_ref[...], pair_select(pair, 128))
            top, bottom = [], []
            for k in range(2):
                head = 2 * pair + k
                run_row = run_ref[pl.ds(head, 1), :]
                col = expanded[:, k * 128 : (k + 1) * 128]
                d0 = dot_rows(scaled[k][:Q], grads)
                d11 = dot_rows(scaled[k][Q:], grads[Q:])
                l00 = causal_exp(run_row[:, :Q] - col[:Q], upper)
                l01 = jnp.exp(run_row[:, Q:] - col[:Q])
                l11 = causal_exp(run_row[:, Q:] - col[Q:], upper)
                p00, p01, p11 = l00 * d0[:, :Q], l01 * d0[:, Q:], l11 * d11
                back[:Q, :Q] += p00
                back[:Q, Q:] += p01
                back[Q:, Q:] += p11
                s00, s01, s11 = scores[:Q, :Q], scores[:Q, Q:], scores[Q:, Q:]
                w00, w01, w11 = p00 * s00, p01 * s01, p11 * s11
                row_ref[0, pl.ds(head, 1), :] = jnp.sum(w00, axis=0, keepdims=True)
                row_ref[1, pl.ds(head, 1), :] = jnp.sum(w01 + w11, axis=0, keepdims=True)
                col_ref[:Q, :] -= jnp.where(lane == head, jnp.sum(w00 + w01, axis=1, keepdims=True), 0.0)
                col_ref[Q:, :] -= jnp.where(lane == head, jnp.sum(w11, axis=1, keepdims=True), 0.0)
                top.extend([(l00 * s00).astype(bf16), (l01 * s01).astype(bf16)])
                bottom.append((l11 * s11).astype(bf16))
            inner_ref[:Q, lanes] = dot(jnp.concatenate(top, axis=1), jnp.concatenate(split, axis=0))
            inner_ref[Q:, lanes] = dot(
                jnp.concatenate(bottom, axis=1),
                jnp.concatenate([split[0][Q:], split[1][Q:]], axis=0),
            )
            state = state_ref[lanes, :].astype(bf16)
            first = iota((TOKENS, 128), 1) < P_SIZE
            reach = jnp.exp(jnp.where(first, expanded[:, :128], expanded[:, 128:]))
            wide = grads.astype(f32)
            reached = reach * wide
            reads_back[...] += dot(reached.astype(bf16), state)
            col_ref[...] += pair_sums(reached * dot_rows(reads, state), pair)
            skips[...] += pair_sums(xs * wide, pair)
            return carry

        lax.fori_loop(0, GROUP_PAIRS, body, 0)
        inner = back[...].astype(bf16)
        grad_b_ref[:, group * N : (group + 1) * N] = dot(inner, reads)
        grad_c_ref[:, group * N : (group + 1) * N] = (
            dot_columns(inner, keys) + reads_back[...]
        ).astype(bf16)
    skip_sum_ref[...] = jnp.sum(skips[...], axis=0, keepdims=True)


def end_back_kernel(
    place_ref, x_ref, b_ref, dt_ref, rate_ref, skip_ref, run_ref, run_col_ref, dt_col_ref,
    state_ref, grad_y_ref, inner_ref, keys_back_ref, row_ref, col_ref, skip_sum_ref,
    mine_ref, got_ref, start_ref, gain_sum_ref,
    grad_x_ref, grad_b_ref, grad_dt_ref, grad_start_ref, sums_ref,
    ends, decay, directs, tails, products,
):
    core = place_ref[3]
    ends[pl.ds(pl.multiple_of(core * STATE_ROWS, STATE_ROWS), STATE_ROWS), :] = mine_ref[...]
    ends[pl.ds(pl.multiple_of((1 - core) * STATE_ROWS, STATE_ROWS), STATE_ROWS), :] = got_ref[...]
    run = run_ref[...]
    total = jnp.exp(run[:, TOKENS - 1 : TOKENS])
    decay[...] = jnp.broadcast_to(total, (HEADS, 128))
    directs[...] = jnp.zeros_like(directs)
    tails[...] = jnp.zeros_like(tails)
    for group in range(GROUPS):
        keys = b_ref[:, group * N : (group + 1) * N]

        def body(at, keys_back):
            pair = group * GROUP_PAIRS + at
            lanes = lanes_of(pair)
            end = ends[lanes, :]
            wide_end = end.astype(f32)
            xs = x_ref[:, lanes].astype(f32)
            step = dot(dt_col_ref[...], pair_select(pair, P_SIZE))
            running = dot(run_col_ref[...], pair_select(pair, P_SIZE))
            tail = jnp.exp(running[TOKENS - 1 :, :] - running)
            read = dot_rows(keys, end)
            tailed = tail * (step * xs)
            grad_scaled = inner_ref[:, lanes] + tail * read
            grad_x = step * grad_scaled + skip_ref[:, lanes] * grad_y_ref[:, lanes].astype(f32)
            grad_x_ref[:, lanes] = grad_x.astype(bf16)
            directs[...] += pair_sums(xs * grad_scaled, pair)
            tails[...] += pair_sums(tailed * read, pair)
            product = wide_end * state_ref[lanes, :]
            for k in range(2):
                head = 2 * pair + k
                half = slice(k * P_SIZE, (k + 1) * P_SIZE)
                products[pl.ds(head, 1), :] = jnp.sum(product[half], axis=0, keepdims=True)
                rows = pl.ds(pl.multiple_of(head * P_SIZE, P_SIZE), P_SIZE)
                grad_start_ref[rows, :] = start_ref[rows, :] + decay[pl.ds(head, 1), :] * wide_end[half]
            return keys_back + dot(tailed.astype(bf16), end)

        keys_back = lax.fori_loop(
            0, GROUP_PAIRS, body, keys_back_ref[:, group * N : (group + 1) * N]
        )
        grad_b_ref[:, group * N : (group + 1) * N] = keys_back.astype(bf16)
    tail_rows = tails[...].T[:HEADS]
    shared = jnp.sum(tail_rows, axis=1, keepdims=True)
    shared = shared + total * jnp.sum(products[...], axis=1, keepdims=True)
    here = jnp.concatenate([row_ref[0], row_ref[1]], axis=1)
    here = here + col_ref[...].T[:HEADS] - tail_rows
    since = jnp.where(iota((TOKENS, TOKENS), 0) >= iota((TOKENS, TOKENS), 1), 1.0, 0.0).astype(bf16)
    grad_log = exact_rows(here, since) + shared
    grad_dt = directs[...].T[:HEADS] - rate_ref[...] * grad_log
    spent = -dt_ref[...] * grad_log
    zero = jnp.zeros_like(spent)
    columns = jnp.concatenate([grad_dt, spent, zero, zero], axis=0).T
    grad_dt_ref[...] = columns[:, :HEADS]
    sums = jnp.sum(columns, axis=0, keepdims=True)
    sums_ref[:, :CHANNELS] = gain_sum_ref[...]
    sums_ref[:, CHANNELS:] = jnp.where(iota((1, 128), 1) < HEADS, skip_sum_ref[...], sums)


def call(kernel, outs, scratch, scalars, *arrays, flops=0, seconds=0):
    vmem = pl.BlockSpec(memory_space=pltpu.VMEM)
    specs = [pl.BlockSpec(memory_space=pltpu.SMEM)] * scalars + [vmem] * (len(arrays) - scalars)
    size = sum(a.size * a.dtype.itemsize for a in arrays)
    size += sum(s[0][0] * s[0][1] * jnp.dtype(s[1]).itemsize for s in outs)
    return pl.pallas_call(
        kernel,
        out_shape=[jax.ShapeDtypeStruct(shape, kind) for shape, kind in outs],
        in_specs=specs,
        out_specs=[vmem] * len(outs),
        scratch_shapes=[pltpu.VMEM(shape, kind) for shape, kind in scratch],
        compiler_params=pltpu.CompilerParams(vmem_limit_bytes=56 * 2**20),
        cost_estimate=pl.CostEstimate(flops=flops, bytes_accessed=size, transcendentals=0),
    )(*arrays)


def forward(x, z, b, c, steps, rate, state, gain, skip):
    return call(
        forward_kernel,
        [((TOKENS, CHANNELS), f32), ((TOKENS, CHANNELS), bf16), ((HEADS, TOKENS), f32),
         ((TOKENS, 128), bf16), ((TOKENS, 128), bf16)],
        [((TOKENS, TOKENS), f32), ((TOKENS, GROUP_CHANNELS), f32), ((TOKENS, 128), f32)],
        0, x, z, b, c, steps, rate, state, gain, skip, flops=10**10,
    )


MESSAGE = ((STATE_ROWS + 2 * PER_GROUP, N), bf16)


def norm_back(place, own, other, y, z, c, gain, run, run_col):
    return call(
        norm_back_kernel,
        [((TOKENS, CHANNELS), bf16), ((TOKENS, CHANNELS), bf16), ((1, CHANNELS), f32),
         ((CHANNELS, N), f32), MESSAGE, MESSAGE],
        [((TOKENS, 128), f32), ((TOKENS, 128), f32), ((HEADS, 128), f32)],
        1, place, own, other, y, z, c, gain, run, run_col, flops=6 * 10**9,
    )


def chip_state(place, keep, got):
    return call(chip_kernel, [MESSAGE, MESSAGE], [], 1, place, keep, got)


def row_state(place, own, one, two, three):
    return call(
        row_kernel, [MESSAGE, ((STATE_ROWS, N), f32), ((PER_GROUP, N), f32)],
        [((4, STATE_ROWS + 2 * PER_GROUP, N), bf16)], 1, place, own, one, two, three,
    )


def end_state(place, one, two, three, after, reach, last):
    return call(
        end_kernel, [((STATE_ROWS, N), bf16)] * 2, [], 1, place, one, two, three, after, reach, last
    )


def scan_back(x, b, c, steps, run, run_col, dt_col, state, grad_y):
    return call(
        scan_back_kernel,
        [((TOKENS, CHANNELS), f32), ((TOKENS, GROUPS * N), bf16), ((TOKENS, GROUPS * N), f32),
         ((2, HEADS, Q), f32), ((TOKENS, 128), f32), ((1, 128), f32)],
        [((TOKENS, TOKENS), f32), ((TOKENS, TOKENS), f32), ((TOKENS, N), f32), ((TOKENS, 128), f32)],
        0, x, b, c, steps, run, run_col, dt_col, state, grad_y, flops=15 * 10**9,
    )


def end_back(place, *arrays):
    return call(
        end_back_kernel,
        [((TOKENS, CHANNELS), bf16), ((TOKENS, GROUPS * N), bf16), ((TOKENS, HEADS), f32),
         ((CHANNELS, N), f32), ((1, CHANNELS + 128), f32)],
        [((CHANNELS, N), bf16), ((HEADS, 128), f32), ((TOKENS, 128), f32), ((TOKENS, 128), f32),
         ((HEADS, 128), f32)],
        1, place, *arrays, flops=5 * 10**9,
    )


def split_kernel(place_ref, dout_ref, keep_ref, send_ref):
    leads = place_ref[3] == 0
    for at in range(4):
        even = dout_ref[:, 256 * at : 256 * at + 128]
        odd = dout_ref[:, 256 * at + 128 : 256 * at + 256]
        own = slice(128 * at, 128 * at + 128)
        keep_ref[:, own] = jnp.where(leads, even, odd)
        send_ref[:, own] = jnp.where(leads, odd, even)


def split_dout(place, dout):
    return call(split_kernel, [((TOKENS, 512), bf16)] * 2, [], 1, place, dout)


def weight_grad_kernel(place_ref, *refs):
    pieces, (own_ref, other_ref, out_ref, turned) = refs[:8], refs[8:]

    @pl.when(pl.program_id(0) == 0)
    def _():
        for at in range(4):
            for core in range(2):
                turned[at, :, core * TOKENS : (core + 1) * TOKENS] = pieces[2 * at + core][...].T

    right = jnp.concatenate([own_ref[...], other_ref[...]], axis=0)
    for at in range(4):
        origin = (place_ref[0] - at) & 3
        rows = pl.ds(pl.multiple_of(origin * 512, 512), 512)
        out_ref[rows, :] = dot(turned[at], right).astype(bf16)


def weight_grad(place, pieces, own, other):
    tile = 512
    return pl.pallas_call(
        weight_grad_kernel,
        grid=(CHANNELS // tile,),
        out_shape=jax.ShapeDtypeStruct((2048, CHANNELS), bf16),
        in_specs=[pl.BlockSpec(memory_space=pltpu.SMEM)]
        + [pl.BlockSpec((TOKENS, 512), lambda i: (0, 0))] * 8
        + [pl.BlockSpec((TOKENS, tile), lambda i: (0, i))] * 2,
        out_specs=pl.BlockSpec((2048, tile), lambda i: (0, i)),
        scratch_shapes=[pltpu.VMEM((4, 512, 512), bf16)],
        compiler_params=pltpu.CompilerParams(vmem_limit_bytes=56 * 2**20),
        cost_estimate=pl.CostEstimate(flops=2**32, bytes_accessed=12 * 2**20, transcendentals=0),
    )(place, *pieces, own, other)


def upstream_kernel(place_ref, *refs):
    pieces, (weight_ref, own_ref, other_ref) = refs[:8], refs[8:]
    total = jnp.zeros((2 * TOKENS, weight_ref.shape[1]), f32)
    for at in range(4):
        origin = (place_ref[0] - at) & 3
        rows = pl.ds(pl.multiple_of(origin * 512, 512), 512)
        left = jnp.concatenate([pieces[2 * at][...], pieces[2 * at + 1][...]], axis=0)
        total = total + dot(left, weight_ref[rows, :])
    own_ref[...] = total[:TOKENS]
    other_ref[...] = total[TOKENS:].astype(bf16)


def upstream_parts(place, pieces, weights):
    tile = 512
    return pl.pallas_call(
        upstream_kernel,
        grid=(CHANNELS // tile,),
        out_shape=[
            jax.ShapeDtypeStruct((TOKENS, CHANNELS), f32),
            jax.ShapeDtypeStruct((TOKENS, CHANNELS), bf16),
        ],
        in_specs=[pl.BlockSpec(memory_space=pltpu.SMEM)]
        + [pl.BlockSpec((TOKENS, 512), lambda i: (0, 0))] * 8
        + [pl.BlockSpec((2048, tile), lambda i: (0, i))],
        out_specs=[pl.BlockSpec((TOKENS, tile), lambda i: (0, i))] * 2,
        compiler_params=pltpu.CompilerParams(vmem_limit_bytes=56 * 2**20),
        cost_estimate=pl.CostEstimate(flops=2**32, bytes_accessed=13 * 2**20, transcendentals=0),
    )(place, *pieces, weights)


def device(y, z, core):
    return (y * 4 + z) * 2 + core


PLACES = [(y, z, core) for y in range(4) for z in range(4) for core in range(2)]
SAME_CORE = [[device(y, z, core) for y in range(4) for z in range(4)] for core in range(2)]
SWAP = [(device(y, z, core), device(y, z, 1 - core)) for y, z, core in PLACES]


def along_z(by):
    return [(device(y, z, core), device(y, (z + by) % 4, core)) for y, z, core in PLACES]


def along_y(by):
    return [(device(y, z, core), device((y + by) % 4, z, core)) for y, z, core in PLACES]


def earlier_y(by):
    return [(device(y, z, core), device(y - by, z, core)) for y, z, core in PLACES if y >= by]


def move(array, pairs):
    return lax.ppermute(array, "ctx", pairs)


def along_x(array, by):
    return lax.ppermute(array, "head", [(x, (x + by) % 4) for x in range(4)])


def gather_pieces(own, other):
    before, after = (along_x(own, 1), along_x(other, 1)), (along_x(own, -1), along_x(other, -1))
    return own, other, *before, along_x(before[0], 1), along_x(after[1], -1), *after


def sum_ctx(array):
    array = array + move(array, SWAP)
    array = array + move(array, along_z(1)) + move(array, along_z(2)) + move(array, along_z(3))
    return array + move(array, along_y(1)) + move(array, along_y(2)) + move(array, along_y(3))


def per_device(dout, out_weight, x_in, z_in, b_in, c_in, dt, rate, skip, gain, start_state):
    at = lax.axis_index("ctx")
    place = jnp.stack([lax.axis_index("head"), at // 8, (at // 2) % 4, at % 2]).astype(jnp.int32)
    weights = lax.all_gather(out_weight, "ctx", axis=0, tiled=True, axis_index_groups=SAME_CORE)
    own_dout, send_dout = split_dout(place, dout)
    pieces = gather_pieces(own_dout, move(send_dout, SWAP))
    steps = dt.T
    rates = rate.reshape(HEADS, 1)
    skips = jnp.repeat(skip, P_SIZE).reshape(1, CHANNELS)
    gains = gain.reshape(1, CHANNELS)
    state = start_state.reshape(CHANNELS, N)
    y, normed, run, run_col, dt_col = forward(
        x_in, z_in, b_in, c_in, steps, rates, state, gains, skips
    )
    term = weight_grad(place, pieces, normed, move(normed, SWAP))
    grad_w = lax.psum_scatter(
        term, "ctx", scatter_dimension=0, tiled=True, axis_index_groups=SAME_CORE
    )
    own_part, other_part = upstream_parts(place, pieces, weights)
    grad_y, grad_z, gain_sum, start, keep, send = norm_back(
        place, own_part, move(other_part, SWAP), y, z_in, c_in, gains, run, run_col
    )
    chip, last = chip_state(place, keep, move(send, SWAP))
    row, after, reach = row_state(place, chip, *[move(chip, along_z(-k)) for k in (1, 2, 3)])
    mine, theirs = end_state(
        place, *[move(row, earlier_y(k)) for k in (1, 2, 3)], after, reach, last
    )
    got = move(theirs, SWAP)
    inner, grad_c, keys_back, row_sums, col_sums, skip_sum = scan_back(
        x_in, b_in, c_in, steps, run, run_col, dt_col, state, grad_y
    )
    grad_x, grad_b, grad_dt, grad_start, sums = end_back(
        place, x_in, b_in, steps, rates, skips, run, run_col, dt_col, state, grad_y, inner,
        keys_back, row_sums, col_sums, skip_sum, mine, got, start, gain_sum,
    )
    sums = sum_ctx(sums)[0]
    return (
        grad_x,
        grad_z,
        grad_b,
        grad_c,
        grad_dt,
        grad_w,
        sums[:CHANNELS],
        sums[CHANNELS + HEADS : CHANNELS + 2 * HEADS],
        sums[CHANNELS : CHANNELS + HEADS],
        grad_start.reshape(start_state.shape),
    )


def solution(mesh):
    full, whole = P("ctx", "head"), P("head")
    state = P("ctx", "head", None, None)
    return jax.shard_map(
        per_device,
        mesh=mesh,
        in_specs=(full,) * 7 + (whole,) * 3 + (state,),
        out_specs=(full,) * 6 + (whole,) * 3 + (state,),
        check_vma=False,
    )
```

profile of v0, /device:TPU:0, one launch (start us, length us, event | category | flops | bytes accessed | tf_op | source)
XLA Modules:
  0.0 219.0 jit_solution(14067461589693765130)
XLA Ops:
  10.7 11.2 %shard_map.186 = (f32[256,2048]{1,0:T(8,128)}, bf16[256,2048]{1,0:T(8,128)(2,1)}, f32[32,256]{1,0:T(8,128)}, bf16[256,128]{1,0:T(8,128)(2,1)}, bf16[256,128]{1,0:T(8,128)(2,1)}) custom-call(bf16[256,2048]{1,0:T(8,128)(2,1)} %x_ref.5, bf16[256,2048]{1,0:T(8,128)(2,1)} %z_ref.3, bf16[256,256]{1,0:T(8,128)(2,1)} %b_ref.5, bf16[256,256]{1,0:T(8,128)(2,1)} %c_ref.5, ...), custom_call_target="tpu_custom_call" | custom-call | flops 10000000000 | bytes 6766720 | tf_op jit(solution)/shard_map/pallas_call | solution.py:414
  22.6 2.0 shard_map.187
  26.6 2.7 %collective-permute-start.4 = (bf16[256,512]{1,0:T(8,128)(2,1)S(1)}, bf16[256,512]{1,0:T(8,128)(2,1)S(1)}, u32[]{:S(2)}, u32[]{:S(2)}) collective-permute-start(bf16[256,512]{1,0:T(8,128)(2,1)S(1)} %collective-permute-done.refs_1_), channel_id=1, source_target_pairs={{0,3},{1,0},{2,1},{3,2},{4,7},{5,4},{6,5},{7,6},{8,11},{9,8},{10,9... | collective-permute-start | bytes 786440 | tf_op jit(solution)/shard_map/ppermute | solution.py:588
  31.3 4.3 %collective-permute-done.1.refs_2_ = bf16[256,512]{1,0:T(8,128)(2,1)S(1)} collective-permute-done((bf16[256,512]{1,0:T(8,128)(2,1)}, bf16[256,512]{1,0:T(8,128)(2,1)S(1)}, u32[]{:S(2)}, u32[]{:S(2)}) %collective-permute-start.1) | collective-permute-done | bytes 262176 | tf_op jit(solution)/shard_map/ppermute | solution.py:588
  36.0 3.6 %collective-permute-start.5 = (bf16[256,512]{1,0:T(8,128)(2,1)S(1)}, bf16[256,512]{1,0:T(8,128)(2,1)S(1)}, u32[]{:S(2)}, u32[]{:S(2)}) collective-permute-start(bf16[256,512]{1,0:T(8,128)(2,1)S(1)} %collective-permute-done.4.refs_7_), channel_id=1, source_target_pairs={{0,3},{1,0},{2,1},{3,2},{4,7},{5,4},{6,5},{7,6},{8,11},{9,8},{10,9... | collective-permute-start | bytes 786440 | tf_op jit(solution)/shard_map/ppermute | solution.py:588
  39.6 2.0 collective-permute-done.6.refs_6_
  41.6 4.3 %collective-permute-done.3.refs_4_ = bf16[256,512]{1,0:T(8,128)(2,1)S(1)} collective-permute-done((bf16[256,512]{1,0:T(8,128)(2,1)S(1)}, bf16[256,512]{1,0:T(8,128)(2,1)S(1)}, u32[]{:S(2)}, u32[]{:S(2)}) %collective-permute-start.3) | collective-permute-done | bytes 262176 | tf_op jit(solution)/shard_map/ppermute | solution.py:588
  48.2 9.1 %shard_map.195 = bf16[2048,2048]{1,0:T(8,128)(2,1)} custom-call(s32[4]{0:T(128)} %pad_add_fusion.place_ref, bf16[256,512]{1,0:T(8,128)(2,1)} %get-tuple-element.46.refs_0_, bf16[256,512]{1,0:T(8,128)(2,1)} %copy-done.9, bf16[256,512]{1,0:T(8,128)(2,1)} %copy-done.10, bf16[256,512]{1,0:T(8,128)(2,1)} %copy-done.13, bf16[256,512]{1,0:T(8,128)(2,1)} %copy-done.14, ...), custom_call_target="tpu_custom_call" | custom-call | flops 4294967296 | bytes 12582912 | tf_op jit(solution)/shard_map/pallas_call | solution.py:518
  57.4 26.1 %all-gather.2.cloned.1.call-done.refs_8_ = bf16[2048,2048]{1,0:T(8,128)(2,1)} async-done(((bf16[128,2048]{1,0:T(8,128)(2,1)}), bf16[2048,2048]{1,0:T(8,128)(2,1)}) %all-gather.2.cloned.1.call-update) | async-done | bytes 8388624 | tf_op jit(solution)/shard_map/all_gather | solution.py:605
  83.5 8.7 %shard_map.188 = (f32[256,2048]{1,0:T(8,128)}, bf16[256,2048]{1,0:T(8,128)(2,1)}) custom-call(s32[4]{0:T(128)} %pad_add_fusion.place_ref, bf16[256,512]{1,0:T(8,128)(2,1)} %get-tuple-element.46.refs_0_, bf16[256,512]{1,0:T(8,128)(2,1)} %copy-done.9, bf16[256,512]{1,0:T(8,128)(2,1)} %copy-done.10, bf16[256,512]{1,0:T(8,128)(2,1)} %copy-done.13, ...), custom_call_target="tpu_custom_call" | custom-call | flops 4294967296 | bytes 13631488 | tf_op jit(solution)/shard_map/pallas_call | solution.py:546
  92.2 2.9 %collective-permute-done.7.other_ref = bf16[256,2048]{1,0:T(8,128)(2,1)S(1)} collective-permute-done((bf16[256,2048]{1,0:T(8,128)(2,1)}, bf16[256,2048]{1,0:T(8,128)(2,1)S(1)}, u32[]{:S(2)}, u32[]{:S(2)}) %collective-permute-start.7) | collective-permute-done | bytes 1048608 | tf_op jit(solution)/shard_map/ppermute | solution.py:584
  96.1 12.6 %shard_map.189 = (bf16[256,2048]{1,0:T(8,128)(2,1)}, bf16[256,2048]{1,0:T(8,128)(2,1)}, f32[1,2048]{1,0:T(1,128)}, f32[2048,128]{1,0:T(8,128)}, bf16[1056,128]{1,0:T(8,128)(2,1)}, /*index=5*/bf16[1056,128]{1,0:T(8,128)(2,1)}) custom-call(s32[4]{0:T(128)} %pad_add_fusion.place_ref, f32[256,2048]{1,0:T(8,128)} %get-tuple-element.48.own_ref, ...), custom_call_target="tpu_custom_call" | custom-call | flops 6000000000 | bytes 10223632 | tf_op jit(solution)/shard_map/pallas_call | solution.py:414
  111.2 2.0 shard_map.191
  114.7 2.9 %collective-permute-start.10 = (bf16[1056,128]{1,0:T(8,128)(2,1)}, bf16[1056,128]{1,0:T(8,128)(2,1)S(1)}, u32[]{:S(2)}, u32[]{:S(2)}) collective-permute-start(bf16[1056,128]{1,0:T(8,128)(2,1)} %get-tuple-element.59.own_ref), channel_id=1, source_target_pairs={{0,16},{4,20},{8,24},{12,28},{16,0},{20,4},{24,8},{28,12},{32,48},... | collective-permute-start | bytes 811016 | tf_op jit(solution)/shard_map/ppermute | solution.py:584
  118.9 9.4 %collective-permute-done.11.three_ref = bf16[1056,128]{1,0:T(8,128)(2,1)S(1)} collective-permute-done((bf16[1056,128]{1,0:T(8,128)(2,1)}, bf16[1056,128]{1,0:T(8,128)(2,1)S(1)}, u32[]{:S(2)}, u32[]{:S(2)}) %collective-permute-start.11) | collective-permute-done | bytes 270368 | tf_op jit(solution)/shard_map/ppermute | solution.py:584
  128.3 11.5 %collective-permute-done.10.two_ref = bf16[1056,128]{1,0:T(8,128)(2,1)S(1)} collective-permute-done((bf16[1056,128]{1,0:T(8,128)(2,1)}, bf16[1056,128]{1,0:T(8,128)(2,1)S(1)}, u32[]{:S(2)}, u32[]{:S(2)}) %collective-permute-start.10) | collective-permute-done | bytes 270368 | tf_op jit(solution)/shard_map/ppermute | solution.py:584
  141.3 2.7 %shard_map.192 = (bf16[1056,128]{1,0:T(8,128)(2,1)}, f32[1024,128]{1,0:T(8,128)}, f32[16,128]{1,0:T(8,128)}) custom-call(s32[4]{0:T(128)} %pad_add_fusion.place_ref, bf16[1056,128]{1,0:T(8,128)(2,1)} %get-tuple-element.59.own_ref, bf16[1056,128]{1,0:T(8,128)(2,1)} %copy-done.6, bf16[1056,128]{1,0:T(8,128)(2,1)} %copy-done.5, bf16[1056,128]{1,0:T(8,128)(2,1)} %copy-done.3), custom_call_target="tpu_custom_call" | custom-call | bytes 1884176 | tf_op jit(solution)/shard_map/pallas_call | solution.py:414
  147.8 17.3 %collective-permute-done.14.three_ref = bf16[1056,128]{1,0:T(8,128)(2,1)S(1)} collective-permute-done((bf16[1056,128]{1,0:T(8,128)(2,1)}, bf16[1056,128]{1,0:T(8,128)(2,1)S(1)}, u32[]{:S(2)}, u32[]{:S(2)}) %collective-permute-start.14) | collective-permute-done | bytes 270368 | tf_op jit(solution)/shard_map/ppermute | solution.py:584
  166.0 2.5 %shard_map.193 = (bf16[1024,128]{1,0:T(8,128)(2,1)}, bf16[1024,128]{1,0:T(8,128)(2,1)}) custom-call(s32[4]{0:T(128)} %pad_add_fusion.place_ref, bf16[1056,128]{1,0:T(8,128)(2,1)} %copy-done.4, bf16[1056,128]{1,0:T(8,128)(2,1)} %copy-done.2, bf16[1056,128]{1,0:T(8,128)(2,1)} %copy-done.1, f32[1024,128]{1,0:T(8,128)} %get-tuple-element.61.after_ref, ...), custom_call_target="tpu_custom_call" | custom-call | bytes 2138128 | tf_op jit(solution)/shard_map/pallas_call | solution.py:414
  168.5 13.4 %shard_map.190 = (f32[256,2048]{1,0:T(8,128)}, bf16[256,256]{1,0:T(8,128)(2,1)}, f32[256,256]{1,0:T(8,128)}, f32[2,32,128]{2,1,0:T(8,128)}, f32[256,128]{1,0:T(8,128)}, /*index=5*/f32[1,128]{1,0:T(1,128)}) custom-call(bf16[256,2048]{1,0:T(8,128)(2,1)} %x_ref.5, bf16[256,256]{1,0:T(8,128)(2,1)} %b_ref.5, bf16[256,256]{1,0:T(8,128)(2,1)} %c_ref.5, ...), custom_call_target="tpu_custom_call" | custom-call | flops 15000000512 | bytes 6226688 | tf_op jit(solution)/shard_map/pallas_call | solution.py:414
  182.6 12.1 %shard_map.194 = (bf16[256,2048]{1,0:T(8,128)(2,1)}, bf16[256,256]{1,0:T(8,128)(2,1)}, f32[256,32]{1,0:T(8,128)}, f32[2048,128]{1,0:T(8,128)}, f32[1,2176]{1,0:T(1,128)}) custom-call(s32[4]{0:T(128)} %pad_add_fusion.place_ref, bf16[256,2048]{1,0:T(8,128)(2,1)} %x_ref.5, bf16[256,256]{1,0:T(8,128)(2,1)} %b_ref.5, f32[32,256]{1,0:T(8,128)} %bitcast.21, ...), custom_call_target="tpu_custom_call" | custom-call | flops 5000000000 | bytes 9856144 | tf_op jit(solution)/shard_map/pallas_call | solution.py:414
  200.8 1.9 collective-permute-done.19
  203.6 2.5 %collective-permute-start.22 = (f32[1,2176]{1,0:T(1,128)S(1)}, f32[1,2176]{1,0:T(1,128)S(1)}, u32[]{:S(2)}, u32[]{:S(2)}) collective-permute-start(f32[1,2176]{1,0:T(1,128)S(1)} %add_add_fusion.1), channel_id=1, source_target_pairs={{0,64},{4,68},{8,72},{12,76},{16,80},{20,84},{24,88},{28,92},{32,9... | collective-permute-start | bytes 26120 | tf_op jit(solution)/shard_map/ppermute | solution.py:584
  208.8 2.1 collective-permute-done.21
  (84 shorter events, 34.9 us)
Async XLA Ops:
  7.2 76.3 %all-gather.2.cloned.1.call-start = ((), (), s32[]{:S(2)}) async-start(), calls=%async_computation.1 | async-start | bytes 8912896 | tf_op jit(solution)/shard_map/all_gather | solution.py:605
  7.9 204.2 %reduce-scatter.2.cloned.1.call-start = ((), (), s32[]{:S(2)}) async-start(), calls=%async_computation.2 | async-start | bytes 8912896 | tf_op jit(solution)/shard_map/reduce_scatter | solution.py:617
  21.9 24.6 %collective-permute-start.16 = (bf16[256,2048]{1,0:T(8,128)(2,1)}, bf16[256,2048]{1,0:T(8,128)(2,1)S(1)}, u32[]{:S(2)}, u32[]{:S(2)}) collective-permute-start(bf16[256,2048]{1,0:T(8,128)(2,1)} %get-tuple-element.73.refs_8_), channel_id=1, source_target_pairs={{0,4},{4,0},{8,12},{12,8},{16,20},{20,16},{24,28},{28,24},{32,36},... | collective-permute-start | bytes 3145736 | tf_op jit(solution)/shard_map/ppermute | solution.py:584
  24.5 2.0 collective-permute-start
  25.0 10.6 %collective-permute-start.1 = (bf16[256,512]{1,0:T(8,128)(2,1)}, bf16[256,512]{1,0:T(8,128)(2,1)S(1)}, u32[]{:S(2)}, u32[]{:S(2)}) collective-permute-start(bf16[256,512]{1,0:T(8,128)(2,1)} %get-tuple-element.46.refs_0_), channel_id=1, source_target_pairs={{0,1},{1,2},{2,3},{3,0},{4,5},{5,6},{6,7},{7,4},{8,9},{9,10},{10,1... | collective-permute-start | bytes 786440 | tf_op jit(solution)/shard_map/ppermute | solution.py:588
  26.6 9.4 %collective-permute-start.4 = (bf16[256,512]{1,0:T(8,128)(2,1)S(1)}, bf16[256,512]{1,0:T(8,128)(2,1)S(1)}, u32[]{:S(2)}, u32[]{:S(2)}) collective-permute-start(bf16[256,512]{1,0:T(8,128)(2,1)S(1)} %collective-permute-done.refs_1_), channel_id=1, source_target_pairs={{0,3},{1,0},{2,1},{3,2},{4,7},{5,4},{6,5},{7,6},{8,11},{9,8},{10,9... | collective-permute-start | bytes 786440 | tf_op jit(solution)/shard_map/ppermute | solution.py:588
  29.2 12.4 %collective-permute-start.6 = (bf16[256,512]{1,0:T(8,128)(2,1)}, bf16[256,512]{1,0:T(8,128)(2,1)S(1)}, u32[]{:S(2)}, u32[]{:S(2)}) collective-permute-start(bf16[256,512]{1,0:T(8,128)(2,1)} %get-tuple-element.46.refs_0_), channel_id=1, source_target_pairs={{0,3},{1,0},{2,1},{3,2},{4,7},{5,4},{6,5},{7,6},{8,11},{9,8},{10,9... | collective-permute-start | bytes 786440 | tf_op jit(solution)/shard_map/ppermute | solution.py:588
  30.1 11.5 %collective-permute-start.2 = (bf16[256,512]{1,0:T(8,128)(2,1)S(1)}, bf16[256,512]{1,0:T(8,128)(2,1)S(1)}, u32[]{:S(2)}, u32[]{:S(2)}) collective-permute-start(bf16[256,512]{1,0:T(8,128)(2,1)S(1)} %collective-permute-done.refs_1_), channel_id=1, source_target_pairs={{0,1},{1,2},{2,3},{3,0},{4,5},{5,6},{6,7},{7,4},{8,9},{9,10},{10,1... | collective-permute-start | bytes 786440 | tf_op jit(solution)/shard_map/ppermute | solution.py:588
  35.6 10.3 %collective-permute-start.3 = (bf16[256,512]{1,0:T(8,128)(2,1)S(1)}, bf16[256,512]{1,0:T(8,128)(2,1)S(1)}, u32[]{:S(2)}, u32[]{:S(2)}) collective-permute-start(bf16[256,512]{1,0:T(8,128)(2,1)S(1)} %collective-permute-done.1.refs_2_), channel_id=1, source_target_pairs={{0,1},{1,2},{2,3},{3,0},{4,5},{5,6},{6,7},{7,4},{8,9},{9,10},{10,1... | collective-permute-start | bytes 786440 | tf_op jit(solution)/shard_map/ppermute | solution.py:588
  36.0 10.6 %collective-permute-start.5 = (bf16[256,512]{1,0:T(8,128)(2,1)S(1)}, bf16[256,512]{1,0:T(8,128)(2,1)S(1)}, u32[]{:S(2)}, u32[]{:S(2)}) collective-permute-start(bf16[256,512]{1,0:T(8,128)(2,1)S(1)} %collective-permute-done.4.refs_7_), channel_id=1, source_target_pairs={{0,3},{1,0},{2,1},{3,2},{4,7},{5,4},{6,5},{7,6},{8,11},{9,8},{10,9... | collective-permute-start | bytes 786440 | tf_op jit(solution)/shard_map/ppermute | solution.py:588
  92.2 2.9 %collective-permute-start.7 = (bf16[256,2048]{1,0:T(8,128)(2,1)}, bf16[256,2048]{1,0:T(8,128)(2,1)S(1)}, u32[]{:S(2)}, u32[]{:S(2)}) collective-permute-start(bf16[256,2048]{1,0:T(8,128)(2,1)} %get-tuple-element.49), channel_id=1, source_target_pairs={{0,4},{4,0},{8,12},{12,8},{16,20},{20,16},{24,28},{28,24},{32,36},... | collective-permute-start | bytes 3145736 | tf_op jit(solution)/shard_map/ppermute | solution.py:584
  113.2 15.1 %collective-permute-start.11 = (bf16[1056,128]{1,0:T(8,128)(2,1)}, bf16[1056,128]{1,0:T(8,128)(2,1)S(1)}, u32[]{:S(2)}, u32[]{:S(2)}) collective-permute-start(bf16[1056,128]{1,0:T(8,128)(2,1)} %get-tuple-element.59.own_ref), channel_id=1, source_target_pairs={{0,8},{4,12},{8,16},{12,20},{16,24},{20,28},{24,0},{28,4},{32,40},... | collective-permute-start | bytes 811016 | tf_op jit(solution)/shard_map/ppermute | solution.py:584
  114.7 25.2 %collective-permute-start.10 = (bf16[1056,128]{1,0:T(8,128)(2,1)}, bf16[1056,128]{1,0:T(8,128)(2,1)S(1)}, u32[]{:S(2)}, u32[]{:S(2)}) collective-permute-start(bf16[1056,128]{1,0:T(8,128)(2,1)} %get-tuple-element.59.own_ref), channel_id=1, source_target_pairs={{0,16},{4,20},{8,24},{12,28},{16,0},{20,4},{24,8},{28,12},{32,48},... | collective-permute-start | bytes 811016 | tf_op jit(solution)/shard_map/ppermute | solution.py:584
  117.6 22.3 %collective-permute-start.9 = (bf16[1056,128]{1,0:T(8,128)(2,1)}, bf16[1056,128]{1,0:T(8,128)(2,1)S(1)}, u32[]{:S(2)}, u32[]{:S(2)}) collective-permute-start(bf16[1056,128]{1,0:T(8,128)(2,1)} %get-tuple-element.59.own_ref), channel_id=1, source_target_pairs={{0,24},{4,28},{8,0},{12,4},{16,8},{20,12},{24,16},{28,20},{32,56},... | collective-permute-start | bytes 811016 | tf_op jit(solution)/shard_map/ppermute | solution.py:584
  144.0 21.2 %collective-permute-start.14 = (bf16[1056,128]{1,0:T(8,128)(2,1)}, bf16[1056,128]{1,0:T(8,128)(2,1)S(1)}, u32[]{:S(2)}, u32[]{:S(2)}) collective-permute-start(bf16[1056,128]{1,0:T(8,128)(2,1)} %get-tuple-element.60), channel_id=1, source_target_pairs={{96,0},{100,4},{104,8},{108,12},{112,16},{116,20},{120,24},{124,28... | collective-permute-start | bytes 811016 | tf_op jit(solution)/shard_map/ppermute | solution.py:584
  145.2 19.9 %collective-permute-start.13 = (bf16[1056,128]{1,0:T(8,128)(2,1)}, bf16[1056,128]{1,0:T(8,128)(2,1)S(1)}, u32[]{:S(2)}, u32[]{:S(2)}) collective-permute-start(bf16[1056,128]{1,0:T(8,128)(2,1)} %get-tuple-element.60), channel_id=1, source_target_pairs={{64,0},{68,4},{72,8},{76,12},{80,16},{84,20},{88,24},{92,28},{96,3... | collective-permute-start | bytes 811016 | tf_op jit(solution)/shard_map/ppermute | solution.py:584
  146.5 18.6 %collective-permute-start.12 = (bf16[1056,128]{1,0:T(8,128)(2,1)}, bf16[1056,128]{1,0:T(8,128)(2,1)S(1)}, u32[]{:S(2)}, u32[]{:S(2)}) collective-permute-start(bf16[1056,128]{1,0:T(8,128)(2,1)} %get-tuple-element.60), channel_id=1, source_target_pairs={{32,0},{36,4},{40,8},{44,12},{48,16},{52,20},{56,24},{60,28},{64,3... | collective-permute-start | bytes 811016 | tf_op jit(solution)/shard_map/ppermute | solution.py:584
  168.5 13.4 %collective-permute-start.15 = (bf16[1024,128]{1,0:T(8,128)(2,1)}, bf16[1024,128]{1,0:T(8,128)(2,1)S(1)}, u32[]{:S(2)}, u32[]{:S(2)}) collective-permute-start(bf16[1024,128]{1,0:T(8,128)(2,1)} %get-tuple-element.65), channel_id=1, source_target_pairs={{0,4},{4,0},{8,12},{12,8},{16,20},{20,16},{24,28},{28,24},{32,36},... | collective-permute-start | bytes 786440 | tf_op jit(solution)/shard_map/ppermute | solution.py:584
  197.1 3.7 %collective-permute-start.20 = (f32[1,2176]{1,0:T(1,128)S(1)}, f32[1,2176]{1,0:T(1,128)S(1)}, u32[]{:S(2)}, u32[]{:S(2)}) collective-permute-start(f32[1,2176]{1,0:T(1,128)S(1)} %add.34), channel_id=1, source_target_pairs={{0,24},{4,28},{8,0},{12,4},{16,8},{20,12},{24,16},{28,20},{32,56},... | collective-permute-start | bytes 26120 | tf_op jit(solution)/shard_map/ppermute | solution.py:584
  197.4 5.2 %collective-permute-start.19 = (f32[1,2176]{1,0:T(1,128)S(1)}, f32[1,2176]{1,0:T(1,128)S(1)}, u32[]{:S(2)}, u32[]{:S(2)}) collective-permute-start(f32[1,2176]{1,0:T(1,128)S(1)} %add.34), channel_id=1, source_target_pairs={{0,16},{4,20},{8,24},{12,28},{16,0},{20,4},{24,8},{28,12},{32,48},... | collective-permute-start | bytes 26120 | tf_op jit(solution)/shard_map/ppermute | solution.py:584
  198.0 5.5 %collective-permute-start.18 = (f32[1,2176]{1,0:T(1,128)S(1)}, f32[1,2176]{1,0:T(1,128)S(1)}, u32[]{:S(2)}, u32[]{:S(2)}) collective-permute-start(f32[1,2176]{1,0:T(1,128)S(1)} %add.34), channel_id=1, source_target_pairs={{0,8},{4,12},{8,16},{12,20},{16,24},{20,28},{24,0},{28,4},{32,40},... | collective-permute-start | bytes 26120 | tf_op jit(solution)/shard_map/ppermute | solution.py:584
  203.5 4.8 %collective-permute-start.23 = (f32[1,2176]{1,0:T(1,128)S(1)}, f32[1,2176]{1,0:T(1,128)S(1)}, u32[]{:S(2)}, u32[]{:S(2)}) collective-permute-start(f32[1,2176]{1,0:T(1,128)S(1)} %add_add_fusion.1), channel_id=1, source_target_pairs={{0,96},{4,100},{8,104},{12,108},{16,112},{20,116},{24,120},{28,124... | collective-permute-start | bytes 26120 | tf_op jit(solution)/shard_map/ppermute | solution.py:584
  203.6 5.2 %collective-permute-start.22 = (f32[1,2176]{1,0:T(1,128)S(1)}, f32[1,2176]{1,0:T(1,128)S(1)}, u32[]{:S(2)}, u32[]{:S(2)}) collective-permute-start(f32[1,2176]{1,0:T(1,128)S(1)} %add_add_fusion.1), channel_id=1, source_target_pairs={{0,64},{4,68},{8,72},{12,76},{16,80},{20,84},{24,88},{28,92},{32,9... | collective-permute-start | bytes 26120 | tf_op jit(solution)/shard_map/ppermute | solution.py:584
  206.1 4.9 %collective-permute-start.21 = (f32[1,2176]{1,0:T(1,128)S(1)}, f32[1,2176]{1,0:T(1,128)S(1)}, u32[]{:S(2)}, u32[]{:S(2)}) collective-permute-start(f32[1,2176]{1,0:T(1,128)S(1)} %add_add_fusion.1), channel_id=1, source_target_pairs={{0,32},{4,36},{8,40},{12,44},{16,48},{20,52},{24,56},{28,60},{32,6... | collective-permute-start | bytes 26120 | tf_op jit(solution)/shard_map/ppermute | solution.py:584
  (19 other events, 75.1 us)
Sparse Core Ops, SparseCore 0:
  10.2 73.3 all-gather.1
  87.5 101.6 reduce-scatter.1
where the time goes:
time: 220 us; the launch traced here: 219 us
  waiting for transfers between devices  88.7 us (40%)
  Pallas kernels  76.3 us (35%)
  starting transfers between devices  26.6 us (12%)
  between operations  14.2 us (6%)
  local copies, waits for them, and re-layouts  11.8 us (5%)
    pallas_call x8, Pallas kernels, call(): pl.pallas_call(kernel, out_shape=[jax.ShapeDtypeStruct(shape, kind) for s...  58.5 us
    ppermute x18, waiting for transfers between devices, move(): return lax.ppermute(array, 'ctx', pairs)  50.5 us
    all_gather x1, waiting for transfers between devices, per_device(): lax.all_gather(out_weight, 'ctx', axis=0, tiled=True, axis_index_groups=S...  26.1 us
    ppermute x18, starting transfers between devices, move(): return lax.ppermute(array, 'ctx', pairs)  16.3 us
    ppermute x6, waiting for transfers between devices, along_x(): return lax.ppermute(array, 'head', [(x, (x + by) % 4) for x in range(4)])  11.3 us
    ppermute x6, starting transfers between devices, along_x(): return lax.ppermute(array, 'head', [(x, (x + by) % 4) for x in range(4)])  10.2 us
    pallas_call x1, Pallas kernels, weight_grad(): pl.pallas_call(weight_grad_kernel, grid=(CHANNELS // tile,), out_shape=ja...  9.14 us
    pallas_call x1, Pallas kernels, upstream_parts(): pl.pallas_call(upstream_kernel, grid=(CHANNELS // tile,), out_shape=[jax....  8.72 us
  transfers between devices with their start and end apart: 26, of which 16 were waited for; matrix products, arithmetic and copies ran while one was open for 3% of the time, Pallas kernels for 35%

commit v1 on v0

v1 whole, which is shorter than its diff:
```python
import functools
import math

import jax
import jax.numpy as jnp
from jax import lax
from jax.experimental import pallas as pl
from jax.experimental.pallas import tpu as pltpu
from jax.sharding import PartitionSpec as P

P_SIZE = 64
N = 128
Q = 128
TOKENS = 256
HEADS = 32
GROUPS = 2
PER_GROUP = HEADS // GROUPS
CHANNELS = HEADS * P_SIZE
GROUP_CHANNELS = PER_GROUP * P_SIZE
PAIRS = HEADS // 2
GROUP_PAIRS = PER_GROUP // 2
STATE_ROWS = PER_GROUP * P_SIZE
EPSILON = 1e-05
UNROLL = 2
SHORT, LONG = 100000000, 20000000000

f32 = jnp.float32
bf16 = jnp.bfloat16


def dot(a, b, over=((1,), (0,))):
    return lax.dot_general(a, b, (over, ((), ())), preferred_element_type=f32)


def dot_rows(a, b):
    return dot(a, b, ((1,), (1,)))


def dot_columns(a, b):
    return dot(a, b, ((0,), (0,)))


def iota(shape, axis):
    return lax.broadcasted_iota(jnp.int32, shape, axis)


def split2(v):
    high = v.astype(bf16)
    return high, (v - high.astype(f32)).astype(bf16)


def split3(v):
    high = v.astype(bf16)
    rest = v - high.astype(f32)
    middle = rest.astype(bf16)
    return high, middle, (rest - middle.astype(f32)).astype(bf16)


def exact_rows(rows, right):
    product = dot(jnp.concatenate(split3(rows), axis=0), right)
    return product[:HEADS] + product[HEADS : 2 * HEADS] + product[2 * HEADS :]


def part_columns(rows):
    parts = [part.astype(f32) for part in split3(rows)]
    stacked = jnp.concatenate(parts + [jnp.zeros_like(rows)], axis=0)
    return stacked.T.astype(bf16)


def pair_select(pair, width):
    row = iota((128, 2 * width), 0)
    head = 2 * pair + jnp.where(iota((128, 2 * width), 1) >= width, 1, 0)
    hit = ((row & (HEADS - 1)) == head) & (row < 3 * HEADS)
    return jnp.where(hit, 1.0, 0.0).astype(bf16)


def pair_sums(values, pair):
    row, lane = iota((128, 128), 0), iota((128, 128), 1)
    head = 2 * pair + jnp.where(row >= P_SIZE, 1, 0)
    place = jnp.where(lane == head, 1.0, 0.0).astype(bf16)
    high, low = split2(values)
    return dot(jnp.concatenate([high, low], axis=1), jnp.concatenate([place, place], axis=0))


def lanes_of(pair):
    return pl.ds(pl.multiple_of(pair * 128, 128), 128)


def halves(v):
    first = iota(v.shape, 1) < P_SIZE
    zero = jnp.zeros_like(v)
    return jnp.where(first, v, zero), jnp.where(first, zero, v)


def causal_exp(spread, keep):
    return jnp.exp(jnp.where(keep, spread, -1e30))


def prepare_kernel(place_ref, dout_ref, dt_ref, rate_ref, keep_ref, send_ref, run_ref, run_col_ref, dt_col_ref):
    leads = place_ref[3] == 0
    for at in range(4):
        even = dout_ref[:, 256 * at : 256 * at + 128]
        odd = dout_ref[:, 256 * at + 128 : 256 * at + 256]
        own = slice(128 * at, 128 * at + 128)
        keep_ref[:, own] = jnp.where(leads, even, odd)
        send_ref[:, own] = jnp.where(leads, odd, even)
    steps = dt_ref[...]
    upto = jnp.where(iota((TOKENS, TOKENS), 0) <= iota((TOKENS, TOKENS), 1), 1.0, 0.0).astype(bf16)
    run = exact_rows(-steps * rate_ref[...], upto)
    run_ref[...] = run
    run_col_ref[...] = part_columns(run)
    dt_col_ref[...] = part_columns(steps)


def forward_kernel(
    group, x_ref, z_ref, b_ref, c_ref, dt_ref, run_ref, run_col_ref, state_ref, gain_ref, skip_ref,
    y_ref, normed_ref,
    scores, gated_ref, power,
):
    lower = iota((Q, Q), 0) >= iota((Q, Q), 1)
    reads = c_ref[...]
    scores[...] = dot_rows(reads, b_ref[...])
    power[...] = jnp.zeros_like(power)

    def body(at, carry):
        pair = group * GROUP_PAIRS + at
        lanes = own = lanes_of(at)
        xs = x_ref[:, lanes]
        expanded = dot(run_col_ref[...], pair_select(pair, 128))
        top, bottom = [], []
        for k in range(2):
            run_row = run_ref[pl.ds(2 * pair + k, 1), :]
            dt_row = dt_ref[pl.ds(2 * pair + k, 1), :]
            col = expanded[:, k * 128 : (k + 1) * 128]
            m00 = causal_exp(col[:Q] - run_row[:, :Q], lower) * (scores[:Q, :Q] * dt_row[:, :Q])
            m10 = jnp.exp(col[Q:] - run_row[:, :Q]) * (scores[Q:, :Q] * dt_row[:, :Q])
            m11 = causal_exp(col[Q:] - run_row[:, Q:], lower) * (scores[Q:, Q:] * dt_row[:, Q:])
            top.append(m00.astype(bf16))
            bottom.extend([m10.astype(bf16), m11.astype(bf16)])
        x0, x1 = halves(xs)
        y0 = dot(jnp.concatenate(top, axis=1), jnp.concatenate([x0[:Q], x1[:Q]], axis=0))
        y1 = dot(jnp.concatenate(bottom, axis=1), jnp.concatenate([x0, x1], axis=0))
        from_start = dot_rows(reads, state_ref[lanes_of(pair), :].astype(bf16))
        first = iota((TOKENS, 128), 1) < P_SIZE
        reach = jnp.exp(jnp.where(first, expanded[:, :128], expanded[:, 128:]))
        y = jnp.concatenate([y0, y1], axis=0) + reach * from_start
        y = y + skip_ref[:, lanes] * xs.astype(f32)
        y_ref[:, lanes] = y
        gate = z_ref[:, lanes].astype(f32)
        gated = y * gate / (1.0 + jnp.exp(-gate))
        gated_ref[:, own] = gated
        power[...] += gated * gated
        return carry

    lax.fori_loop(0, GROUP_PAIRS, body, 0, unroll=UNROLL)
    mean = jnp.sum(power[...], axis=1, keepdims=True) * (1.0 / GROUP_CHANNELS)
    scale = jnp.broadcast_to(lax.rsqrt(mean + EPSILON), (TOKENS, 128))

    def finish(at, carry):
        lanes = own = lanes_of(at)
        normed_ref[:, lanes] = (gated_ref[:, own] * scale * gain_ref[:, lanes]).astype(bf16)
        return carry

    lax.fori_loop(0, GROUP_PAIRS, finish, 0, unroll=UNROLL)


def norm_back_kernel(
    group, place_ref, own_ref, other_ref, y_ref, z_ref, c_ref, gain_ref, run_ref, run_col_ref, *rest
):
    first_ref, rest = (rest[0], rest[1:]) if group else (None, rest)
    grad_y_ref, grad_z_ref, gain_sum_ref, start_ref = rest[:4]
    outs, (power, along) = rest[4:-2], rest[-2:]
    reads = c_ref[...]
    power[...] = jnp.zeros_like(power)
    along[...] = jnp.zeros_like(along)

    def pieces(at):
        lanes = lanes_of(at)
        upstream = own_ref[:, lanes] + other_ref[:, lanes].astype(f32)
        gate = z_ref[:, lanes].astype(f32)
        sigmoid = 1.0 / (1.0 + jnp.exp(-gate))
        y = y_ref[:, lanes]
        return lanes, upstream, gate, sigmoid, y, y * gate * sigmoid

    def first(at, carry):
        lanes, upstream, gate, sigmoid, y, gated = pieces(at)
        power[...] += gated * gated
        along[...] += upstream * gain_ref[:, lanes] * gated
        return carry

    lax.fori_loop(0, GROUP_PAIRS, first, 0, unroll=UNROLL)
    mean = jnp.sum(power[...], axis=1, keepdims=True) * (1.0 / GROUP_CHANNELS)
    scale = lax.rsqrt(mean + EPSILON)
    shared = jnp.sum(along[...], axis=1, keepdims=True) * (1.0 / GROUP_CHANNELS)
    pull = jnp.broadcast_to(scale * scale * scale * shared, (TOKENS, 128))
    scale = jnp.broadcast_to(scale, (TOKENS, 128))

    def second(at, carry):
        lanes, upstream, gate, sigmoid, y, gated = pieces(at)
        grad_gated = scale * (upstream * gain_ref[:, lanes]) - gated * pull
        grad_y = grad_gated * (gate * sigmoid)
        grad_y_ref[:, lanes] = grad_y.astype(bf16)
        slope = sigmoid * (1.0 + gate * (1.0 - sigmoid))
        grad_z_ref[:, lanes] = (grad_gated * y * slope).astype(bf16)
        gain_sum_ref[:, lanes] = jnp.sum(upstream * gated * scale, axis=0, keepdims=True)
        pair = group * GROUP_PAIRS + at
        reach = jnp.exp(dot(run_col_ref[...], pair_select(pair, P_SIZE)))
        start_ref[lanes, :] = dot_columns((grad_y * reach).astype(bf16), reads)
        return carry

    lax.fori_loop(0, GROUP_PAIRS, second, 0, unroll=UNROLL)
    total = jnp.exp(run_ref[group * PER_GROUP : (group + 1) * PER_GROUP, TOKENS - 1 :])
    high, low = split2(jnp.broadcast_to(total, (PER_GROUP, 128)))
    states = start_ref[...].astype(bf16)
    if first_ref is None:
        ref = outs[0]
        ref[:STATE_ROWS, :] = states
        ref[STATE_ROWS : STATE_ROWS + PER_GROUP, :] = high
        ref[STATE_ROWS + PER_GROUP :, :] = low
    else:
        message = jnp.concatenate([states, high, low], axis=0)
        leads = place_ref[3] == 0
        outs[0][...] = jnp.where(leads, first_ref[...], message)
        outs[1][...] = jnp.where(leads, message, first_ref[...])


QUARTER = STATE_ROWS // 4
QUARTER_HEADS = PER_GROUP // 4


def by_head(decay):
    heads = decay.shape[0]
    return jnp.broadcast_to(decay[:, None, :], (heads, P_SIZE, N)).reshape(heads * P_SIZE, N)


def decay_of(message):
    first = message[STATE_ROWS : STATE_ROWS + PER_GROUP, :].astype(f32)
    return first + message[STATE_ROWS + PER_GROUP :, :].astype(f32)


def state_of(message):
    return message[:STATE_ROWS, :].astype(f32)


def put_quarter(ref, state, decay):
    ref[:QUARTER, :] = state.astype(bf16)
    high, low = split2(decay)
    ref[QUARTER:, :] = jnp.concatenate([high.astype(f32), low.astype(f32)], axis=0).astype(bf16)


def quarter_of(message):
    decay = message[QUARTER:, :].astype(f32)
    return message[:QUARTER, :].astype(f32), decay[:8] + decay[8:]


def chip_kernel(place_ref, keep_ref, got_ref, *refs):
    outs, last_ref, states, decays = refs[:4], refs[4], refs[5], refs[6]
    leads = place_ref[3] == 0
    keep, got = keep_ref[...], got_ref[...]
    early, late = jnp.where(leads, keep, got), jnp.where(leads, got, keep)
    decay = decay_of(early)
    states[...] = state_of(early) + by_head(decay) * state_of(late)
    decay = decay * decay_of(late)
    decays[...] = jnp.zeros_like(decays)
    for at in range(4):
        decays[at, :QUARTER_HEADS, :] = decay[at * QUARTER_HEADS : (at + 1) * QUARTER_HEADS]
    for by, ref in enumerate(outs):
        at = (place_ref[2] + by) & 3
        put_quarter(ref, states[pl.ds(pl.multiple_of(at * QUARTER, QUARTER), QUARTER), :], decays[at])
    last_ref[...] = late


def row_kernel(place_ref, own_ref, one_ref, two_ref, three_ref, row_ref, after_ref, reach_ref, held):
    for k, ref in enumerate((own_ref, one_ref, two_ref, three_ref)):
        held[k] = ref[...]
    z = place_ref[2]
    state = jnp.zeros((QUARTER, N), f32)
    decay = jnp.ones((8, N), f32)
    for at in (3, 2, 1, 0):
        after_ref[at] = state
        reach_ref[at] = decay
        here_state, here = quarter_of(held[(at - z) & 3])
        state = here_state + by_head(here[:QUARTER_HEADS]) * state
        decay = here * decay
    put_quarter(row_ref, state, decay)


def end_kernel(place_ref, one_ref, two_ref, three_ref, after_ref, reach_ref, *outs):
    state = jnp.zeros((QUARTER, N), f32)
    for ref in (three_ref, two_ref, one_ref):
        here_state, here = quarter_of(ref[...])
        state = here_state + by_head(here[:QUARTER_HEADS]) * state
    for by, ref in enumerate(outs):
        at = (place_ref[2] + by) & 3
        reach = reach_ref[at]
        ref[...] = (after_ref[at] + by_head(reach[:QUARTER_HEADS]) * state).astype(bf16)


def last_kernel(place_ref, own_ref, one_ref, two_ref, three_ref, last_ref, mine_ref, send_ref, late):
    for by, ref in enumerate((own_ref, one_ref, two_ref, three_ref)):
        at = (place_ref[2] - by) & 3
        late[pl.ds(pl.multiple_of(at * QUARTER, QUARTER), QUARTER), :] = ref[...]
    message = last_ref[...]
    early = (state_of(message) + by_head(decay_of(message)) * late[...].astype(f32)).astype(bf16)
    leads = place_ref[3] == 0
    mine_ref[...] = jnp.where(leads, early, late[...])
    send_ref[...] = jnp.where(leads, late[...], early)


def scan_back_kernel(
    group, x_ref, b_ref, c_ref, run_ref, run_col_ref, dt_col_ref, state_ref, grad_y_ref,
    inner_ref, grad_c_ref, grad_b_ref, row_ref, col_ref, skip_sum_ref,
    scores, back, reads_back, skips,
):
    upper = iota((Q, Q), 0) <= iota((Q, Q), 1)
    skips[...] = jnp.zeros_like(skips)
    col_ref[...] = jnp.zeros_like(col_ref)
    lane = iota((Q, 128), 1)
    keys = b_ref[...]
    reads = c_ref[...]
    scores[...] = dot_rows(keys, reads)
    back[...] = jnp.zeros_like(back)
    reads_back[...] = jnp.zeros_like(reads_back)

    def body(at, carry):
        pair = group * GROUP_PAIRS + at
        lanes = lanes_of(at)
        xs = x_ref[:, lanes].astype(f32)
        grads = grad_y_ref[:, lanes]
        step = dot(dt_col_ref[...], pair_select(pair, P_SIZE))
        scaled = halves((step * xs).astype(bf16))
        split = halves(grads)
        expanded = dot(run_col_ref[...], pair_select(pair, 128))
        top, bottom = [], []
        for k in range(2):
            head = 2 * pair + k
            run_row = run_ref[pl.ds(head, 1), :]
            col = expanded[:, k * 128 : (k + 1) * 128]
            d0 = dot_rows(scaled[k][:Q], grads)
            d11 = dot_rows(scaled[k][Q:], grads[Q:])
            l00 = causal_exp(run_row[:, :Q] - col[:Q], upper)
            l01 = jnp.exp(run_row[:, Q:] - col[:Q])
            l11 = causal_exp(run_row[:, Q:] - col[Q:], upper)
            p00, p01, p11 = l00 * d0[:, :Q], l01 * d0[:, Q:], l11 * d11
            back[:Q, :Q] += p00
            back[:Q, Q:] += p01
            back[Q:, Q:] += p11
            s00, s01, s11 = scores[:Q, :Q], scores[:Q, Q:], scores[Q:, Q:]
            w00, w01, w11 = p00 * s00, p01 * s01, p11 * s11
            row_ref[0, pl.ds(2 * at + k, 1), :] = jnp.sum(w00, axis=0, keepdims=True)
            row_ref[1, pl.ds(2 * at + k, 1), :] = jnp.sum(w01 + w11, axis=0, keepdims=True)
            col_ref[:Q, :] -= jnp.where(lane == head, jnp.sum(w00 + w01, axis=1, keepdims=True), 0.0)
            col_ref[Q:, :] -= jnp.where(lane == head, jnp.sum(w11, axis=1, keepdims=True), 0.0)
            top.extend([(l00 * s00).astype(bf16), (l01 * s01).astype(bf16)])
            bottom.append((l11 * s11).astype(bf16))
        inner_ref[:Q, lanes] = dot(jnp.concatenate(top, axis=1), jnp.concatenate(split, axis=0))
        inner_ref[Q:, lanes] = dot(
            jnp.concatenate(bottom, axis=1),
            jnp.concatenate([split[0][Q:], split[1][Q:]], axis=0),
        )
        state = state_ref[lanes_of(pair), :].astype(bf16)
        first = iota((TOKENS, 128), 1) < P_SIZE
        reach = jnp.exp(jnp.where(first, expanded[:, :128], expanded[:, 128:]))
        wide = grads.astype(f32)
        reached = reach * wide
        reads_back[...] += dot(reached.astype(bf16), state)
        col_ref[...] += pair_sums(reached * dot_rows(reads, state), pair)
        skips[...] += pair_sums(xs * wide, pair)
        return carry

    lax.fori_loop(0, GROUP_PAIRS, body, 0, unroll=UNROLL)
    inner = back[...].astype(bf16)
    grad_b_ref[...] = dot(inner, reads)
    grad_c_ref[...] = (
        dot_columns(inner, keys) + reads_back[...]
    ).astype(bf16)
    skip_sum_ref[...] = jnp.sum(skips[...], axis=0, keepdims=True)


def end_back_kernel(
    place_ref, x_ref, b_ref, dt_ref, rate_ref, skip_ref, run_ref, run_col_ref, dt_col_ref,
    state_ref, mine_ref, got_ref, *refs
):
    per_group, rest = (refs[:8], refs[8:16]), refs[16:]
    end_back_body(
        place_ref, x_ref, b_ref, dt_ref, rate_ref, skip_ref, run_ref, run_col_ref, dt_col_ref,
        state_ref, mine_ref, got_ref, per_group, *rest
    )


def end_back_body(
    place_ref, x_ref, b_ref, dt_ref, rate_ref, skip_ref, run_ref, run_col_ref, dt_col_ref,
    state_ref, mine_ref, got_ref, per_group,
    grad_x_ref, grad_b_ref, grad_dt_ref, grad_start_ref, sums_ref,
    ends, decay, directs, tails, products,
):
    core = place_ref[3]
    ends[pl.ds(pl.multiple_of(core * STATE_ROWS, STATE_ROWS), STATE_ROWS), :] = mine_ref[...]
    ends[pl.ds(pl.multiple_of((1 - core) * STATE_ROWS, STATE_ROWS), STATE_ROWS), :] = got_ref[...]
    run = run_ref[...]
    total = jnp.exp(run[:, TOKENS - 1 : TOKENS])
    decay[...] = jnp.broadcast_to(total, (HEADS, 128))
    directs[...] = jnp.zeros_like(directs)
    tails[...] = jnp.zeros_like(tails)
    for group in range(GROUPS):
        grad_y_ref, inner_ref, keys_back_ref, _, _, _, start_ref, _ = per_group[group]
        keys = b_ref[:, group * N : (group + 1) * N]

        def body(at, keys_back):
            pair = group * GROUP_PAIRS + at
            lanes, local = lanes_of(pair), lanes_of(at)
            end = ends[lanes, :]
            wide_end = end.astype(f32)
            xs = x_ref[:, lanes].astype(f32)
            step = dot(dt_col_ref[...], pair_select(pair, P_SIZE))
            running = dot(run_col_ref[...], pair_select(pair, P_SIZE))
            tail = jnp.exp(running[TOKENS - 1 :, :] - running)
            read = dot_rows(keys, end)
            tailed = tail * (step * xs)
            grad_scaled = inner_ref[:, local] + tail * read
            grad_x = step * grad_scaled + skip_ref[:, lanes] * grad_y_ref[:, local].astype(f32)
            grad_x_ref[:, lanes] = grad_x.astype(bf16)
            directs[...] += pair_sums(xs * grad_scaled, pair)
            tails[...] += pair_sums(tailed * read, pair)
            product = wide_end * state_ref[lanes, :]
            for k in range(2):
                head = 2 * pair + k
                half = slice(k * P_SIZE, (k + 1) * P_SIZE)
                products[pl.ds(head, 1), :] = jnp.sum(product[half], axis=0, keepdims=True)
                rows = pl.ds(pl.multiple_of(head * P_SIZE, P_SIZE), P_SIZE)
                own = pl.ds(pl.multiple_of((2 * at + k) * P_SIZE, P_SIZE), P_SIZE)
                grad_start_ref[rows, :] = start_ref[own, :] + decay[pl.ds(head, 1), :] * wide_end[half]
            return keys_back + dot(tailed.astype(bf16), end)

        keys_back = lax.fori_loop(
            0, GROUP_PAIRS, body, keys_back_ref[...], unroll=UNROLL
        )
        grad_b_ref[:, group * N : (group + 1) * N] = keys_back.astype(bf16)
    tail_rows = tails[...].T[:HEADS]
    shared = jnp.sum(tail_rows, axis=1, keepdims=True)
    shared = shared + total * jnp.sum(products[...], axis=1, keepdims=True)
    rows = [jnp.concatenate([group[3][0], group[3][1]], axis=1) for group in per_group]
    columns = per_group[0][4][...] + per_group[1][4][...] - tails[...]
    here = jnp.concatenate(rows, axis=0) + columns.T[:HEADS]
    since = jnp.where(iota((TOKENS, TOKENS), 0) >= iota((TOKENS, TOKENS), 1), 1.0, 0.0).astype(bf16)
    grad_log = exact_rows(here, since) + shared
    grad_dt = directs[...].T[:HEADS] - rate_ref[...] * grad_log
    spent = -dt_ref[...] * grad_log
    zero = jnp.zeros_like(spent)
    columns = jnp.concatenate([grad_dt, spent, zero, zero], axis=0).T
    grad_dt_ref[...] = columns[:, :HEADS]
    sums = jnp.sum(columns, axis=0, keepdims=True)
    for group in range(GROUPS):
        own = slice(group * GROUP_CHANNELS, (group + 1) * GROUP_CHANNELS)
        sums_ref[:, own] = per_group[group][7][...]
    skips = per_group[0][5][...] + per_group[1][5][...]
    sums_ref[:, CHANNELS:] = jnp.where(iota((1, 128), 1) < HEADS, skips, sums)


def call(kernel, outs, scratch, scalars, *arrays, flops=0, limit=24, after=()):
    specs = [pl.BlockSpec(memory_space=pltpu.SMEM)] * scalars
    plain, size = list(arrays[:scalars]), 0
    for array in arrays[scalars:]:
        array, group = array if isinstance(array, tuple) else (array, None)
        shape = array.shape
        if group is None:
            specs.append(pl.BlockSpec(shape, lambda i, n=len(shape): (0,) * n))
        else:
            shape = shape[:-1] + (shape[-1] // GROUPS,)
            specs.append(pl.BlockSpec(shape, lambda i, group=group: (0, group)))
        size += math.prod(shape) * array.dtype.itemsize
        plain.append(array)
    size += sum(math.prod(shape) * jnp.dtype(kind).itemsize for shape, kind in outs)
    used = len(plain)

    def body(*refs):
        kernel(*refs[:used], *refs[used + len(after) :])

    return pl.pallas_call(
        body,
        grid=(1,),
        out_shape=[jax.ShapeDtypeStruct(shape, kind) for shape, kind in outs],
        in_specs=specs + [pl.BlockSpec(memory_space=pl.ANY)] * len(after),
        out_specs=[pl.BlockSpec(shape, lambda i, n=len(shape): (0,) * n) for shape, _ in outs],
        scratch_shapes=[pltpu.VMEM(shape, kind) for shape, kind in scratch],
        name=getattr(kernel, "func", kernel).__name__,
        compiler_params=pltpu.CompilerParams(vmem_limit_bytes=limit * 2**20),
        cost_estimate=pl.CostEstimate(flops=flops, bytes_accessed=size, transcendentals=0),
    )(*plain, *after)


WIDE = (TOKENS, GROUP_CHANNELS)


def prepare(place, dout, steps, rate):
    return call(
        prepare_kernel,
        [((TOKENS, 512), bf16)] * 2
        + [((HEADS, TOKENS), f32), ((TOKENS, 128), bf16), ((TOKENS, 128), bf16)],
        [], 1, place, dout, steps, rate,
    )


def forward(group, x, z, b, c, steps, run, run_col, state, gain, skip, after):
    return call(
        functools.partial(forward_kernel, group),
        [(WIDE, f32), (WIDE, bf16)],
        [((TOKENS, TOKENS), f32), (WIDE, f32), ((TOKENS, 128), f32)],
        0, (x, group), (z, group), (b, group), (c, group), steps, run, run_col,
        state, (gain, group), (skip, group), flops=SHORT, after=after,
    )


MESSAGE = ((STATE_ROWS + 2 * PER_GROUP, N), bf16)


def norm_back(group, place, own, other, y, z, c, gain, run, run_col, first, after):
    outs = [(WIDE, bf16), (WIDE, bf16), ((1, GROUP_CHANNELS), f32), ((STATE_ROWS, N), f32), MESSAGE]
    return call(
        functools.partial(norm_back_kernel, group),
        outs + ([MESSAGE] if group else []),
        [((TOKENS, 128), f32), ((TOKENS, 128), f32)],
        1, place, own, other, y, (z, group), (c, group), (gain, group), run, run_col, *first,
        flops=LONG, after=after,
    )


PART = ((QUARTER + 16, N), bf16)


def chip_state(place, keep, got):
    return call(
        chip_kernel, [PART] * 4 + [MESSAGE], [((STATE_ROWS, N), f32), ((4, 8, N), f32)],
        1, place, keep, got,
    )


def row_state(place, own, one, two, three, after):
    return call(
        row_kernel, [PART, ((4, QUARTER, N), f32), ((4, 8, N), f32)],
        [((4, QUARTER + 16, N), bf16)], 1, place, own, one, two, three, after=after,
    )


def end_state(place, one, two, three, follows, reach, after):
    return call(
        end_kernel, [((QUARTER, N), bf16)] * 4, [], 1, place, one, two, three, follows, reach,
        after=after,
    )


def last_state(place, own, one, two, three, last):
    return call(
        last_kernel, [((STATE_ROWS, N), bf16)] * 2, [((STATE_ROWS, N), bf16)],
        1, place, own, one, two, three, last,
    )


def scan_back(group, x, b, c, run, run_col, dt_col, state, grad_y, after):
    return call(
        functools.partial(scan_back_kernel, group),
        [(WIDE, f32), ((TOKENS, N), bf16), ((TOKENS, N), f32), ((2, PER_GROUP, Q), f32),
         ((TOKENS, 128), f32), ((1, 128), f32)],
        [((TOKENS, TOKENS), f32), ((TOKENS, TOKENS), f32), ((TOKENS, N), f32), ((TOKENS, 128), f32)],
        0, (x, group), (b, group), (c, group), run, run_col, dt_col, state, grad_y,
        flops=LONG, after=after,
    )


def end_back(place, *arrays, after):
    return call(
        end_back_kernel,
        [((TOKENS, CHANNELS), bf16), ((TOKENS, GROUPS * N), bf16), ((TOKENS, HEADS), f32),
         ((CHANNELS, N), f32), ((1, CHANNELS + 128), f32)],
        [((CHANNELS, N), bf16), ((HEADS, 128), f32), ((TOKENS, 128), f32), ((TOKENS, 128), f32),
         ((HEADS, 128), f32)],
        1, place, *arrays, flops=LONG, limit=32, after=after,
    )


HALF = CHANNELS // 2
TILE = 512


def turn_kernel(place_ref, own_ref, before_ref, after_ref, far0_ref, far1_ref, pieces_ref, turned_ref):
    far = jnp.concatenate([far0_ref[...], far1_ref[...]], axis=0)
    for by, piece in ((0, own_ref[...]), (-1, before_ref[...]), (1, after_ref[...]), (2, far)):
        at = (place_ref[0] + by) & 3
        rows = pl.ds(pl.multiple_of(at * 512, 512), 512)
        pieces_ref[rows, :] = piece
        turned_ref[rows, :] = piece.T


def turn(place, *pieces, after):
    return call(
        turn_kernel, [((2048, 512), bf16)] * 2, [], 1, place, *pieces, flops=SHORT, after=after
    )


def weight_grad_kernel(turned_ref, own0_ref, other0_ref, own1_ref, other1_ref, out_ref):
    first = pl.program_id(0) < HALF // TILE
    own = jnp.where(first, own0_ref[...], own1_ref[...])
    other = jnp.where(first, other0_ref[...], other1_ref[...])
    right = jnp.concatenate([own, other], axis=0)
    for at in range(0, 2048, 512):
        out_ref[at : at + 512, :] = dot(turned_ref[at : at + 512, :], right).astype(bf16)


def weight_grad(turned, *normed):
    last = HALF // TILE - 1
    early = pl.BlockSpec((TOKENS, TILE), lambda i: (0, jnp.minimum(i, last)))
    late = pl.BlockSpec((TOKENS, TILE), lambda i: (0, jnp.maximum(i - last - 1, 0)))
    return pl.pallas_call(
        weight_grad_kernel,
        name="weight_grad",
        grid=(CHANNELS // TILE,),
        out_shape=jax.ShapeDtypeStruct((2048, CHANNELS), bf16),
        in_specs=[pl.BlockSpec((2048, 512), lambda i: (0, 0)), early, early, late, late],
        out_specs=pl.BlockSpec((2048, TILE), lambda i: (0, i)),
        compiler_params=pltpu.CompilerParams(vmem_limit_bytes=24 * 2**20),
        cost_estimate=pl.CostEstimate(flops=SHORT, bytes_accessed=1024, transcendentals=0),
    )(turned, *normed)


def upstream_whole_kernel(half, place_ref, pieces_ref, weight_ref, *refs):
    own_ref, other_ref = refs[-2:]
    total = None
    for at in range(0, 2048, 512):
        product = dot(pieces_ref[at : at + 512, :], weight_ref[at : at + 512, :])
        total = product if total is None else total + product
    own_ref[...] = total[:TOKENS]
    other_ref[...] = total[TOKENS:].astype(bf16)


def upstream(kernel, half, place, pieces, arrays, outs, after):
    return pl.pallas_call(
        functools.partial(kernel, half),
        name=f"{kernel.__name__}_{half}",
        grid=(HALF // TILE,),
        out_shape=[jax.ShapeDtypeStruct((rows, HALF), kind) for rows, kind in outs],
        in_specs=[pl.BlockSpec(memory_space=pltpu.SMEM), pl.BlockSpec((2048, 512), lambda i: (0, 0))]
        + [pl.BlockSpec((a.shape[0], TILE), lambda i: (0, half * (HALF // TILE) + i)) for a in arrays]
        + [pl.BlockSpec(memory_space=pl.ANY)] * len(after),
        out_specs=[pl.BlockSpec((rows, TILE), lambda i: (0, i)) for rows, _ in outs],
        compiler_params=pltpu.CompilerParams(vmem_limit_bytes=24 * 2**20),
        cost_estimate=pl.CostEstimate(flops=SHORT, bytes_accessed=1024, transcendentals=0),
    )(place, pieces, *arrays, *after)


def upstream_whole(half, place, pieces, weights, after):
    outs = [(TOKENS, f32), (TOKENS, bf16)]
    return upstream(upstream_whole_kernel, half, place, pieces, (weights,), outs, after)


def device(y, z, core):
    return (y * 4 + z) * 2 + core


PLACES = [(y, z, core) for y in range(4) for z in range(4) for core in range(2)]
SAME_CORE = [[device(y, z, core) for y in range(4) for z in range(4)] for core in range(2)]
SWAP = [(device(y, z, core), device(y, z, 1 - core)) for y, z, core in PLACES]


def along_z(by):
    return [(device(y, z, core), device(y, (z + by) % 4, core)) for y, z, core in PLACES]


def along_y(by):
    return [(device(y, z, core), device((y + by) % 4, z, core)) for y, z, core in PLACES]


def earlier_y(by):
    return [(device(y, z, core), device(y - by, z, core)) for y, z, core in PLACES if y >= by]


def move(array, pairs):
    return lax.ppermute(array, "ctx", pairs)


def along_x(array, by):
    return lax.ppermute(array, "head", [(x, (x + by) % 4) for x in range(4)])


def sum_ctx(array):
    array = array + move(array, SWAP)
    array = array + move(array, along_z(1)) + move(array, along_z(2)) + move(array, along_z(3))
    return array + move(array, along_y(1)) + move(array, along_y(2)) + move(array, along_y(3))


def per_device(dout, out_weight, x_in, z_in, b_in, c_in, dt, rate, skip, gain, start_state):
    at = lax.axis_index("ctx")
    place = jnp.stack([lax.axis_index("head"), at // 8, (at // 2) % 4, at % 2]).astype(jnp.int32)
    steps = dt.T
    rates = rate.reshape(HEADS, 1)
    skips = jnp.repeat(skip, P_SIZE).reshape(1, CHANNELS)
    gains = gain.reshape(1, CHANNELS)
    state = start_state.reshape(CHANNELS, N)
    weights = lax.all_gather(out_weight, "ctx", axis=0, tiled=True, axis_index_groups=SAME_CORE)
    keep, send, run, run_col, dt_col = prepare(place, dout, steps, rates)
    both = jnp.concatenate([keep, move(send, SWAP)], axis=0)
    x_before, x_after = along_x(both, 1), along_x(both, -1)
    scan_in = (x_in, z_in, b_in, c_in, steps, run, run_col, state, gains, skips)
    y0, normed0 = forward(0, *scan_in, (both,))
    y1, normed1 = forward(1, *scan_in, (normed0, x_before, x_after))
    x_far = along_x(x_before[:TOKENS], 1), along_x(x_after[TOKENS:], -1)
    other0, other1 = move(normed0, SWAP), move(normed1, SWAP)
    pieces, turned = turn(place, both, x_before, x_after, *x_far, after=(normed1,))
    term = weight_grad(turned, normed0, other0, normed1, other1)
    grad_w = lax.psum_scatter(
        term, "ctx", scatter_dimension=0, tiled=True, axis_index_groups=SAME_CORE
    )
    part0, send0 = upstream_whole(0, place, pieces, weights, (term,))
    part1, send1 = upstream_whole(1, place, pieces, weights, (part0,))
    back_in = (z_in, c_in, gains, run, run_col)
    grad_y0, grad_z0, gain_sum0, start0, message0 = norm_back(
        0, place, part0, move(send0, SWAP), y0, *back_in, (), (part1,)
    )
    grad_y1, grad_z1, gain_sum1, start1, keep, send = norm_back(
        1, place, part1, move(send1, SWAP), y1, *back_in, (message0,), (grad_y0,)
    )
    *quarters, last = chip_state(place, keep, move(send, SWAP))
    from_z = [move(quarters[-k], along_z(-k)) for k in (1, 2, 3)]
    back0 = scan_back(
        0, x_in, b_in, c_in, run, run_col, dt_col, state, grad_y0, (quarters[0],)
    )
    row, after, reach = row_state(place, quarters[0], *from_z, after=(back0[0],))
    from_y = [move(row, earlier_y(k)) for k in (1, 2, 3)]
    back1 = scan_back(
        1, x_in, b_in, c_in, run, run_col, dt_col, state, grad_y1, (row,)
    )
    ends = end_state(place, *from_y, after, reach, after=(back1[0],))
    mine, theirs = last_state(place, ends[0], *[move(ends[k], along_z(k)) for k in (1, 2, 3)], last)
    grad_x, grad_b, grad_dt, grad_start, sums = end_back(
        place, x_in, b_in, steps, rates, skips, run, run_col, dt_col, state, mine,
        move(theirs, SWAP),
        grad_y0, *[back0[i] for i in (0, 2, 3, 4, 5)], start0, gain_sum0,
        grad_y1, *[back1[i] for i in (0, 2, 3, 4, 5)], start1, gain_sum1,
        after=(),
    )
    sums = sum_ctx(sums)[0]
    return (
        grad_x,
        jnp.concatenate([grad_z0, grad_z1], axis=1),
        grad_b,
        jnp.concatenate([back0[1], back1[1]], axis=1),
        grad_dt,
        grad_w,
        sums[:CHANNELS],
        sums[CHANNELS + HEADS : CHANNELS + 2 * HEADS],
        sums[CHANNELS : CHANNELS + HEADS],
        grad_start.reshape(start_state.shape),
    )


def solution(mesh):
    full, whole = P("ctx", "head"), P("head")
    state = P("ctx", "head", None, None)
    return jax.shard_map(
        per_device,
        mesh=mesh,
        in_specs=(full,) * 7 + (whole,) * 3 + (state,),
        out_specs=(full,) * 6 + (whole,) * 3 + (state,),
        check_vma=False,
    )
```

time: 220 us -> 184 us (0.84)
  Pallas kernels: 76.3 us -> 50.5 us
  waiting for transfers between devices: 88.7 us -> 64.8 us
  local copies, waits for them, and re-layouts: 11.8 us -> 24 us
    ppermute x18 -> x23, waiting for transfers between devices: 50.5 us -> 21.2 us  [move(): return lax.ppermute(array, 'ctx', pairs)]
    pallas_call x10 -> x16, Pallas kernels: 76.3 us -> 50.5 us  [the longest x13 37.9 us: call(): pl.pallas_call(body, grid=(1,), out_shape=[jax.ShapeDtypeStruct(shape, ki...]
    unnamed x35 -> x54, local copies, waits for them, and re-layouts: 7.87 us -> 18.6 us
    reduce_scatter x1, waiting for transfers between devices: 0.01 us -> 5.82 us  [per_device(): lax.psum_scatter(term, 'ctx', scatter_dimension=0, tiled=True, axis_index...]
    ppermute x18 -> x23, starting transfers between devices: 16.3 us -> 21.1 us  [move(): return lax.ppermute(array, 'ctx', pairs)]
    ppermute x6 -> x4, starting transfers between devices: 10.2 us -> 6.62 us  [along_x(): return lax.ppermute(array, 'head', [(x, (x + by) % 4) for x in range(4)])]
    ppermute x6 -> x4, waiting for transfers between devices: 11.3 us -> 11.3 us  [along_x(): return lax.ppermute(array, 'head', [(x, (x + by) % 4) for x in range(4)])]
  transfers between devices with their start and end apart: 26 -> 29, of which waited for: 16 -> 20; matrix products, arithmetic and copies ran while one was open for 3% -> 5% of each run, Pallas kernels for 35% -> 28%
where the time goes in v1:
time: 184 us; the launch traced here: 183 us
  waiting for transfers between devices  64.8 us (35%)
  Pallas kernels  50.5 us (27%)
  starting transfers between devices  27.8 us (15%)
  local copies, waits for them, and re-layouts  24 us (13%)
  between operations  14.5 us (8%)
  other arithmetic  1.85 us (1%)
    pallas_call x13, Pallas kernels, call(): pl.pallas_call(body, grid=(1,), out_shape=[jax.ShapeDtypeStruct(shape, ki...  37.9 us
    all_gather x1, waiting for transfers between devices, per_device(): lax.all_gather(out_weight, 'ctx', axis=0, tiled=True, axis_index_groups=S...  25.8 us
    ppermute x23, waiting for transfers between devices, move(): return lax.ppermute(array, 'ctx', pairs)  21.2 us
    ppermute x23, starting transfers between devices, move(): return lax.ppermute(array, 'ctx', pairs)  21.1 us
    unnamed x54, local copies, waits for them, and re-layouts  18.6 us
    ppermute x4, waiting for transfers between devices, along_x(): return lax.ppermute(array, 'head', [(x, (x + by) % 4) for x in range(4)])  11.3 us
    pallas_call x2, Pallas kernels, upstream(): pl.pallas_call(functools.partial(kernel, half), name=f'{kernel.__name__}_...  6.66 us
    ppermute x4, starting transfers between devices, along_x(): return lax.ppermute(array, 'head', [(x, (x + by) % 4) for x in range(4)])  6.62 us
  transfers between devices with their start and end apart: 29, of which 20 were waited for; matrix products, arithmetic and copies ran while one was open for 5% of the time, Pallas kernels for 28%

profile of v1, /device:TPU:0, one launch (start us, length us, event | category | flops | bytes accessed | tf_op | source)
XLA Modules:
  0.0 183.4 jit_solution(2551355048334475025)
XLA Ops:
  21.6 3.2 %forward_kernel.2 = (f32[256,1024]{1,0:T(8,128)S(1)}, bf16[256,1024]{1,0:T(8,128)(2,1)S(1)}) custom-call(bf16[256,2048]{1,0:T(8,128)(2,1)S(1)} %copy-done.4, bf16[256,2048]{1,0:T(8,128)(2,1)S(1)} %copy-done.3, bf16[256,256]{1,0:T(8,128)(2,1)S(1)} %copy-done.9, bf16[256,256]{1,0:T(8,128)(2,1)S(1)} %copy-done.8, f32[32,256]{1,0:T(8,128)S(1)} %bitcast.20, ...), custom_call_target="tpu_custom_call" | custom-call | flops 100000000 | bytes 3940352 | tf_op jit(solution)/shard_map/forward_kernel/pallas_call | solution.py:479
  24.9 4.5 %collective-permute-done.1.refs_11_.refs_2_ = bf16[512,512]{1,0:T(8,128)(2,1)} collective-permute-done((bf16[512,512]{1,0:T(8,128)(2,1)}, bf16[512,512]{1,0:T(8,128)(2,1)}, u32[]{:S(2)}, u32[]{:S(2)}) %collective-permute-start.1) | collective-permute-done | bytes 524320 | tf_op jit(solution)/shard_map/ppermute | solution.py:681
  30.2 3.2 %forward_kernel.3 = (f32[256,1024]{1,0:T(8,128)S(1)}, bf16[256,1024]{1,0:T(8,128)(2,1)S(1)}) custom-call(bf16[256,2048]{1,0:T(8,128)(2,1)S(1)} %copy-done.4, bf16[256,2048]{1,0:T(8,128)(2,1)S(1)} %copy-done.3, bf16[256,256]{1,0:T(8,128)(2,1)S(1)} %copy-done.10, bf16[256,256]{1,0:T(8,128)(2,1)S(1)} %copy-done.8, f32[32,256]{1,0:T(8,128)S(1)} %bitcast.21, ...), custom_call_target="tpu_custom_call" | custom-call | flops 100000000 | bytes 3940352 | tf_op jit(solution)/shard_map/forward_kernel/pallas_call | solution.py:479
  39.7 5.7 %collective-permute-done.3.refs_4_ = bf16[256,512]{1,0:T(8,128)(2,1)S(1)} collective-permute-done((bf16[256,512]{1,0:T(8,128)(2,1)S(1)}, bf16[256,512]{1,0:T(8,128)(2,1)S(1)}, u32[]{:S(2)}, u32[]{:S(2)}) %collective-permute-start.3) | collective-permute-done | bytes 262176 | tf_op jit(solution)/shard_map/ppermute | solution.py:681
  46.4 2.2 %turn_kernel.1 = (bf16[2048,512]{1,0:T(8,128)(2,1)S(1)}, bf16[2048,512]{1,0:T(8,128)(2,1)S(1)}) custom-call(s32[4]{0:T(128)S(1)} %pad_add_fusion.refs_0_.place_ref, bf16[512,512]{1,0:T(8,128)(2,1)} %constant_dynamic-update-slice_fusion.refs_10_.refs_1_, bf16[512,512]{1,0:T(8,128)(2,1)} %collective-permute-done.1.refs_11_.refs_2_, ...), custom_call_target="tpu_custom_call" | custom-call | flops 100000000 | bytes 6291456 | tf_op jit(solution)/shard_map/turn_kernel/pallas_call | solution.py:479
  48.6 5.9 %weight_grad.1.refs_0_ = bf16[2048,2048]{1,0:T(8,128)(2,1)S(1)} custom-call(bf16[2048,512]{1,0:T(8,128)(2,1)S(1)} %get-tuple-element.75.turned_ref, bf16[256,1024]{1,0:T(8,128)(2,1)S(1)} %get-tuple-element.72.refs_10_.own0_ref, bf16[256,1024]{1,0:T(8,128)(2,1)S(1)} %collective-permute-done.5.other0_ref, ...), custom_call_target="tpu_custom_call" | custom-call | flops 100000000 | bytes 1024 | tf_op jit(solution)/shard_map/weight_grad/pallas_call | solution.py:613
  54.6 3.3 %copy-done = bf16[2048,2048]{1,0:T(8,128)(2,1)} copy-done((bf16[2048,2048]{1,0:T(8,128)(2,1)}, bf16[2048,2048]{1,0:T(8,128)(2,1)S(1)}, u32[]{:S(2)}) %copy-start) | copy-done | bytes 8388632
  57.8 25.8 %all-gather.2.cloned.1.call-done.weight_ref = bf16[2048,2048]{1,0:T(8,128)(2,1)} async-done(((bf16[128,2048]{1,0:T(8,128)(2,1)}), bf16[2048,2048]{1,0:T(8,128)(2,1)}) %all-gather.2.cloned.1.call-update) | async-done | bytes 8388624 | tf_op jit(solution)/shard_map/all_gather | solution.py:698
  83.6 3.4 %copy-done.1 = bf16[2048,2048]{1,0:T(8,128)(2,1)S(1)} copy-done((bf16[2048,2048]{1,0:T(8,128)(2,1)S(1)}, bf16[2048,2048]{1,0:T(8,128)(2,1)}, u32[]{:S(2)}) %copy-start.1) | copy-done | bytes 8388632
  87.0 3.4 %copy-done.2 = bf16[2048,2048]{1,0:T(8,128)(2,1)S(1)} copy-done((bf16[2048,2048]{1,0:T(8,128)(2,1)S(1)}, bf16[2048,2048]{1,0:T(8,128)(2,1)}, u32[]{:S(2)}) %copy-start.2) | copy-done | bytes 8388632
  90.4 3.3 %upstream_whole_kernel_0.1 = (f32[256,1024]{1,0:T(8,128)S(1)}, bf16[256,1024]{1,0:T(8,128)(2,1)S(1)}) custom-call(s32[4]{0:T(128)S(1)} %pad_add_fusion.refs_0_.place_ref, bf16[2048,512]{1,0:T(8,128)(2,1)S(1)} %get-tuple-element.74.pieces_ref, bf16[2048,2048]{1,0:T(8,128)(2,1)S(1)} %copy-done.2, bf16[2048,2048]{1,0:T(8,128)(2,1)S(1)} %copy-done.1), custom_call_target="tpu_custom_call" | custom-call | flops 100000000 | bytes 1024 | tf_op jit(solution)/shard_map/upstream_whole_kernel_0/pallas_call | solution.py:636
  93.9 3.3 %upstream_whole_kernel_1.1 = (f32[256,1024]{1,0:T(8,128)S(1)}, bf16[256,1024]{1,0:T(8,128)(2,1)S(1)}) custom-call(s32[4]{0:T(128)S(1)} %pad_add_fusion.refs_0_.place_ref, bf16[2048,512]{1,0:T(8,128)(2,1)S(1)} %get-tuple-element.74.pieces_ref, bf16[2048,2048]{1,0:T(8,128)(2,1)S(1)} %copy-done.2, f32[256,1024]{1,0:T(8,128)S(1)} %get-tuple-element.76.refs_0_.refs_1_), custom_call_target="tpu_custom_call" | custom-call | flops 100000000 | bytes 1024 | tf_op jit(solution)/shard_map/upstream_whole_kernel_1/pallas_call | solution.py:636
  97.8 3.8 %norm_back_kernel.2 = (bf16[256,1024]{1,0:T(8,128)(2,1)S(1)}, bf16[256,1024]{1,0:T(8,128)(2,1)S(1)}, f32[1,1024]{1,0:T(1,128)S(1)}, f32[1024,128]{1,0:T(8,128)S(1)}, bf16[1056,128]{1,0:T(8,128)(2,1)S(1)}) custom-call(s32[4]{0:T(128)S(1)} %pad_add_fusion.refs_0_.place_ref, f32[256,1024]{1,0:T(8,128)S(1)} %get-tuple-element.76.refs_0_.refs_1_, ...), custom_call_target="tpu_custom_call" | custom-call | flops 20000000000 | bytes 5160960 | tf_op jit(solution)/shard_map/norm_back_kernel/pallas_call | solution.py:479
  101.6 3.9 %norm_back_kernel.3 = (bf16[256,1024]{1,0:T(8,128)(2,1)S(1)}, bf16[256,1024]{1,0:T(8,128)(2,1)S(1)}, f32[1,1024]{1,0:T(1,128)S(1)}, f32[1024,128]{1,0:T(8,128)S(...) custom-call(s32[4]{0:T(128)S(1)} %pad_add_fusion.refs_0_.place_ref, ...), custom_call_target="tpu_custom_call" | custom-call | flops 20000000000 | bytes 5701632 | tf_op jit(solution)/shard_map/norm_back_kernel/pallas_call | solution.py:479
  108.0 2.8 %collective-permute-start.10 = (bf16[272,128]{1,0:T(8,128)(2,1)S(1)}, bf16[272,128]{1,0:T(8,128)(2,1)S(1)}, u32[]{:S(2)}, u32[]{:S(2)}) collective-permute-start(bf16[272,128]{1,0:T(8,128)(2,1)S(1)} %get-tuple-element.87), channel_id=1, source_target_pairs={{0,24},{4,28},{8,0},{12,4},{16,8},{20,12},{24,16},{28,20},{32,56},... | collective-permute-start | bytes 208904 | tf_op jit(solution)/shard_map/ppermute | solution.py:677
  112.5 4.7 %scan_back_kernel.2 = (f32[256,1024]{1,0:T(8,128)S(1)}, bf16[256,128]{1,0:T(8,128)(2,1)S(1)}, f32[256,128]{1,0:T(8,128)S(1)}, f32[2,16,128]{2,1,0:T(8,128)S(1)},...) custom-call(bf16[256,2048]{1,0:T(8,128)(2,1)S(1)} %copy-done.5, bf16[256,256]{1,0:T(8,128)(2,1)S(1)} %copy-done.10, ...), custom_call_target="tpu_custom_call" | custom-call | flops 20000000000 | bytes 3785216 | tf_op jit(solution)/shard_map/scan_back_kernel/pallas_call | solution.py:479
  124.1 4.7 %scan_back_kernel.3 = (f32[256,1024]{1,0:T(8,128)S(1)}, bf16[256,128]{1,0:T(8,128)(2,1)S(1)}, f32[256,128]{1,0:T(8,128)S(1)}, f32[2,16,128]{2,1,0:T(8,128)S(1)},...) custom-call(bf16[256,2048]{1,0:T(8,128)(2,1)S(1)} %copy-done.5, bf16[256,256]{1,0:T(8,128)(2,1)S(1)} %copy-done.10, ...), custom_call_target="tpu_custom_call" | custom-call | flops 20000000000 | bytes 3785216 | tf_op jit(solution)/shard_map/scan_back_kernel/pallas_call | solution.py:479
  130.9 3.3 %collective-permute-done.15.refs_3_ = bf16[272,128]{1,0:T(8,128)(2,1)S(1)} collective-permute-done((bf16[272,128]{1,0:T(8,128)(2,1)S(1)}, bf16[272,128]{1,0:T(8,128)(2,1)S(1)}, u32[]{:S(2)}, u32[]{:S(2)}) %collective-permute-start.15) | collective-permute-done | bytes 69664 | tf_op jit(solution)/shard_map/ppermute | solution.py:677
  135.0 3.3 %collective-permute-start.17 = (bf16[256,128]{1,0:T(8,128)(2,1)S(1)}, bf16[256,128]{1,0:T(8,128)(2,1)S(1)}, u32[]{:S(2)}, u32[]{:S(2)}) collective-permute-start(bf16[256,128]{1,0:T(8,128)(2,1)S(1)} %get-tuple-element.98), channel_id=1, source_target_pairs={{0,16},{4,20},{8,24},{12,28},{16,0},{20,4},{24,8},{28,12},{32,48},... | collective-permute-start | bytes 196616 | tf_op jit(solution)/shard_map/ppermute | solution.py:677
  138.6 3.5 %collective-permute-done.16.refs_2_ = bf16[256,128]{1,0:T(8,128)(2,1)S(1)} collective-permute-done((bf16[256,128]{1,0:T(8,128)(2,1)S(1)}, bf16[256,128]{1,0:T(8,128)(2,1)S(1)}, u32[]{:S(2)}, u32[]{:S(2)}) %collective-permute-start.16) | collective-permute-done | bytes 65568 | tf_op jit(solution)/shard_map/ppermute | solution.py:677
  146.5 8.4 %end_back_kernel.1 = (bf16[256,2048]{1,0:T(8,128)(2,1)}, bf16[256,256]{1,0:T(8,128)(2,1)}, f32[256,32]{1,0:T(8,128)S(1)}, f32[2048,128]{1,0:T(8,128)}, f32[1,2176]{1,0:T(1,128)S(1)}) custom-call(s32[4]{0:T(128)S(1)} %pad_add_fusion.refs_0_.place_ref, bf16[256,2048]{1,0:T(8,128)(2,1)S(1)} %copy-done.5, bf16[256,256]{1,0:T(8,128)(2,1)S(1)} %copy-done.10, ...), custom_call_target="tpu_custom_call" | custom-call | flops 20000000000 | bytes 9987712 | tf_op jit(solution)/shard_map/end_back_kernel/pallas_call | solution.py:479
  156.5 3.1 %collective-permute-start.22 = (f32[1,2176]{1,0:T(1,128)S(1)}, f32[1,2176]{1,0:T(1,128)S(1)}, u32[]{:S(2)}, u32[]{:S(2)}) collective-permute-start(f32[1,2176]{1,0:T(1,128)S(1)} %add.34), channel_id=1, source_target_pairs={{0,16},{4,20},{8,24},{12,28},{16,0},{20,4},{24,8},{28,12},{32,48},... | collective-permute-start | bytes 26120 | tf_op jit(solution)/shard_map/ppermute | solution.py:677
  163.4 2.5 %collective-permute-start.25 = (f32[1,2176]{1,0:T(1,128)S(1)}, f32[1,2176]{1,0:T(1,128)S(1)}, u32[]{:S(2)}, u32[]{:S(2)}) collective-permute-start(f32[1,2176]{1,0:T(1,128)S(1)} %add_add_fusion.1), channel_id=1, source_target_pairs={{0,64},{4,68},{8,72},{12,76},{16,80},{20,84},{24,88},{28,92},{32,9... | collective-permute-start | bytes 26120 | tf_op jit(solution)/shard_map/ppermute | solution.py:677
  170.7 5.8 %reduce-scatter.2.cloned.1.call-done = bf16[128,2048]{1,0:T(8,128)(2,1)} async-done(((bf16[2048,2048]{1,0:T(8,128)(2,1)}), bf16[128,2048]{1,0:T(8,128)(2,1)}) %reduce-scatter.2.cloned.1.call-update) | async-done | bytes 524304 | tf_op jit(solution)/shard_map/reduce_scatter | solution.py:709
  (120 shorter events, 52.1 us)
Async XLA Ops:
  7.2 76.4 %all-gather.2.cloned.1.call-start = ((), (), s32[]{:S(2)}) async-start(), calls=%async_computation.1 | async-start | bytes 8912896 | tf_op jit(solution)/shard_map/all_gather | solution.py:698
  7.9 168.6 %reduce-scatter.2.cloned.1.call-start = ((), (), s32[]{:S(2)}) async-start(), calls=%async_computation.2 | async-start | bytes 8912896 | tf_op jit(solution)/shard_map/reduce_scatter | solution.py:709
  13.9 15.5 %collective-permute-start.1 = (bf16[512,512]{1,0:T(8,128)(2,1)}, bf16[512,512]{1,0:T(8,128)(2,1)}, u32[]{:S(2)}, u32[]{:S(2)}) collective-permute-start(bf16[512,512]{1,0:T(8,128)(2,1)} %constant_dynamic-update-slice_fusion.refs_10_.refs_1_), channel_id=1, source_target_pairs={{0,1},{1,2},{2,3},{3,0},{4,5},{5,6},{6,7},{7,4},{8,9},{9,10},{10,1... | collective-permute-start | bytes 1572872 | tf_op jit(solution)/shard_map/ppermute | solution.py:681
  15.5 14.0 %collective-permute-start.2 = (bf16[512,512]{1,0:T(8,128)(2,1)}, bf16[512,512]{1,0:T(8,128)(2,1)}, u32[]{:S(2)}, u32[]{:S(2)}) collective-permute-start(bf16[512,512]{1,0:T(8,128)(2,1)} %constant_dynamic-update-slice_fusion.refs_10_.refs_1_), channel_id=1, source_target_pairs={{0,3},{1,0},{2,1},{3,2},{4,7},{5,4},{6,5},{7,6},{8,11},{9,8},{10,9... | collective-permute-start | bytes 1572872 | tf_op jit(solution)/shard_map/ppermute | solution.py:681
  24.8 23.8 %collective-permute-start.5 = (bf16[256,1024]{1,0:T(8,128)(2,1)S(1)}, bf16[256,1024]{1,0:T(8,128)(2,1)S(1)}, u32[]{:S(2)}, u32[]{:S(2)}) collective-permute-start(bf16[256,1024]{1,0:T(8,128)(2,1)S(1)} %get-tuple-element.72.refs_10_.own0_ref), channel_id=1, source_target_pairs={{0,4},{4,0},{8,12},{12,8},{16,20},{20,16},{24,28},{28,24},{32,36},... | collective-permute-start | bytes 1572872 | tf_op jit(solution)/shard_map/ppermute | solution.py:677
  34.4 14.2 %collective-permute-start.6 = (bf16[256,1024]{1,0:T(8,128)(2,1)S(1)}, bf16[256,1024]{1,0:T(8,128)(2,1)S(1)}, u32[]{:S(2)}, u32[]{:S(2)}) collective-permute-start(bf16[256,1024]{1,0:T(8,128)(2,1)S(1)} %get-tuple-element.73.refs_6_.own1_ref), channel_id=1, source_target_pairs={{0,4},{4,0},{8,12},{12,8},{16,20},{20,16},{24,28},{28,24},{32,36},... | collective-permute-start | bytes 1572872 | tf_op jit(solution)/shard_map/ppermute | solution.py:677
  35.3 10.0 %collective-permute-start.3 = (bf16[256,512]{1,0:T(8,128)(2,1)S(1)}, bf16[256,512]{1,0:T(8,128)(2,1)S(1)}, u32[]{:S(2)}, u32[]{:S(2)}) collective-permute-start(bf16[256,512]{1,0:T(8,128)(2,1)S(1)} %slice.32), channel_id=1, source_target_pairs={{0,1},{1,2},{2,3},{3,0},{4,5},{5,6},{6,7},{7,4},{8,9},{9,10},{10,1... | collective-permute-start | bytes 786440 | tf_op jit(solution)/shard_map/ppermute | solution.py:681
  37.9 8.5 %collective-permute-start.4 = (bf16[256,512]{1,0:T(8,128)(2,1)S(1)}, bf16[256,512]{1,0:T(8,128)(2,1)S(1)}, u32[]{:S(2)}, u32[]{:S(2)}) collective-permute-start(bf16[256,512]{1,0:T(8,128)(2,1)S(1)} %slice.33), channel_id=1, source_target_pairs={{0,3},{1,0},{2,1},{3,2},{4,7},{5,4},{6,5},{7,6},{8,11},{9,8},{10,9... | collective-permute-start | bytes 786440 | tf_op jit(solution)/shard_map/ppermute | solution.py:681
  93.7 4.0 %collective-permute-start.8 = (bf16[256,1024]{1,0:T(8,128)(2,1)S(1)}, bf16[256,1024]{1,0:T(8,128)(2,1)S(1)}, u32[]{:S(2)}, u32[]{:S(2)}) collective-permute-start(bf16[256,1024]{1,0:T(8,128)(2,1)S(1)} %get-tuple-element.80), channel_id=1, source_target_pairs={{0,4},{4,0},{8,12},{12,8},{16,20},{20,16},{24,28},{28,24},{32,36},... | collective-permute-start | bytes 1572872 | tf_op jit(solution)/shard_map/ppermute | solution.py:677
  97.2 4.3 %collective-permute-start.7 = (bf16[256,1024]{1,0:T(8,128)(2,1)S(1)}, bf16[256,1024]{1,0:T(8,128)(2,1)S(1)}, u32[]{:S(2)}, u32[]{:S(2)}) collective-permute-start(bf16[256,1024]{1,0:T(8,128)(2,1)S(1)} %get-tuple-element.78), channel_id=1, source_target_pairs={{0,4},{4,0},{8,12},{12,8},{16,20},{20,16},{24,28},{28,24},{32,36},... | collective-permute-start | bytes 1572872 | tf_op jit(solution)/shard_map/ppermute | solution.py:677
  108.0 9.1 %collective-permute-start.10 = (bf16[272,128]{1,0:T(8,128)(2,1)S(1)}, bf16[272,128]{1,0:T(8,128)(2,1)S(1)}, u32[]{:S(2)}, u32[]{:S(2)}) collective-permute-start(bf16[272,128]{1,0:T(8,128)(2,1)S(1)} %get-tuple-element.87), channel_id=1, source_target_pairs={{0,24},{4,28},{8,0},{12,4},{16,8},{20,12},{24,16},{28,20},{32,56},... | collective-permute-start | bytes 208904 | tf_op jit(solution)/shard_map/ppermute | solution.py:677
  110.8 7.6 %collective-permute-start.11 = (bf16[272,128]{1,0:T(8,128)(2,1)S(1)}, bf16[272,128]{1,0:T(8,128)(2,1)S(1)}, u32[]{:S(2)}, u32[]{:S(2)}) collective-permute-start(bf16[272,128]{1,0:T(8,128)(2,1)S(1)} %get-tuple-element.88), channel_id=1, source_target_pairs={{0,16},{4,20},{8,24},{12,28},{16,0},{20,4},{24,8},{28,12},{32,48},... | collective-permute-start | bytes 208904 | tf_op jit(solution)/shard_map/ppermute | solution.py:677
  111.5 8.1 %collective-permute-start.12 = (bf16[272,128]{1,0:T(8,128)(2,1)S(1)}, bf16[272,128]{1,0:T(8,128)(2,1)S(1)}, u32[]{:S(2)}, u32[]{:S(2)}) collective-permute-start(bf16[272,128]{1,0:T(8,128)(2,1)S(1)} %get-tuple-element.89), channel_id=1, source_target_pairs={{0,8},{4,12},{8,16},{12,20},{16,24},{20,28},{24,0},{28,4},{32,40},... | collective-permute-start | bytes 208904 | tf_op jit(solution)/shard_map/ppermute | solution.py:677
  120.2 8.6 %collective-permute-start.13 = (bf16[272,128]{1,0:T(8,128)(2,1)S(1)}, bf16[272,128]{1,0:T(8,128)(2,1)S(1)}, u32[]{:S(2)}, u32[]{:S(2)}) collective-permute-start(bf16[272,128]{1,0:T(8,128)(2,1)S(1)} %get-tuple-element.91.refs_8_), channel_id=1, source_target_pairs={{32,0},{36,4},{40,8},{44,12},{48,16},{52,20},{56,24},{60,28},{64,3... | collective-permute-start | bytes 208904 | tf_op jit(solution)/shard_map/ppermute | solution.py:677
  121.5 9.3 %collective-permute-start.14 = (bf16[272,128]{1,0:T(8,128)(2,1)S(1)}, bf16[272,128]{1,0:T(8,128)(2,1)S(1)}, u32[]{:S(2)}, u32[]{:S(2)}) collective-permute-start(bf16[272,128]{1,0:T(8,128)(2,1)S(1)} %get-tuple-element.91.refs_8_), channel_id=1, source_target_pairs={{64,0},{68,4},{72,8},{76,12},{80,16},{84,20},{88,24},{92,28},{96,3... | collective-permute-start | bytes 208904 | tf_op jit(solution)/shard_map/ppermute | solution.py:677
  122.8 11.3 %collective-permute-start.15 = (bf16[272,128]{1,0:T(8,128)(2,1)S(1)}, bf16[272,128]{1,0:T(8,128)(2,1)S(1)}, u32[]{:S(2)}, u32[]{:S(2)}) collective-permute-start(bf16[272,128]{1,0:T(8,128)(2,1)S(1)} %get-tuple-element.91.refs_8_), channel_id=1, source_target_pairs={{96,0},{100,4},{104,8},{108,12},{112,16},{116,20},{120,24},{124,28... | collective-permute-start | bytes 208904 | tf_op jit(solution)/shard_map/ppermute | solution.py:677
  134.8 7.3 %collective-permute-start.16 = (bf16[256,128]{1,0:T(8,128)(2,1)S(1)}, bf16[256,128]{1,0:T(8,128)(2,1)S(1)}, u32[]{:S(2)}, u32[]{:S(2)}) collective-permute-start(bf16[256,128]{1,0:T(8,128)(2,1)S(1)} %get-tuple-element.97), channel_id=1, source_target_pairs={{0,8},{4,12},{8,16},{12,20},{16,24},{20,28},{24,0},{28,4},{32,40},... | collective-permute-start | bytes 196616 | tf_op jit(solution)/shard_map/ppermute | solution.py:677
  135.0 9.1 %collective-permute-start.17 = (bf16[256,128]{1,0:T(8,128)(2,1)S(1)}, bf16[256,128]{1,0:T(8,128)(2,1)S(1)}, u32[]{:S(2)}, u32[]{:S(2)}) collective-permute-start(bf16[256,128]{1,0:T(8,128)(2,1)S(1)} %get-tuple-element.98), channel_id=1, source_target_pairs={{0,16},{4,20},{8,24},{12,28},{16,0},{20,4},{24,8},{28,12},{32,48},... | collective-permute-start | bytes 196616 | tf_op jit(solution)/shard_map/ppermute | solution.py:677
  138.2 5.8 %collective-permute-start.18 = (bf16[256,128]{1,0:T(8,128)(2,1)S(1)}, bf16[256,128]{1,0:T(8,128)(2,1)S(1)}, u32[]{:S(2)}, u32[]{:S(2)}) collective-permute-start(bf16[256,128]{1,0:T(8,128)(2,1)S(1)} %get-tuple-element.99), channel_id=1, source_target_pairs={{0,24},{4,28},{8,0},{12,4},{16,8},{20,12},{24,16},{28,20},{32,56},... | collective-permute-start | bytes 196616 | tf_op jit(solution)/shard_map/ppermute | solution.py:677
  156.1 5.6 %collective-permute-start.21 = (f32[1,2176]{1,0:T(1,128)S(1)}, f32[1,2176]{1,0:T(1,128)S(1)}, u32[]{:S(2)}, u32[]{:S(2)}) collective-permute-start(f32[1,2176]{1,0:T(1,128)S(1)} %add.34), channel_id=1, source_target_pairs={{0,8},{4,12},{8,16},{12,20},{16,24},{20,28},{24,0},{28,4},{32,40},... | collective-permute-start | bytes 26120 | tf_op jit(solution)/shard_map/ppermute | solution.py:677
  156.5 5.2 %collective-permute-start.22 = (f32[1,2176]{1,0:T(1,128)S(1)}, f32[1,2176]{1,0:T(1,128)S(1)}, u32[]{:S(2)}, u32[]{:S(2)}) collective-permute-start(f32[1,2176]{1,0:T(1,128)S(1)} %add.34), channel_id=1, source_target_pairs={{0,16},{4,20},{8,24},{12,28},{16,0},{20,4},{24,8},{28,12},{32,48},... | collective-permute-start | bytes 26120 | tf_op jit(solution)/shard_map/ppermute | solution.py:677
  163.3 5.0 %collective-permute-start.24 = (f32[1,2176]{1,0:T(1,128)S(1)}, f32[1,2176]{1,0:T(1,128)S(1)}, u32[]{:S(2)}, u32[]{:S(2)}) collective-permute-start(f32[1,2176]{1,0:T(1,128)S(1)} %add_add_fusion.1), channel_id=1, source_target_pairs={{0,32},{4,36},{8,40},{12,44},{16,48},{20,52},{24,56},{28,60},{32,6... | collective-permute-start | bytes 26120 | tf_op jit(solution)/shard_map/ppermute | solution.py:677
  163.4 5.3 %collective-permute-start.25 = (f32[1,2176]{1,0:T(1,128)S(1)}, f32[1,2176]{1,0:T(1,128)S(1)}, u32[]{:S(2)}, u32[]{:S(2)}) collective-permute-start(f32[1,2176]{1,0:T(1,128)S(1)} %add_add_fusion.1), channel_id=1, source_target_pairs={{0,64},{4,68},{8,72},{12,76},{16,80},{20,84},{24,88},{28,92},{32,9... | collective-permute-start | bytes 26120 | tf_op jit(solution)/shard_map/ppermute | solution.py:677
  165.8 3.7 %collective-permute-start.26 = (f32[1,2176]{1,0:T(1,128)S(1)}, f32[1,2176]{1,0:T(1,128)S(1)}, u32[]{:S(2)}, u32[]{:S(2)}) collective-permute-start(f32[1,2176]{1,0:T(1,128)S(1)} %add_add_fusion.1), channel_id=1, source_target_pairs={{0,96},{4,100},{8,104},{12,108},{16,112},{20,116},{24,120},{28,124... | collective-permute-start | bytes 26120 | tf_op jit(solution)/shard_map/ppermute | solution.py:677
  (31 other events, 167.9 us)
Sparse Core Ops, SparseCore 0:
  10.2 73.4 all-gather.1
  87.6 88.8 reduce-scatter.1

commit v2 on v1

--- a/solution.py
+++ b/solution.py
@@ -21,8 +21,8 @@
 GROUP_PAIRS = PER_GROUP // 2
 STATE_ROWS = PER_GROUP * P_SIZE
 EPSILON = 1e-05
-UNROLL = 2
-SHORT, LONG = 100000000, 20000000000
+UNROLL = 4
+SHORT, LONG = 100000000, 28000000000
 
 f32 = jnp.float32
 bf16 = jnp.bfloat16
@@ -113,10 +113,11 @@
 
 
 def forward_kernel(
-    group, x_ref, z_ref, b_ref, c_ref, dt_ref, run_ref, run_col_ref, state_ref, gain_ref, skip_ref,
+    x_ref, z_ref, b_ref, c_ref, dt_ref, run_ref, run_col_ref, state_ref, gain_ref, skip_ref,
     y_ref, normed_ref,
     scores, gated_ref, power,
 ):
+    group = pl.program_id(0)
     lower = iota((Q, Q), 0) >= iota((Q, Q), 1)
     reads = c_ref[...]
     scores[...] = dot_rows(reads, b_ref[...])
@@ -140,7 +141,7 @@
         x0, x1 = halves(xs)
         y0 = dot(jnp.concatenate(top, axis=1), jnp.concatenate([x0[:Q], x1[:Q]], axis=0))
         y1 = dot(jnp.concatenate(bottom, axis=1), jnp.concatenate([x0, x1], axis=0))
-        from_start = dot_rows(reads, state_ref[lanes_of(pair), :].astype(bf16))
+        from_start = dot_rows(reads, state_ref[lanes_of(at), :].astype(bf16))
         first = iota((TOKENS, 128), 1) < P_SIZE
         reach = jnp.exp(jnp.where(first, expanded[:, :128], expanded[:, 128:]))
         y = jnp.concatenate([y0, y1], axis=0) + reach * from_start
@@ -501,14 +502,32 @@
     )
 
 
-def forward(group, x, z, b, c, steps, run, run_col, state, gain, skip, after):
-    return call(
-        functools.partial(forward_kernel, group),
-        [(WIDE, f32), (WIDE, bf16)],
-        [((TOKENS, TOKENS), f32), (WIDE, f32), ((TOKENS, 128), f32)],
-        0, (x, group), (z, group), (b, group), (c, group), steps, run, run_col,
-        state, (gain, group), (skip, group), flops=SHORT, after=after,
-    )
+def forward(x, z, b, c, steps, run, run_col, state, gain, skip, after):
+    def columns(array):
+        return pl.BlockSpec((array.shape[0], array.shape[1] // GROUPS), lambda g: (0, g))
+
+    def fixed(array):
+        return pl.BlockSpec(array.shape, lambda g: (0, 0))
+
+    def body(*refs):
+        forward_kernel(*refs[:10], *refs[10 + len(after) :])
+
+    wide = (TOKENS, CHANNELS)
+    return pl.pallas_call(
+        body,
+        name="forward",
+        grid=(GROUPS,),
+        out_shape=[jax.ShapeDtypeStruct(wide, f32), jax.ShapeDtypeStruct(wide, bf16)],
+        in_specs=[columns(x), columns(z), columns(b), columns(c), fixed(steps), fixed(run),
+                  fixed(run_col), pl.BlockSpec((STATE_ROWS, N), lambda g: (g, 0)), columns(gain),
+                  columns(skip)]
+        + [pl.BlockSpec(memory_space=pl.ANY)] * len(after),
+        out_specs=[pl.BlockSpec(WIDE, lambda g: (0, g))] * 2,
+        scratch_shapes=[pltpu.VMEM((TOKENS, TOKENS), f32), pltpu.VMEM(WIDE, f32),
+                        pltpu.VMEM((TOKENS, 128), f32)],
+        compiler_params=pltpu.CompilerParams(vmem_limit_bytes=56 * 2**20),
+        cost_estimate=pl.CostEstimate(flops=SHORT, bytes_accessed=1024, transcendentals=0),
+    )(x, z, b, c, steps, run, run_col, state, gain, skip, *after)
 
 
 MESSAGE = ((STATE_ROWS + 2 * PER_GROUP, N), bf16)
@@ -520,7 +539,7 @@
         functools.partial(norm_back_kernel, group),
         outs + ([MESSAGE] if group else []),
         [((TOKENS, 128), f32), ((TOKENS, 128), f32)],
-        1, place, own, other, y, (z, group), (c, group), (gain, group), run, run_col, *first,
+        1, place, own, other, (y, group), (z, group), (c, group), (gain, group), run, run_col, *first,
         flops=LONG, after=after,
     )
 
@@ -582,52 +601,85 @@
 TILE = 512
 
 
-def turn_kernel(place_ref, own_ref, before_ref, after_ref, far0_ref, far1_ref, pieces_ref, turned_ref):
-    far = jnp.concatenate([far0_ref[...], far1_ref[...]], axis=0)
-    for by, piece in ((0, own_ref[...]), (-1, before_ref[...]), (1, after_ref[...]), (2, far)):
-        at = (place_ref[0] + by) & 3
-        rows = pl.ds(pl.multiple_of(at * 512, 512), 512)
-        pieces_ref[rows, :] = piece
-        turned_ref[rows, :] = piece.T
-
-
-def turn(place, *pieces, after):
-    return call(
-        turn_kernel, [((2048, 512), bf16)] * 2, [], 1, place, *pieces, flops=SHORT, after=after
-    )
-
-
-def weight_grad_kernel(turned_ref, own0_ref, other0_ref, own1_ref, other1_ref, out_ref):
-    first = pl.program_id(0) < HALF // TILE
-    own = jnp.where(first, own0_ref[...], own1_ref[...])
-    other = jnp.where(first, other0_ref[...], other1_ref[...])
-    right = jnp.concatenate([own, other], axis=0)
+def weight_grad_kernel(pieces_ref, own_ref, other_ref, *refs):
+    out_ref, turned = refs[-2:]
+
+    @pl.when(pl.program_id(0) == 0)
+    def _():
+        for at in range(0, 2048, 512):
+            turned[at : at + 512, :] = pieces_ref[at : at + 512, :].T
+
+    right = jnp.concatenate([own_ref[...], other_ref[...]], axis=0)
     for at in range(0, 2048, 512):
-        out_ref[at : at + 512, :] = dot(turned_ref[at : at + 512, :], right).astype(bf16)
-
-
-def weight_grad(turned, *normed):
-    last = HALF // TILE - 1
-    early = pl.BlockSpec((TOKENS, TILE), lambda i: (0, jnp.minimum(i, last)))
-    late = pl.BlockSpec((TOKENS, TILE), lambda i: (0, jnp.maximum(i - last - 1, 0)))
+        out_ref[at : at + 512, :] = dot(turned[at : at + 512, :], right).astype(bf16)
+
+
+def weight_grad(pieces, own, other, after):
     return pl.pallas_call(
         weight_grad_kernel,
         name="weight_grad",
         grid=(CHANNELS // TILE,),
         out_shape=jax.ShapeDtypeStruct((2048, CHANNELS), bf16),
-        in_specs=[pl.BlockSpec((2048, 512), lambda i: (0, 0)), early, early, late, late],
+        in_specs=[pl.BlockSpec((2048, 512), lambda i: (0, 0))]
+        + [pl.BlockSpec((TOKENS, TILE), lambda i: (0, i))] * 2
+        + [pl.BlockSpec(memory_space=pl.ANY)] * len(after),
         out_specs=pl.BlockSpec((2048, TILE), lambda i: (0, i)),
-        compiler_params=pltpu.CompilerParams(vmem_limit_bytes=24 * 2**20),
+        scratch_shapes=[pltpu.VMEM((2048, 512), bf16)],
+        compiler_params=pltpu.CompilerParams(vmem_limit_bytes=48 * 2**20),
         cost_estimate=pl.CostEstimate(flops=SHORT, bytes_accessed=1024, transcendentals=0),
-    )(turned, *normed)
-
-
-def upstream_whole_kernel(half, place_ref, pieces_ref, weight_ref, *refs):
+    )(pieces, own, other, *after)
+
+
+NEAR = (0, -1, 1, 2)
+
+
+def join_kernel(*refs):
+    for half in range(2):
+        for at in range(4):
+            refs[8 + half][128 * at : 128 * (at + 1), :] = refs[4 * half + at][...]
+
+
+def join(first, second, after):
+    return call(
+        join_kernel, [((512, HALF), bf16)] * 2, [], 0, *first, *second, flops=SHORT, limit=16,
+        after=after,
+    )
+
+
+def halve_kernel(up_ref, down_ref, low_ref, high_ref):
+    low_ref[...] = up_ref[:256, :]
+    high_ref[...] = down_ref[256:, :]
+
+
+def halve(up, down, after):
+    return call(
+        halve_kernel, [((256, HALF), bf16)] * 2, [], 0, up, down, flops=SHORT, limit=8, after=after
+    )
+
+
+def left_rows(place_ref, pieces_ref, half, firsts, second):
+    left = []
+    for first in firsts:
+        by_y, by_z = (first, second) if half else (second, first)
+        at_y, at_z = (place_ref[1] + by_y) & 3, (place_ref[2] + by_z) & 3
+        rows = pl.ds(pl.multiple_of(at_y * 512, 512), 512)
+        left.append(pieces_ref[rows, pl.ds(pl.multiple_of(at_z * 128, 128), 128)])
+    return jnp.concatenate(left, axis=1)
+
+
+def upstream_near_kernel(half, place_ref, pieces_ref, own_ref, up_ref, down_ref, *refs):
+    total = None
+    for second, ref in ((0, own_ref), (-1, up_ref), (1, down_ref)):
+        product = dot(left_rows(place_ref, pieces_ref, half, NEAR, second), ref[...])
+        total = product if total is None else total + product
+    refs[-1][...] = total
+
+
+def upstream_far_kernel(half, place_ref, pieces_ref, near_ref, low_ref, high_ref, *refs):
     own_ref, other_ref = refs[-2:]
-    total = None
-    for at in range(0, 2048, 512):
-        product = dot(pieces_ref[at : at + 512, :], weight_ref[at : at + 512, :])
-        total = product if total is None else total + product
+    total = near_ref[...]
+    total = total + dot(left_rows(place_ref, pieces_ref, half, NEAR[:2], 2), low_ref[...])
+    total = total + dot(left_rows(place_ref, pieces_ref, half, NEAR[2:], 2), high_ref[...])
     own_ref[...] = total[:TOKENS]
     other_ref[...] = total[TOKENS:].astype(bf16)
 
@@ -639,17 +691,23 @@
         grid=(HALF // TILE,),
         out_shape=[jax.ShapeDtypeStruct((rows, HALF), kind) for rows, kind in outs],
         in_specs=[pl.BlockSpec(memory_space=pltpu.SMEM), pl.BlockSpec((2048, 512), lambda i: (0, 0))]
-        + [pl.BlockSpec((a.shape[0], TILE), lambda i: (0, half * (HALF // TILE) + i)) for a in arrays]
+        + [pl.BlockSpec((a.shape[0], TILE), lambda i: (0, i)) for a in arrays]
         + [pl.BlockSpec(memory_space=pl.ANY)] * len(after),
         out_specs=[pl.BlockSpec((rows, TILE), lambda i: (0, i)) for rows, _ in outs],
         compiler_params=pltpu.CompilerParams(vmem_limit_bytes=24 * 2**20),
-        cost_estimate=pl.CostEstimate(flops=SHORT, bytes_accessed=1024, transcendentals=0),
+        cost_estimate=pl.CostEstimate(
+            flops=SHORT, bytes_accessed=1024, transcendentals=0),
     )(place, pieces, *arrays, *after)
 
 
-def upstream_whole(half, place, pieces, weights, after):
+def upstream_near(half, place, pieces, own, up, down, after):
+    outs = [(2 * TOKENS, f32)]
+    return upstream(upstream_near_kernel, half, place, pieces, (own, up, down), outs, after)[0]
+
+
+def upstream_far(half, place, pieces, near, low, high, after):
     outs = [(TOKENS, f32), (TOKENS, bf16)]
-    return upstream(upstream_whole_kernel, half, place, pieces, (weights,), outs, after)
+    return upstream(upstream_far_kernel, half, place, pieces, (near, low, high), outs, after)
 
 
 def device(y, z, core):
@@ -677,8 +735,10 @@
     return lax.ppermute(array, "ctx", pairs)
 
 
-def along_x(array, by):
-    return lax.ppermute(array, "head", [(x, (x + by) % 4) for x in range(4)])
+RINGS = (
+    (along_z(1), along_z(-1), along_z(2), along_y(1), along_y(-1)),
+    (along_y(1), along_y(-1), along_y(2), along_z(1), along_z(-1)),
+)
 
 
 def sum_ctx(array):
@@ -695,28 +755,33 @@
     skips = jnp.repeat(skip, P_SIZE).reshape(1, CHANNELS)
     gains = gain.reshape(1, CHANNELS)
     state = start_state.reshape(CHANNELS, N)
-    weights = lax.all_gather(out_weight, "ctx", axis=0, tiled=True, axis_index_groups=SAME_CORE)
+    cut = [out_weight[:, :HALF], out_weight[:, HALF:]]
+    ringed = [[cut[h]] + [move(cut[h], RINGS[h][k]) for k in range(3)] for h in range(2)]
     keep, send, run, run_col, dt_col = prepare(place, dout, steps, rates)
     both = jnp.concatenate([keep, move(send, SWAP)], axis=0)
-    x_before, x_after = along_x(both, 1), along_x(both, -1)
+    pieces = lax.all_gather(both, "head", axis=0, tiled=True)
     scan_in = (x_in, z_in, b_in, c_in, steps, run, run_col, state, gains, skips)
-    y0, normed0 = forward(0, *scan_in, (both,))
-    y1, normed1 = forward(1, *scan_in, (normed0, x_before, x_after))
-    x_far = along_x(x_before[:TOKENS], 1), along_x(x_after[TOKENS:], -1)
-    other0, other1 = move(normed0, SWAP), move(normed1, SWAP)
-    pieces, turned = turn(place, both, x_before, x_after, *x_far, after=(normed1,))
-    term = weight_grad(turned, normed0, other0, normed1, other1)
+    four = join(*ringed, (run,))
+    up = [move(four[h], RINGS[h][3]) for h in range(2)]
+    down = [move(four[h], RINGS[h][4]) for h in range(2)]
+    y, normed = forward(*scan_in, (both,))
+    term = weight_grad(pieces, normed, move(normed, SWAP), ())
     grad_w = lax.psum_scatter(
         term, "ctx", scatter_dimension=0, tiled=True, axis_index_groups=SAME_CORE
     )
-    part0, send0 = upstream_whole(0, place, pieces, weights, (term,))
-    part1, send1 = upstream_whole(1, place, pieces, weights, (part0,))
+    ends = [halve(up[h], down[h], (term,)) for h in range(2)]
+    low = [move(ends[h][0], RINGS[h][3]) for h in range(2)]
+    high = [move(ends[h][1], RINGS[h][4]) for h in range(2)]
+    near0 = upstream_near(0, place, pieces, four[0], up[0], down[0], (ends[1][0],))
+    near1 = upstream_near(1, place, pieces, four[1], up[1], down[1], (near0,))
+    part0, send0 = upstream_far(0, place, pieces, near0, low[0], high[0], (near1,))
+    part1, send1 = upstream_far(1, place, pieces, near1, low[1], high[1], (part0,))
     back_in = (z_in, c_in, gains, run, run_col)
     grad_y0, grad_z0, gain_sum0, start0, message0 = norm_back(
-        0, place, part0, move(send0, SWAP), y0, *back_in, (), (part1,)
+        0, place, part0, move(send0, SWAP), y, *back_in, (), (part1,)
     )
     grad_y1, grad_z1, gain_sum1, start1, keep, send = norm_back(
-        1, place, part1, move(send1, SWAP), y1, *back_in, (message0,), (grad_y0,)
+        1, place, part1, move(send1, SWAP), y, *back_in, (message0,), (grad_y0,)
     )
     *quarters, last = chip_state(place, keep, move(send, SWAP))
     from_z = [move(quarters[-k], along_z(-k)) for k in (1, 2, 3)]

time: 184 us -> 182 us (0.989)
  starting transfers between devices: 27.8 us -> 42.5 us
  waiting for transfers between devices: 64.8 us -> 50.7 us
  local copies, waits for them, and re-layouts: 24 us -> 15.5 us
  Pallas kernels: 50.5 us -> 55.9 us
    ppermute x23 -> x36, waiting for transfers between devices: 21.2 us -> 47.2 us  [move(): return lax.ppermute(array, 'ctx', pairs)]
    all_gather x1, waiting for transfers between devices: 25.8 us -> 3.49 us  [per_device(): pieces = lax.all_gather(both, 'head', axis=0, tiled=True)]
    ppermute x23 -> x36, starting transfers between devices: 21.1 us -> 42.4 us  [move(): return lax.ppermute(array, 'ctx', pairs)]
    ppermute x4 -> x0, waiting for transfers between devices: 11.3 us -> none  [along_x(): return lax.ppermute(array, 'head', [(x, (x + by) % 4) for x in range(4)])]
    pallas_call x0 -> x1, Pallas kernels: none -> 8.44 us  [forward(): pl.pallas_call(body, name='forward', grid=(GROUPS,), out_shape=[jax.Shape...]
    pallas_call x13, Pallas kernels: 37.9 us -> 30.3 us  [call(): pl.pallas_call(body, grid=(1,), out_shape=[jax.ShapeDtypeStruct(shape, ki...]
    ppermute x4 -> x0, starting transfers between devices: 6.62 us -> none  [along_x(): return lax.ppermute(array, 'head', [(x, (x + by) % 4) for x in range(4)])]
    reduce_scatter x1, waiting for transfers between devices: 5.82 us -> 0.01 us  [per_device(): lax.psum_scatter(term, 'ctx', scatter_dimension=0, tiled=True, axis_index...]
  transfers between devices with their start and end apart: 29 -> 38, of which waited for: 20 -> 21; matrix products, arithmetic and copies ran while one was open for 5% -> 2% of each run, Pallas kernels for 28% -> 30%
where the time goes in v2:
time: 182 us; the launch traced here: 181 us
  Pallas kernels  55.9 us (31%)
  waiting for transfers between devices  50.7 us (28%)
  starting transfers between devices  42.5 us (23%)
  local copies, waits for them, and re-layouts  15.5 us (9%)
  between operations  14.5 us (8%)
  other arithmetic  1.84 us (1%)
    ppermute x36, waiting for transfers between devices, move(): return lax.ppermute(array, 'ctx', pairs)  47.2 us
    ppermute x36, starting transfers between devices, move(): return lax.ppermute(array, 'ctx', pairs)  42.4 us
    pallas_call x13, Pallas kernels, call(): pl.pallas_call(body, grid=(1,), out_shape=[jax.ShapeDtypeStruct(shape, ki...  30.3 us
    unnamed x50, local copies, waits for them, and re-layouts  12.8 us
    pallas_call x4, Pallas kernels, upstream(): pl.pallas_call(functools.partial(kernel, half), name=f'{kernel.__name__}_...  9.9 us
    pallas_call x1, Pallas kernels, forward(): pl.pallas_call(body, name='forward', grid=(GROUPS,), out_shape=[jax.Shape...  8.44 us
    pallas_call x1, Pallas kernels, weight_grad(): pl.pallas_call(weight_grad_kernel, name='weight_grad', grid=(CHANNELS //...  7.32 us
  transfers between devices with their start and end apart: 38, of which 21 were waited for; matrix products, arithmetic and copies ran while one was open for 2% of the time, Pallas kernels for 30%

profile of v2, /device:TPU:0, one launch (start us, length us, event | category | flops | bytes accessed | tf_op | source)
XLA Modules:
  0.0 181.0 jit_solution(10410768351534124137)
XLA Ops:
  13.4 3.4 %collective-permute-start.6 = (bf16[128,1024]{1,0:T(8,128)(2,1)S(1)}, bf16[128,1024]{1,0:T(8,128)(2,1)S(1)}, u32[]{:S(2)}, u32[]{:S(2)}) collective-permute-start(bf16[128,1024]{1,0:T(8,128)(2,1)S(1)} %get-tuple-element.138.refs_4_), channel_id=1, source_target_pairs={{0,64},{4,68},{8,72},{12,76},{16,80},{20,84},{24,88},{28,92},{32,9... | collective-permute-start | bytes 786440 | tf_op jit(solution)/shard_map/ppermute | solution.py:735
  18.8 3.9 %collective-permute-start.3 = (bf16[128,1024]{1,0:T(8,128)(2,1)S(1)}, bf16[128,1024]{1,0:T(8,128)(2,1)S(1)}, u32[]{:S(2)}, u32[]{:S(2)}) collective-permute-start(bf16[128,1024]{1,0:T(8,128)(2,1)S(1)} %get-tuple-element.139.refs_0_), channel_id=1, source_target_pairs={{0,16},{4,20},{8,24},{12,28},{16,0},{20,4},{24,8},{28,12},{32,48},... | collective-permute-start | bytes 786440 | tf_op jit(solution)/shard_map/ppermute | solution.py:735
  26.9 8.4 %forward.1 = (f32[256,2048]{1,0:T(8,128)}, bf16[256,2048]{1,0:T(8,128)(2,1)}) custom-call(bf16[256,2048]{1,0:T(8,128)(2,1)} %refs_1_.9, bf16[256,2048]{1,0:T(8,128)(2,1)} %refs_4_.3, bf16[256,256]{1,0:T(8,128)(2,1)} %refs_2_.7, bf16[256,256]{1,0:T(8,128)(2,1)} %refs_2_.6, f32[32,256]{1,0:T(8,128)} %bitcast.18, f32[32,256]{1,0:T(8,128)} %copy-done.10, ...), custom_call_target="tpu_custom_call" | custom-call | flops 100000000 | bytes 1024 | tf_op jit(solution)/shard_map/forward/pallas_call | solution.py:516
  36.9 3.1 %collective-permute-start.10 = (bf16[512,1024]{1,0:T(8,128)(2,1)}, bf16[512,1024]{1,0:T(8,128)(2,1)S(1)}, u32[]{:S(2)}, u32[]{:S(2)}) collective-permute-start(bf16[512,1024]{1,0:T(8,128)(2,1)} %get-tuple-element.75.own_ref), channel_id=1, source_target_pairs={{0,96},{4,100},{8,104},{12,108},{16,112},{20,116},{24,120},{28,124... | collective-permute-start | bytes 3145736 | tf_op jit(solution)/shard_map/ppermute | solution.py:735
  43.2 3.5 %all-gather.2.cloned.1.call-done.pieces_ref = bf16[2048,512]{1,0:T(8,128)(2,1)} async-done(((bf16[512,512]{1,0:T(8,128)(2,1)}), bf16[2048,512]{1,0:T(8,128)(2,1)}) %all-gather.2.cloned.1.call-update) | async-done | bytes 2097168 | tf_op jit(solution)/shard_map/all_gather | solution.py:762
  50.7 7.3 %weight_grad.1.refs_2_ = bf16[2048,2048]{1,0:T(8,128)(2,1)} custom-call(bf16[2048,512]{1,0:T(8,128)(2,1)S(1)} %copy-done.1, bf16[256,2048]{1,0:T(8,128)(2,1)S(1)} %copy-done.3, bf16[256,2048]{1,0:T(8,128)(2,1)S(1)} %copy-done.5), custom_call_target="tpu_custom_call" | custom-call | flops 100000000 | bytes 1024 | tf_op jit(solution)/shard_map/weight_grad/pallas_call | solution.py:618
  58.1 5.3 %collective-permute-done.10.down_ref.refs_1_ = bf16[512,1024]{1,0:T(8,128)(2,1)S(1)} collective-permute-done((bf16[512,1024]{1,0:T(8,128)(2,1)}, bf16[512,1024]{1,0:T(8,128)(2,1)S(1)}, u32[]{:S(2)}, u32[]{:S(2)}) %collective-permute-start.10) | collective-permute-done | bytes 1048608 | tf_op jit(solution)/shard_map/ppermute | solution.py:735
  63.4 3.3 %collective-permute-done.9.up_ref.refs_0_ = bf16[512,1024]{1,0:T(8,128)(2,1)S(1)} collective-permute-done((bf16[512,1024]{1,0:T(8,128)(2,1)}, bf16[512,1024]{1,0:T(8,128)(2,1)S(1)}, u32[]{:S(2)}, u32[]{:S(2)}) %collective-permute-start.9) | collective-permute-done | bytes 1048608 | tf_op jit(solution)/shard_map/ppermute | solution.py:735
  66.7 3.8 %copy-done = bf16[2048,2048]{1,0:T(8,128)(2,1)S(1)} copy-done((bf16[2048,2048]{1,0:T(8,128)(2,1)S(1)}, bf16[2048,2048]{1,0:T(8,128)(2,1)}, u32[]{:S(2)}) %copy-start) | copy-done | bytes 8388632
  70.6 3.2 %collective-permute-start.15 = (bf16[256,1024]{1,0:T(8,128)(2,1)S(1)}, bf16[256,1024]{1,0:T(8,128)(2,1)S(1)}, u32[]{:S(2)}, u32[]{:S(2)}) collective-permute-start(bf16[256,1024]{1,0:T(8,128)(2,1)S(1)} %get-tuple-element.80), channel_id=1, source_target_pairs={{0,96},{4,100},{8,104},{12,108},{16,112},{20,116},{24,120},{28,124... | collective-permute-start | bytes 1572872 | tf_op jit(solution)/shard_map/ppermute | solution.py:735
  77.5 3.2 %upstream_near_kernel_0.1.refs_0_.near_ref = f32[512,1024]{1,0:T(8,128)S(1)} custom-call(s32[4]{0:T(128)S(1)} %pad_add_fusion.refs_0_.place_ref, bf16[2048,512]{1,0:T(8,128)(2,1)S(1)} %copy-done.2, bf16[512,1024]{1,0:T(8,128)(2,1)} %get-tuple-element.75.own_ref, bf16[512,1024]{1,0:T(8,128)(2,1)S(1)} %collective-permute-done.9.up_ref.refs_0_, ...), custom_call_target="tpu_custom_call" | custom-call | flops 100000000 | bytes 1024 | tf_op jit(solution)/shard_map/upstream_near_kernel_0/pallas_call | solution.py:688
  80.6 3.4 %upstream_near_kernel_1.1.refs_0_.near_ref = f32[512,1024]{1,0:T(8,128)S(1)} custom-call(s32[4]{0:T(128)S(1)} %pad_add_fusion.refs_0_.place_ref, bf16[2048,512]{1,0:T(8,128)(2,1)S(1)} %copy-done.2, bf16[512,1024]{1,0:T(8,128)(2,1)} %get-tuple-element.74.own_ref, bf16[512,1024]{1,0:T(8,128)(2,1)} %collective-permute-done.7.refs_0_.up_ref, ...), custom_call_target="tpu_custom_call" | custom-call | flops 100000000 | bytes 1024 | tf_op jit(solution)/shard_map/upstream_near_kernel_1/pallas_call | solution.py:688
  84.0 12.0 %collective-permute-done.14.low_ref = bf16[256,1024]{1,0:T(8,128)(2,1)S(1)} collective-permute-done((bf16[256,1024]{1,0:T(8,128)(2,1)S(1)}, bf16[256,1024]{1,0:T(8,128)(2,1)S(1)}, u32[]{:S(2)}, u32[]{:S(2)}) %collective-permute-start.14) | collective-permute-done | bytes 524320 | tf_op jit(solution)/shard_map/ppermute | solution.py:735
  98.9 3.7 %collective-permute-done.12.low_ref = bf16[256,1024]{1,0:T(8,128)(2,1)S(1)} collective-permute-done((bf16[256,1024]{1,0:T(8,128)(2,1)S(1)}, bf16[256,1024]{1,0:T(8,128)(2,1)S(1)}, u32[]{:S(2)}, u32[]{:S(2)}) %collective-permute-start.12) | collective-permute-done | bytes 524320 | tf_op jit(solution)/shard_map/ppermute | solution.py:735
  104.8 3.3 %norm_back_kernel.2 = (bf16[256,1024]{1,0:T(8,128)(2,1)S(1)}, bf16[256,1024]{1,0:T(8,128)(2,1)S(1)}, f32[1,1024]{1,0:T(1,128)S(1)}, f32[1024,128]{1,0:T(8,128)S(1)}, bf16[1056,128]{1,0:T(8,128)(2,1)S(1)}) custom-call(s32[4]{0:T(128)S(1)} %pad_add_fusion.refs_0_.place_ref, f32[256,1024]{1,0:T(8,128)S(1)} %get-tuple-element.81.refs_0_.refs_1_, ...), custom_call_target="tpu_custom_call" | custom-call | flops 28000000000 | bytes 5160960 | tf_op jit(solution)/shard_map/norm_back_kernel/pallas_call | solution.py:480
  108.1 3.4 %norm_back_kernel.3 = (bf16[256,1024]{1,0:T(8,128)(2,1)S(1)}, bf16[256,1024]{1,0:T(8,128)(2,1)S(1)}, f32[1,1024]{1,0:T(1,128)S(1)}, f32[1024,128]{1,0:T(8,128)S(...) custom-call(s32[4]{0:T(128)S(1)} %pad_add_fusion.refs_0_.place_ref, ...), custom_call_target="tpu_custom_call" | custom-call | flops 28000000000 | bytes 5701632 | tf_op jit(solution)/shard_map/norm_back_kernel/pallas_call | solution.py:480
  116.1 4.5 %scan_back_kernel.2 = (f32[256,1024]{1,0:T(8,128)S(1)}, bf16[256,128]{1,0:T(8,128)(2,1)S(1)}, f32[256,128]{1,0:T(8,128)S(1)}, f32[2,16,128]{2,1,0:T(8,128)S(1)},...) custom-call(bf16[256,2048]{1,0:T(8,128)(2,1)S(1)} %copy-done.7, bf16[256,256]{1,0:T(8,128)(2,1)S(1)} %copy-done.15, ...), custom_call_target="tpu_custom_call" | custom-call | flops 28000000000 | bytes 3785216 | tf_op jit(solution)/shard_map/scan_back_kernel/pallas_call | solution.py:480
  128.2 4.5 %scan_back_kernel.3 = (f32[256,1024]{1,0:T(8,128)S(1)}, bf16[256,128]{1,0:T(8,128)(2,1)S(1)}, f32[256,128]{1,0:T(8,128)S(1)}, f32[2,16,128]{2,1,0:T(8,128)S(1)},...) custom-call(bf16[256,2048]{1,0:T(8,128)(2,1)S(1)} %copy-done.7, bf16[256,256]{1,0:T(8,128)(2,1)S(1)} %copy-done.15, ...), custom_call_target="tpu_custom_call" | custom-call | flops 28000000000 | bytes 3785216 | tf_op jit(solution)/shard_map/scan_back_kernel/pallas_call | solution.py:480
  134.1 3.4 %collective-permute-start.26 = (bf16[256,128]{1,0:T(8,128)(2,1)S(1)}, bf16[256,128]{1,0:T(8,128)(2,1)S(1)}, u32[]{:S(2)}, u32[]{:S(2)}) collective-permute-start(bf16[256,128]{1,0:T(8,128)(2,1)S(1)} %get-tuple-element.102), channel_id=1, source_target_pairs={{0,16},{4,20},{8,24},{12,28},{16,0},{20,4},{24,8},{28,12},{32,48},... | collective-permute-start | bytes 196616 | tf_op jit(solution)/shard_map/ppermute | solution.py:735
  137.8 2.5 %collective-permute-done.25.refs_2_ = bf16[256,128]{1,0:T(8,128)(2,1)S(1)} collective-permute-done((bf16[256,128]{1,0:T(8,128)(2,1)S(1)}, bf16[256,128]{1,0:T(8,128)(2,1)S(1)}, u32[]{:S(2)}, u32[]{:S(2)}) %collective-permute-start.25) | collective-permute-done | bytes 65568 | tf_op jit(solution)/shard_map/ppermute | solution.py:735
  146.6 7.9 %end_back_kernel.1 = (bf16[256,2048]{1,0:T(8,128)(2,1)}, bf16[256,256]{1,0:T(8,128)(2,1)}, f32[256,32]{1,0:T(8,128)S(1)}, f32[2048,128]{1,0:T(8,128)}, f32[1,2176]{1,0:T(1,128)S(1)}) custom-call(s32[4]{0:T(128)S(1)} %pad_add_fusion.refs_0_.place_ref, bf16[256,2048]{1,0:T(8,128)(2,1)S(1)} %copy-done.7, bf16[256,256]{1,0:T(8,128)(2,1)S(1)} %copy-done.15, ...), custom_call_target="tpu_custom_call" | custom-call | flops 28000000000 | bytes 9987712 | tf_op jit(solution)/shard_map/end_back_kernel/pallas_call | solution.py:480
  159.4 2.6 %collective-permute-done.31 = f32[1,2176]{1,0:T(1,128)S(1)} collective-permute-done((f32[1,2176]{1,0:T(1,128)S(1)}, f32[1,2176]{1,0:T(1,128)S(1)}, u32[]{:S(2)}, u32[]{:S(2)}) %collective-permute-start.31) | collective-permute-done | bytes 8736 | tf_op jit(solution)/shard_map/ppermute | solution.py:735
  162.8 5.0 %collective-permute-start.35 = (f32[1,2176]{1,0:T(1,128)S(1)}, f32[1,2176]{1,0:T(1,128)S(1)}, u32[]{:S(2)}, u32[]{:S(2)}) collective-permute-start(f32[1,2176]{1,0:T(1,128)S(1)} %add_add_fusion.1), channel_id=1, source_target_pairs={{0,96},{4,100},{8,104},{12,108},{16,112},{20,116},{24,120},{28,124... | collective-permute-start | bytes 26120 | tf_op jit(solution)/shard_map/ppermute | solution.py:735
  170.1 2.8 %collective-permute-done.34 = f32[1,2176]{1,0:T(1,128)S(1)} collective-permute-done((f32[1,2176]{1,0:T(1,128)S(1)}, f32[1,2176]{1,0:T(1,128)S(1)}, u32[]{:S(2)}, u32[]{:S(2)}) %collective-permute-start.34) | collective-permute-done | bytes 8736 | tf_op jit(solution)/shard_map/ppermute | solution.py:735
  (136 shorter events, 59.1 us)
Async XLA Ops:
  7.2 39.5 %all-gather.2.cloned.1.call-start = ((), (), s32[]{:S(2)}) async-start(), calls=%async_computation.1 | async-start | bytes 2621440 | tf_op jit(solution)/shard_map/all_gather | solution.py:762
  13.3 160.9 %reduce-scatter.2.cloned.1.call-start = ((), (), s32[]{:S(2)}) async-start(), calls=%async_computation.2 | async-start | bytes 8912896 | tf_op jit(solution)/shard_map/reduce_scatter | solution.py:769
  13.4 10.7 %collective-permute-start.6 = (bf16[128,1024]{1,0:T(8,128)(2,1)S(1)}, bf16[128,1024]{1,0:T(8,128)(2,1)S(1)}, u32[]{:S(2)}, u32[]{:S(2)}) collective-permute-start(bf16[128,1024]{1,0:T(8,128)(2,1)S(1)} %get-tuple-element.138.refs_4_), channel_id=1, source_target_pairs={{0,64},{4,68},{8,72},{12,76},{16,80},{20,84},{24,88},{28,92},{32,9... | collective-permute-start | bytes 786440 | tf_op jit(solution)/shard_map/ppermute | solution.py:735
  16.8 18.6 %collective-permute-start.5 = (bf16[128,1024]{1,0:T(8,128)(2,1)S(1)}, bf16[128,1024]{1,0:T(8,128)(2,1)S(1)}, u32[]{:S(2)}, u32[]{:S(2)}) collective-permute-start(bf16[128,1024]{1,0:T(8,128)(2,1)S(1)} %get-tuple-element.138.refs_4_), channel_id=1, source_target_pairs={{0,96},{4,100},{8,104},{12,108},{16,112},{20,116},{24,120},{28,124... | collective-permute-start | bytes 786440 | tf_op jit(solution)/shard_map/ppermute | solution.py:735
  17.8 17.6 %collective-permute-start.4 = (bf16[128,1024]{1,0:T(8,128)(2,1)S(1)}, bf16[128,1024]{1,0:T(8,128)(2,1)S(1)}, u32[]{:S(2)}, u32[]{:S(2)}) collective-permute-start(bf16[128,1024]{1,0:T(8,128)(2,1)S(1)} %get-tuple-element.138.refs_4_), channel_id=1, source_target_pairs={{0,32},{4,36},{8,40},{12,44},{16,48},{20,52},{24,56},{28,60},{32,6... | collective-permute-start | bytes 786440 | tf_op jit(solution)/shard_map/ppermute | solution.py:735
  18.8 16.7 %collective-permute-start.3 = (bf16[128,1024]{1,0:T(8,128)(2,1)S(1)}, bf16[128,1024]{1,0:T(8,128)(2,1)S(1)}, u32[]{:S(2)}, u32[]{:S(2)}) collective-permute-start(bf16[128,1024]{1,0:T(8,128)(2,1)S(1)} %get-tuple-element.139.refs_0_), channel_id=1, source_target_pairs={{0,16},{4,20},{8,24},{12,28},{16,0},{20,4},{24,8},{28,12},{32,48},... | collective-permute-start | bytes 786440 | tf_op jit(solution)/shard_map/ppermute | solution.py:735
  22.7 12.8 %collective-permute-start.2 = (bf16[128,1024]{1,0:T(8,128)(2,1)S(1)}, bf16[128,1024]{1,0:T(8,128)(2,1)S(1)}, u32[]{:S(2)}, u32[]{:S(2)}) collective-permute-start(bf16[128,1024]{1,0:T(8,128)(2,1)S(1)} %get-tuple-element.139.refs_0_), channel_id=1, source_target_pairs={{0,24},{4,28},{8,0},{12,4},{16,8},{20,12},{24,16},{28,20},{32,56},... | collective-permute-start | bytes 786440 | tf_op jit(solution)/shard_map/ppermute | solution.py:735
  24.1 11.3 %collective-permute-start.1 = (bf16[128,1024]{1,0:T(8,128)(2,1)S(1)}, bf16[128,1024]{1,0:T(8,128)(2,1)S(1)}, u32[]{:S(2)}, u32[]{:S(2)}) collective-permute-start(bf16[128,1024]{1,0:T(8,128)(2,1)S(1)} %get-tuple-element.139.refs_0_), channel_id=1, source_target_pairs={{0,8},{4,12},{8,16},{12,20},{16,24},{20,28},{24,0},{28,4},{32,40},... | collective-permute-start | bytes 786440 | tf_op jit(solution)/shard_map/ppermute | solution.py:735
  35.3 6.9 %collective-permute-start.11 = (bf16[256,2048]{1,0:T(8,128)(2,1)}, bf16[256,2048]{1,0:T(8,128)(2,1)S(1)}, u32[]{:S(2)}, u32[]{:S(2)}) collective-permute-start(bf16[256,2048]{1,0:T(8,128)(2,1)} %get-tuple-element.76.own_ref), channel_id=1, source_target_pairs={{0,4},{4,0},{8,12},{12,8},{16,20},{20,16},{24,28},{28,24},{32,36},... | collective-permute-start | bytes 3145736 | tf_op jit(solution)/shard_map/ppermute | solution.py:735
  36.9 26.4 %collective-permute-start.10 = (bf16[512,1024]{1,0:T(8,128)(2,1)}, bf16[512,1024]{1,0:T(8,128)(2,1)S(1)}, u32[]{:S(2)}, u32[]{:S(2)}) collective-permute-start(bf16[512,1024]{1,0:T(8,128)(2,1)} %get-tuple-element.75.own_ref), channel_id=1, source_target_pairs={{0,96},{4,100},{8,104},{12,108},{16,112},{20,116},{24,120},{28,124... | collective-permute-start | bytes 3145736 | tf_op jit(solution)/shard_map/ppermute | solution.py:735
  40.0 26.7 %collective-permute-start.9 = (bf16[512,1024]{1,0:T(8,128)(2,1)}, bf16[512,1024]{1,0:T(8,128)(2,1)S(1)}, u32[]{:S(2)}, u32[]{:S(2)}) collective-permute-start(bf16[512,1024]{1,0:T(8,128)(2,1)} %get-tuple-element.75.own_ref), channel_id=1, source_target_pairs={{0,32},{4,36},{8,40},{12,44},{16,48},{20,52},{24,56},{28,60},{32,6... | collective-permute-start | bytes 3145736 | tf_op jit(solution)/shard_map/ppermute | solution.py:735
  40.0 33.8 %collective-permute-start.8 = (bf16[512,1024]{1,0:T(8,128)(2,1)}, bf16[512,1024]{1,0:T(8,128)(2,1)S(1)}, u32[]{:S(2)}, u32[]{:S(2)}) collective-permute-start(bf16[512,1024]{1,0:T(8,128)(2,1)} %get-tuple-element.74.own_ref), channel_id=1, source_target_pairs={{0,24},{4,28},{8,0},{12,4},{16,8},{20,12},{24,16},{28,20},{32,56},... | collective-permute-start | bytes 3145736 | tf_op jit(solution)/shard_map/ppermute | solution.py:735
  42.2 31.6 %collective-permute-start.7 = (bf16[512,1024]{1,0:T(8,128)(2,1)}, bf16[512,1024]{1,0:T(8,128)(2,1)}, u32[]{:S(2)}, u32[]{:S(2)}) collective-permute-start(bf16[512,1024]{1,0:T(8,128)(2,1)} %get-tuple-element.74.own_ref), channel_id=1, source_target_pairs={{0,8},{4,12},{8,16},{12,20},{16,24},{20,28},{24,0},{28,4},{32,40},... | collective-permute-start | bytes 3145736 | tf_op jit(solution)/shard_map/ppermute | solution.py:735
  70.5 25.5 %collective-permute-start.14 = (bf16[256,1024]{1,0:T(8,128)(2,1)S(1)}, bf16[256,1024]{1,0:T(8,128)(2,1)S(1)}, u32[]{:S(2)}, u32[]{:S(2)}) collective-permute-start(bf16[256,1024]{1,0:T(8,128)(2,1)S(1)} %get-tuple-element.79), channel_id=1, source_target_pairs={{0,32},{4,36},{8,40},{12,44},{16,48},{20,52},{24,56},{28,60},{32,6... | collective-permute-start | bytes 1572872 | tf_op jit(solution)/shard_map/ppermute | solution.py:735
  70.6 25.5 %collective-permute-start.15 = (bf16[256,1024]{1,0:T(8,128)(2,1)S(1)}, bf16[256,1024]{1,0:T(8,128)(2,1)S(1)}, u32[]{:S(2)}, u32[]{:S(2)}) collective-permute-start(bf16[256,1024]{1,0:T(8,128)(2,1)S(1)} %get-tuple-element.80), channel_id=1, source_target_pairs={{0,96},{4,100},{8,104},{12,108},{16,112},{20,116},{24,120},{28,124... | collective-permute-start | bytes 1572872 | tf_op jit(solution)/shard_map/ppermute | solution.py:735
  75.1 23.8 %collective-permute-start.13 = (bf16[256,1024]{1,0:T(8,128)(2,1)S(1)}, bf16[256,1024]{1,0:T(8,128)(2,1)S(1)}, u32[]{:S(2)}, u32[]{:S(2)}) collective-permute-start(bf16[256,1024]{1,0:T(8,128)(2,1)S(1)} %get-tuple-element.78), channel_id=1, source_target_pairs={{0,24},{4,28},{8,0},{12,4},{16,8},{20,12},{24,16},{28,20},{32,56},... | collective-permute-start | bytes 1572872 | tf_op jit(solution)/shard_map/ppermute | solution.py:735
  77.5 25.2 %collective-permute-start.12 = (bf16[256,1024]{1,0:T(8,128)(2,1)S(1)}, bf16[256,1024]{1,0:T(8,128)(2,1)S(1)}, u32[]{:S(2)}, u32[]{:S(2)}) collective-permute-start(bf16[256,1024]{1,0:T(8,128)(2,1)S(1)} %get-tuple-element.77.refs_0_), channel_id=1, source_target_pairs={{0,8},{4,12},{8,16},{12,20},{16,24},{20,28},{24,0},{28,4},{32,40},... | collective-permute-start | bytes 1572872 | tf_op jit(solution)/shard_map/ppermute | solution.py:735
  97.7 6.9 %collective-permute-start.17 = (bf16[256,1024]{1,0:T(8,128)(2,1)S(1)}, bf16[256,1024]{1,0:T(8,128)(2,1)S(1)}, u32[]{:S(2)}, u32[]{:S(2)}) collective-permute-start(bf16[256,1024]{1,0:T(8,128)(2,1)S(1)} %get-tuple-element.85), channel_id=1, source_target_pairs={{0,4},{4,0},{8,12},{12,8},{16,20},{20,16},{24,28},{28,24},{32,36},... | collective-permute-start | bytes 1572872 | tf_op jit(solution)/shard_map/ppermute | solution.py:735
  114.5 8.0 %collective-permute-start.20 = (bf16[272,128]{1,0:T(8,128)(2,1)S(1)}, bf16[272,128]{1,0:T(8,128)(2,1)S(1)}, u32[]{:S(2)}, u32[]{:S(2)}) collective-permute-start(bf16[272,128]{1,0:T(8,128)(2,1)S(1)} %get-tuple-element.92), channel_id=1, source_target_pairs={{0,16},{4,20},{8,24},{12,28},{16,0},{20,4},{24,8},{28,12},{32,48},... | collective-permute-start | bytes 208904 | tf_op jit(solution)/shard_map/ppermute | solution.py:735
  114.7 9.0 %collective-permute-start.21 = (bf16[272,128]{1,0:T(8,128)(2,1)S(1)}, bf16[272,128]{1,0:T(8,128)(2,1)S(1)}, u32[]{:S(2)}, u32[]{:S(2)}) collective-permute-start(bf16[272,128]{1,0:T(8,128)(2,1)S(1)} %get-tuple-element.93), channel_id=1, source_target_pairs={{0,8},{4,12},{8,16},{12,20},{16,24},{20,28},{24,0},{28,4},{32,40},... | collective-permute-start | bytes 208904 | tf_op jit(solution)/shard_map/ppermute | solution.py:735
  124.3 8.4 %collective-permute-start.24 = (bf16[272,128]{1,0:T(8,128)(2,1)S(1)}, bf16[272,128]{1,0:T(8,128)(2,1)S(1)}, u32[]{:S(2)}, u32[]{:S(2)}) collective-permute-start(bf16[272,128]{1,0:T(8,128)(2,1)S(1)} %get-tuple-element.95.refs_8_), channel_id=1, source_target_pairs={{96,0},{100,4},{104,8},{108,12},{112,16},{116,20},{120,24},{124,28... | collective-permute-start | bytes 208904 | tf_op jit(solution)/shard_map/ppermute | solution.py:735
  125.6 7.7 %collective-permute-start.23 = (bf16[272,128]{1,0:T(8,128)(2,1)S(1)}, bf16[272,128]{1,0:T(8,128)(2,1)S(1)}, u32[]{:S(2)}, u32[]{:S(2)}) collective-permute-start(bf16[272,128]{1,0:T(8,128)(2,1)S(1)} %get-tuple-element.95.refs_8_), channel_id=1, source_target_pairs={{64,0},{68,4},{72,8},{76,12},{80,16},{84,20},{88,24},{92,28},{96,3... | collective-permute-start | bytes 208904 | tf_op jit(solution)/shard_map/ppermute | solution.py:735
  134.1 8.5 %collective-permute-start.26 = (bf16[256,128]{1,0:T(8,128)(2,1)S(1)}, bf16[256,128]{1,0:T(8,128)(2,1)S(1)}, u32[]{:S(2)}, u32[]{:S(2)}) collective-permute-start(bf16[256,128]{1,0:T(8,128)(2,1)S(1)} %get-tuple-element.102), channel_id=1, source_target_pairs={{0,16},{4,20},{8,24},{12,28},{16,0},{20,4},{24,8},{28,12},{32,48},... | collective-permute-start | bytes 196616 | tf_op jit(solution)/shard_map/ppermute | solution.py:735
  162.8 7.3 %collective-permute-start.35 = (f32[1,2176]{1,0:T(1,128)S(1)}, f32[1,2176]{1,0:T(1,128)S(1)}, u32[]{:S(2)}, u32[]{:S(2)}) collective-permute-start(f32[1,2176]{1,0:T(1,128)S(1)} %add_add_fusion.1), channel_id=1, source_target_pairs={{0,96},{4,100},{8,104},{12,108},{16,112},{20,116},{24,120},{28,124... | collective-permute-start | bytes 26120 | tf_op jit(solution)/shard_map/ppermute | solution.py:735
  (38 other events, 186.9 us)
Sparse Core Ops, SparseCore 0:
  13.4 33.2 all-gather.1
  58.2 95.4 reduce-scatter.1

commit v3 on v2

--- a/solution.py
+++ b/solution.py
@@ -21,7 +21,7 @@
 GROUP_PAIRS = PER_GROUP // 2
 STATE_ROWS = PER_GROUP * P_SIZE
 EPSILON = 1e-05
-UNROLL = 4
+UNROLL = 8
 SHORT, LONG = 100000000, 28000000000
 
 f32 = jnp.float32

time: 182 us -> 177 us (0.973)
  Pallas kernels: 55.9 us -> 51.6 us
    pallas_call x13, Pallas kernels: 30.3 us -> 27.1 us  [call(): pl.pallas_call(body, grid=(1,), out_shape=[jax.ShapeDtypeStruct(shape, ki...]
  transfers between devices with their start and end apart: 38 -> 38, of which waited for: 21 -> 20; matrix products, arithmetic and copies ran while one was open for 2% -> 3% of each run, Pallas kernels for 30% -> 29%
where the time goes in v3:
time: 177 us; the launch traced here: 176 us
  Pallas kernels  51.6 us (29%)
  waiting for transfers between devices  50.1 us (28%)
  starting transfers between devices  42.4 us (24%)
  local copies, waits for them, and re-layouts  15.7 us (9%)
  between operations  14.5 us (8%)
  other arithmetic  1.84 us (1%)
    ppermute x36, waiting for transfers between devices, move(): return lax.ppermute(array, 'ctx', pairs)  45.6 us
    ppermute x36, starting transfers between devices, move(): return lax.ppermute(array, 'ctx', pairs)  42.3 us
    pallas_call x13, Pallas kernels, call(): pl.pallas_call(body, grid=(1,), out_shape=[jax.ShapeDtypeStruct(shape, ki...  27.1 us
    unnamed x50, local copies, waits for them, and re-layouts  13 us
    pallas_call x4, Pallas kernels, upstream(): pl.pallas_call(functools.partial(kernel, half), name=f'{kernel.__name__}_...  9.91 us
    pallas_call x1, Pallas kernels, weight_grad(): pl.pallas_call(weight_grad_kernel, name='weight_grad', grid=(CHANNELS //...  7.32 us
    pallas_call x1, Pallas kernels, forward(): pl.pallas_call(body, name='forward', grid=(GROUPS,), out_shape=[jax.Shape...  7.26 us
    all_gather x1, waiting for transfers between devices, per_device(): pieces = lax.all_gather(both, 'head', axis=0, tiled=True)  4.54 us
  transfers between devices with their start and end apart: 38, of which 20 were waited for; matrix products, arithmetic and copies ran while one was open for 3% of the time, Pallas kernels for 29%

profile of v3, /device:TPU:0, one launch (start us, length us, event | category | flops | bytes accessed | tf_op | source)
XLA Modules:
  0.0 176.1 jit_solution(11468553580485605372)
XLA Ops:
  13.4 3.4 %collective-permute-start.6 = (bf16[128,1024]{1,0:T(8,128)(2,1)S(1)}, bf16[128,1024]{1,0:T(8,128)(2,1)S(1)}, u32[]{:S(2)}, u32[]{:S(2)}) collective-permute-start(bf16[128,1024]{1,0:T(8,128)(2,1)S(1)} %get-tuple-element.138.refs_4_), channel_id=1, source_target_pairs={{0,64},{4,68},{8,72},{12,76},{16,80},{20,84},{24,88},{28,92},{32,9... | collective-permute-start | bytes 786440 | tf_op jit(solution)/shard_map/ppermute | solution.py:735
  18.8 3.9 %collective-permute-start.3 = (bf16[128,1024]{1,0:T(8,128)(2,1)S(1)}, bf16[128,1024]{1,0:T(8,128)(2,1)S(1)}, u32[]{:S(2)}, u32[]{:S(2)}) collective-permute-start(bf16[128,1024]{1,0:T(8,128)(2,1)S(1)} %get-tuple-element.139.refs_0_), channel_id=1, source_target_pairs={{0,16},{4,20},{8,24},{12,28},{16,0},{20,4},{24,8},{28,12},{32,48},... | collective-permute-start | bytes 786440 | tf_op jit(solution)/shard_map/ppermute | solution.py:735
  26.9 7.3 %forward.1 = (f32[256,2048]{1,0:T(8,128)}, bf16[256,2048]{1,0:T(8,128)(2,1)}) custom-call(bf16[256,2048]{1,0:T(8,128)(2,1)} %refs_1_.9, bf16[256,2048]{1,0:T(8,128)(2,1)} %refs_4_.3, bf16[256,256]{1,0:T(8,128)(2,1)} %refs_2_.7, bf16[256,256]{1,0:T(8,128)(2,1)} %refs_2_.6, f32[32,256]{1,0:T(8,128)} %bitcast.18, f32[32,256]{1,0:T(8,128)} %copy-done.10, ...), custom_call_target="tpu_custom_call" | custom-call | flops 100000000 | bytes 1024 | tf_op jit(solution)/shard_map/forward/pallas_call | solution.py:516
  36.3 2.5 %collective-permute-start.10 = (bf16[512,1024]{1,0:T(8,128)(2,1)}, bf16[512,1024]{1,0:T(8,128)(2,1)S(1)}, u32[]{:S(2)}, u32[]{:S(2)}) collective-permute-start(bf16[512,1024]{1,0:T(8,128)(2,1)} %get-tuple-element.75.own_ref), channel_id=1, source_target_pairs={{0,96},{4,100},{8,104},{12,108},{16,112},{20,116},{24,120},{28,124... | collective-permute-start | bytes 3145736 | tf_op jit(solution)/shard_map/ppermute | solution.py:735
  42.2 4.5 %all-gather.2.cloned.1.call-done.pieces_ref = bf16[2048,512]{1,0:T(8,128)(2,1)} async-done(((bf16[512,512]{1,0:T(8,128)(2,1)}), bf16[2048,512]{1,0:T(8,128)(2,1)}) %all-gather.2.cloned.1.call-update) | async-done | bytes 2097168 | tf_op jit(solution)/shard_map/all_gather | solution.py:762
  50.7 7.3 %weight_grad.1.refs_2_ = bf16[2048,2048]{1,0:T(8,128)(2,1)} custom-call(bf16[2048,512]{1,0:T(8,128)(2,1)S(1)} %copy-done.1, bf16[256,2048]{1,0:T(8,128)(2,1)S(1)} %copy-done.3, bf16[256,2048]{1,0:T(8,128)(2,1)S(1)} %copy-done.5), custom_call_target="tpu_custom_call" | custom-call | flops 100000000 | bytes 1024 | tf_op jit(solution)/shard_map/weight_grad/pallas_call | solution.py:618
  58.1 4.1 %collective-permute-done.10.down_ref.refs_1_ = bf16[512,1024]{1,0:T(8,128)(2,1)S(1)} collective-permute-done((bf16[512,1024]{1,0:T(8,128)(2,1)}, bf16[512,1024]{1,0:T(8,128)(2,1)S(1)}, u32[]{:S(2)}, u32[]{:S(2)}) %collective-permute-start.10) | collective-permute-done | bytes 1048608 | tf_op jit(solution)/shard_map/ppermute | solution.py:735
  62.2 3.3 %collective-permute-done.9.up_ref.refs_0_ = bf16[512,1024]{1,0:T(8,128)(2,1)S(1)} collective-permute-done((bf16[512,1024]{1,0:T(8,128)(2,1)}, bf16[512,1024]{1,0:T(8,128)(2,1)S(1)}, u32[]{:S(2)}, u32[]{:S(2)}) %collective-permute-start.9) | collective-permute-done | bytes 1048608 | tf_op jit(solution)/shard_map/ppermute | solution.py:735
  65.5 3.8 %copy-done = bf16[2048,2048]{1,0:T(8,128)(2,1)S(1)} copy-done((bf16[2048,2048]{1,0:T(8,128)(2,1)S(1)}, bf16[2048,2048]{1,0:T(8,128)(2,1)}, u32[]{:S(2)}) %copy-start) | copy-done | bytes 8388632
  69.4 3.2 %collective-permute-start.15 = (bf16[256,1024]{1,0:T(8,128)(2,1)S(1)}, bf16[256,1024]{1,0:T(8,128)(2,1)S(1)}, u32[]{:S(2)}, u32[]{:S(2)}) collective-permute-start(bf16[256,1024]{1,0:T(8,128)(2,1)S(1)} %get-tuple-element.80), channel_id=1, source_target_pairs={{0,96},{4,100},{8,104},{12,108},{16,112},{20,116},{24,120},{28,124... | collective-permute-start | bytes 1572872 | tf_op jit(solution)/shard_map/ppermute | solution.py:735
  76.2 3.2 %upstream_near_kernel_0.1.refs_0_.near_ref = f32[512,1024]{1,0:T(8,128)S(1)} custom-call(s32[4]{0:T(128)S(1)} %pad_add_fusion.refs_0_.place_ref, bf16[2048,512]{1,0:T(8,128)(2,1)S(1)} %copy-done.2, bf16[512,1024]{1,0:T(8,128)(2,1)} %get-tuple-element.75.own_ref, bf16[512,1024]{1,0:T(8,128)(2,1)S(1)} %collective-permute-done.9.up_ref.refs_0_, ...), custom_call_target="tpu_custom_call" | custom-call | flops 100000000 | bytes 1024 | tf_op jit(solution)/shard_map/upstream_near_kernel_0/pallas_call | solution.py:688
  79.4 3.4 %upstream_near_kernel_1.1.refs_0_.near_ref = f32[512,1024]{1,0:T(8,128)S(1)} custom-call(s32[4]{0:T(128)S(1)} %pad_add_fusion.refs_0_.place_ref, bf16[2048,512]{1,0:T(8,128)(2,1)S(1)} %copy-done.2, bf16[512,1024]{1,0:T(8,128)(2,1)} %get-tuple-element.74.own_ref, bf16[512,1024]{1,0:T(8,128)(2,1)} %collective-permute-done.7.refs_0_.up_ref, ...), custom_call_target="tpu_custom_call" | custom-call | flops 100000000 | bytes 1024 | tf_op jit(solution)/shard_map/upstream_near_kernel_1/pallas_call | solution.py:688
  82.8 11.9 %collective-permute-done.14.low_ref = bf16[256,1024]{1,0:T(8,128)(2,1)S(1)} collective-permute-done((bf16[256,1024]{1,0:T(8,128)(2,1)S(1)}, bf16[256,1024]{1,0:T(8,128)(2,1)S(1)}, u32[]{:S(2)}, u32[]{:S(2)}) %collective-permute-start.14) | collective-permute-done | bytes 524320 | tf_op jit(solution)/shard_map/ppermute | solution.py:735
  98.7 2.5 %collective-permute-done.12.low_ref = bf16[256,1024]{1,0:T(8,128)(2,1)S(1)} collective-permute-done((bf16[256,1024]{1,0:T(8,128)(2,1)S(1)}, bf16[256,1024]{1,0:T(8,128)(2,1)S(1)}, u32[]{:S(2)}, u32[]{:S(2)}) %collective-permute-start.12) | collective-permute-done | bytes 524320 | tf_op jit(solution)/shard_map/ppermute | solution.py:735
  103.4 2.5 %norm_back_kernel.2 = (bf16[256,1024]{1,0:T(8,128)(2,1)S(1)}, bf16[256,1024]{1,0:T(8,128)(2,1)S(1)}, f32[1,1024]{1,0:T(1,128)S(1)}, f32[1024,128]{1,0:T(8,128)S(1)}, bf16[1056,128]{1,0:T(8,128)(2,1)S(1)}) custom-call(s32[4]{0:T(128)S(1)} %pad_add_fusion.refs_0_.place_ref, f32[256,1024]{1,0:T(8,128)S(1)} %get-tuple-element.81.refs_0_.refs_1_, ...), custom_call_target="tpu_custom_call" | custom-call | flops 28000000000 | bytes 5160960 | tf_op jit(solution)/shard_map/norm_back_kernel/pallas_call | solution.py:480
  105.9 2.5 %norm_back_kernel.3 = (bf16[256,1024]{1,0:T(8,128)(2,1)S(1)}, bf16[256,1024]{1,0:T(8,128)(2,1)S(1)}, f32[1,1024]{1,0:T(1,128)S(1)}, f32[1024,128]{1,0:T(8,128)S(...) custom-call(s32[4]{0:T(128)S(1)} %pad_add_fusion.refs_0_.place_ref, ...), custom_call_target="tpu_custom_call" | custom-call | flops 28000000000 | bytes 5701632 | tf_op jit(solution)/shard_map/norm_back_kernel/pallas_call | solution.py:480
  113.4 4.0 %scan_back_kernel.2 = (f32[256,1024]{1,0:T(8,128)S(1)}, bf16[256,128]{1,0:T(8,128)(2,1)S(1)}, f32[256,128]{1,0:T(8,128)S(1)}, f32[2,16,128]{2,1,0:T(8,128)S(1)},...) custom-call(bf16[256,2048]{1,0:T(8,128)(2,1)S(1)} %copy-done.7, bf16[256,256]{1,0:T(8,128)(2,1)S(1)} %copy-done.15, ...), custom_call_target="tpu_custom_call" | custom-call | flops 28000000000 | bytes 3785216 | tf_op jit(solution)/shard_map/scan_back_kernel/pallas_call | solution.py:480
  124.8 4.0 %scan_back_kernel.3 = (f32[256,1024]{1,0:T(8,128)S(1)}, bf16[256,128]{1,0:T(8,128)(2,1)S(1)}, f32[256,128]{1,0:T(8,128)S(1)}, f32[2,16,128]{2,1,0:T(8,128)S(1)},...) custom-call(bf16[256,2048]{1,0:T(8,128)(2,1)S(1)} %copy-done.7, bf16[256,256]{1,0:T(8,128)(2,1)S(1)} %copy-done.15, ...), custom_call_target="tpu_custom_call" | custom-call | flops 28000000000 | bytes 3785216 | tf_op jit(solution)/shard_map/scan_back_kernel/pallas_call | solution.py:480
  131.6 2.9 %collective-permute-start.26 = (bf16[256,128]{1,0:T(8,128)(2,1)S(1)}, bf16[256,128]{1,0:T(8,128)(2,1)S(1)}, u32[]{:S(2)}, u32[]{:S(2)}) collective-permute-start(bf16[256,128]{1,0:T(8,128)(2,1)S(1)} %get-tuple-element.102), channel_id=1, source_target_pairs={{0,16},{4,20},{8,24},{12,28},{16,0},{20,4},{24,8},{28,12},{32,48},... | collective-permute-start | bytes 196616 | tf_op jit(solution)/shard_map/ppermute | solution.py:735
  142.2 7.4 %end_back_kernel.1 = (bf16[256,2048]{1,0:T(8,128)(2,1)}, bf16[256,256]{1,0:T(8,128)(2,1)}, f32[256,32]{1,0:T(8,128)S(1)}, f32[2048,128]{1,0:T(8,128)}, f32[1,2176]{1,0:T(1,128)S(1)}) custom-call(s32[4]{0:T(128)S(1)} %pad_add_fusion.refs_0_.place_ref, bf16[256,2048]{1,0:T(8,128)(2,1)S(1)} %copy-done.7, bf16[256,256]{1,0:T(8,128)(2,1)S(1)} %copy-done.15, ...), custom_call_target="tpu_custom_call" | custom-call | flops 28000000000 | bytes 9987712 | tf_op jit(solution)/shard_map/end_back_kernel/pallas_call | solution.py:480
  150.7 2.7 %collective-permute-start.32 = (f32[1,2176]{1,0:T(1,128)S(1)}, f32[1,2176]{1,0:T(1,128)S(1)}, u32[]{:S(2)}, u32[]{:S(2)}) collective-permute-start(f32[1,2176]{1,0:T(1,128)S(1)} %add.34), channel_id=1, source_target_pairs={{0,24},{4,28},{8,0},{12,4},{16,8},{20,12},{24,16},{28,20},{32,56},... | collective-permute-start | bytes 26120 | tf_op jit(solution)/shard_map/ppermute | solution.py:735
  155.4 3.2 %collective-permute-done.31 = f32[1,2176]{1,0:T(1,128)S(1)} collective-permute-done((f32[1,2176]{1,0:T(1,128)S(1)}, f32[1,2176]{1,0:T(1,128)S(1)}, u32[]{:S(2)}, u32[]{:S(2)}) %collective-permute-start.31) | collective-permute-done | bytes 8736 | tf_op jit(solution)/shard_map/ppermute | solution.py:735
  158.6 4.4 %collective-permute-start.35 = (f32[1,2176]{1,0:T(1,128)S(1)}, f32[1,2176]{1,0:T(1,128)S(1)}, u32[]{:S(2)}, u32[]{:S(2)}) collective-permute-start(f32[1,2176]{1,0:T(1,128)S(1)} %add_add_fusion.1), channel_id=1, source_target_pairs={{0,96},{4,100},{8,104},{12,108},{16,112},{20,116},{24,120},{28,124... | collective-permute-start | bytes 26120 | tf_op jit(solution)/shard_map/ppermute | solution.py:735
  165.2 2.8 %collective-permute-done.34 = f32[1,2176]{1,0:T(1,128)S(1)} collective-permute-done((f32[1,2176]{1,0:T(1,128)S(1)}, f32[1,2176]{1,0:T(1,128)S(1)}, u32[]{:S(2)}, u32[]{:S(2)}) %collective-permute-start.34) | collective-permute-done | bytes 8736 | tf_op jit(solution)/shard_map/ppermute | solution.py:735
  (136 shorter events, 61.1 us)
Async XLA Ops:
  7.2 39.5 %all-gather.2.cloned.1.call-start = ((), (), s32[]{:S(2)}) async-start(), calls=%async_computation.1 | async-start | bytes 2621440 | tf_op jit(solution)/shard_map/all_gather | solution.py:762
  13.3 156.0 %reduce-scatter.2.cloned.1.call-start = ((), (), s32[]{:S(2)}) async-start(), calls=%async_computation.2 | async-start | bytes 8912896 | tf_op jit(solution)/shard_map/reduce_scatter | solution.py:769
  13.4 10.7 %collective-permute-start.6 = (bf16[128,1024]{1,0:T(8,128)(2,1)S(1)}, bf16[128,1024]{1,0:T(8,128)(2,1)S(1)}, u32[]{:S(2)}, u32[]{:S(2)}) collective-permute-start(bf16[128,1024]{1,0:T(8,128)(2,1)S(1)} %get-tuple-element.138.refs_4_), channel_id=1, source_target_pairs={{0,64},{4,68},{8,72},{12,76},{16,80},{20,84},{24,88},{28,92},{32,9... | collective-permute-start | bytes 786440 | tf_op jit(solution)/shard_map/ppermute | solution.py:735
  16.8 17.4 %collective-permute-start.5 = (bf16[128,1024]{1,0:T(8,128)(2,1)S(1)}, bf16[128,1024]{1,0:T(8,128)(2,1)S(1)}, u32[]{:S(2)}, u32[]{:S(2)}) collective-permute-start(bf16[128,1024]{1,0:T(8,128)(2,1)S(1)} %get-tuple-element.138.refs_4_), channel_id=1, source_target_pairs={{0,96},{4,100},{8,104},{12,108},{16,112},{20,116},{24,120},{28,124... | collective-permute-start | bytes 786440 | tf_op jit(solution)/shard_map/ppermute | solution.py:735
  17.8 16.4 %collective-permute-start.4 = (bf16[128,1024]{1,0:T(8,128)(2,1)S(1)}, bf16[128,1024]{1,0:T(8,128)(2,1)S(1)}, u32[]{:S(2)}, u32[]{:S(2)}) collective-permute-start(bf16[128,1024]{1,0:T(8,128)(2,1)S(1)} %get-tuple-element.138.refs_4_), channel_id=1, source_target_pairs={{0,32},{4,36},{8,40},{12,44},{16,48},{20,52},{24,56},{28,60},{32,6... | collective-permute-start | bytes 786440 | tf_op jit(solution)/shard_map/ppermute | solution.py:735
  18.8 15.5 %collective-permute-start.3 = (bf16[128,1024]{1,0:T(8,128)(2,1)S(1)}, bf16[128,1024]{1,0:T(8,128)(2,1)S(1)}, u32[]{:S(2)}, u32[]{:S(2)}) collective-permute-start(bf16[128,1024]{1,0:T(8,128)(2,1)S(1)} %get-tuple-element.139.refs_0_), channel_id=1, source_target_pairs={{0,16},{4,20},{8,24},{12,28},{16,0},{20,4},{24,8},{28,12},{32,48},... | collective-permute-start | bytes 786440 | tf_op jit(solution)/shard_map/ppermute | solution.py:735
  22.7 12.2 %collective-permute-start.2 = (bf16[128,1024]{1,0:T(8,128)(2,1)S(1)}, bf16[128,1024]{1,0:T(8,128)(2,1)S(1)}, u32[]{:S(2)}, u32[]{:S(2)}) collective-permute-start(bf16[128,1024]{1,0:T(8,128)(2,1)S(1)} %get-tuple-element.139.refs_0_), channel_id=1, source_target_pairs={{0,24},{4,28},{8,0},{12,4},{16,8},{20,12},{24,16},{28,20},{32,56},... | collective-permute-start | bytes 786440 | tf_op jit(solution)/shard_map/ppermute | solution.py:735
  24.1 10.7 %collective-permute-start.1 = (bf16[128,1024]{1,0:T(8,128)(2,1)S(1)}, bf16[128,1024]{1,0:T(8,128)(2,1)S(1)}, u32[]{:S(2)}, u32[]{:S(2)}) collective-permute-start(bf16[128,1024]{1,0:T(8,128)(2,1)S(1)} %get-tuple-element.139.refs_0_), channel_id=1, source_target_pairs={{0,8},{4,12},{8,16},{12,20},{16,24},{20,28},{24,0},{28,4},{32,40},... | collective-permute-start | bytes 786440 | tf_op jit(solution)/shard_map/ppermute | solution.py:735
  34.2 7.0 %collective-permute-start.11 = (bf16[256,2048]{1,0:T(8,128)(2,1)}, bf16[256,2048]{1,0:T(8,128)(2,1)S(1)}, u32[]{:S(2)}, u32[]{:S(2)}) collective-permute-start(bf16[256,2048]{1,0:T(8,128)(2,1)} %get-tuple-element.76.own_ref), channel_id=1, source_target_pairs={{0,4},{4,0},{8,12},{12,8},{16,20},{20,16},{24,28},{28,24},{32,36},... | collective-permute-start | bytes 3145736 | tf_op jit(solution)/shard_map/ppermute | solution.py:735
  36.3 25.9 %collective-permute-start.10 = (bf16[512,1024]{1,0:T(8,128)(2,1)}, bf16[512,1024]{1,0:T(8,128)(2,1)S(1)}, u32[]{:S(2)}, u32[]{:S(2)}) collective-permute-start(bf16[512,1024]{1,0:T(8,128)(2,1)} %get-tuple-element.75.own_ref), channel_id=1, source_target_pairs={{0,96},{4,100},{8,104},{12,108},{16,112},{20,116},{24,120},{28,124... | collective-permute-start | bytes 3145736 | tf_op jit(solution)/shard_map/ppermute | solution.py:735
  38.8 26.7 %collective-permute-start.9 = (bf16[512,1024]{1,0:T(8,128)(2,1)}, bf16[512,1024]{1,0:T(8,128)(2,1)S(1)}, u32[]{:S(2)}, u32[]{:S(2)}) collective-permute-start(bf16[512,1024]{1,0:T(8,128)(2,1)} %get-tuple-element.75.own_ref), channel_id=1, source_target_pairs={{0,32},{4,36},{8,40},{12,44},{16,48},{20,52},{24,56},{28,60},{32,6... | collective-permute-start | bytes 3145736 | tf_op jit(solution)/shard_map/ppermute | solution.py:735
  38.8 33.8 %collective-permute-start.8 = (bf16[512,1024]{1,0:T(8,128)(2,1)}, bf16[512,1024]{1,0:T(8,128)(2,1)S(1)}, u32[]{:S(2)}, u32[]{:S(2)}) collective-permute-start(bf16[512,1024]{1,0:T(8,128)(2,1)} %get-tuple-element.74.own_ref), channel_id=1, source_target_pairs={{0,24},{4,28},{8,0},{12,4},{16,8},{20,12},{24,16},{28,20},{32,56},... | collective-permute-start | bytes 3145736 | tf_op jit(solution)/shard_map/ppermute | solution.py:735
  41.2 31.5 %collective-permute-start.7 = (bf16[512,1024]{1,0:T(8,128)(2,1)}, bf16[512,1024]{1,0:T(8,128)(2,1)}, u32[]{:S(2)}, u32[]{:S(2)}) collective-permute-start(bf16[512,1024]{1,0:T(8,128)(2,1)} %get-tuple-element.74.own_ref), channel_id=1, source_target_pairs={{0,8},{4,12},{8,16},{12,20},{16,24},{20,28},{24,0},{28,4},{32,40},... | collective-permute-start | bytes 3145736 | tf_op jit(solution)/shard_map/ppermute | solution.py:735
  69.3 25.4 %collective-permute-start.14 = (bf16[256,1024]{1,0:T(8,128)(2,1)S(1)}, bf16[256,1024]{1,0:T(8,128)(2,1)S(1)}, u32[]{:S(2)}, u32[]{:S(2)}) collective-permute-start(bf16[256,1024]{1,0:T(8,128)(2,1)S(1)} %get-tuple-element.79), channel_id=1, source_target_pairs={{0,32},{4,36},{8,40},{12,44},{16,48},{20,52},{24,56},{28,60},{32,6... | collective-permute-start | bytes 1572872 | tf_op jit(solution)/shard_map/ppermute | solution.py:735
  69.4 25.3 %collective-permute-start.15 = (bf16[256,1024]{1,0:T(8,128)(2,1)S(1)}, bf16[256,1024]{1,0:T(8,128)(2,1)S(1)}, u32[]{:S(2)}, u32[]{:S(2)}) collective-permute-start(bf16[256,1024]{1,0:T(8,128)(2,1)S(1)} %get-tuple-element.80), channel_id=1, source_target_pairs={{0,96},{4,100},{8,104},{12,108},{16,112},{20,116},{24,120},{28,124... | collective-permute-start | bytes 1572872 | tf_op jit(solution)/shard_map/ppermute | solution.py:735
  74.0 24.7 %collective-permute-start.13 = (bf16[256,1024]{1,0:T(8,128)(2,1)S(1)}, bf16[256,1024]{1,0:T(8,128)(2,1)S(1)}, u32[]{:S(2)}, u32[]{:S(2)}) collective-permute-start(bf16[256,1024]{1,0:T(8,128)(2,1)S(1)} %get-tuple-element.78), channel_id=1, source_target_pairs={{0,24},{4,28},{8,0},{12,4},{16,8},{20,12},{24,16},{28,20},{32,56},... | collective-permute-start | bytes 1572872 | tf_op jit(solution)/shard_map/ppermute | solution.py:735
  76.2 25.1 %collective-permute-start.12 = (bf16[256,1024]{1,0:T(8,128)(2,1)S(1)}, bf16[256,1024]{1,0:T(8,128)(2,1)S(1)}, u32[]{:S(2)}, u32[]{:S(2)}) collective-permute-start(bf16[256,1024]{1,0:T(8,128)(2,1)S(1)} %get-tuple-element.77.refs_0_), channel_id=1, source_target_pairs={{0,8},{4,12},{8,16},{12,20},{16,24},{20,28},{24,0},{28,4},{32,40},... | collective-permute-start | bytes 1572872 | tf_op jit(solution)/shard_map/ppermute | solution.py:735
  96.4 6.6 %collective-permute-start.17 = (bf16[256,1024]{1,0:T(8,128)(2,1)S(1)}, bf16[256,1024]{1,0:T(8,128)(2,1)S(1)}, u32[]{:S(2)}, u32[]{:S(2)}) collective-permute-start(bf16[256,1024]{1,0:T(8,128)(2,1)S(1)} %get-tuple-element.85), channel_id=1, source_target_pairs={{0,4},{4,0},{8,12},{12,8},{16,20},{20,16},{24,28},{28,24},{32,36},... | collective-permute-start | bytes 1572872 | tf_op jit(solution)/shard_map/ppermute | solution.py:735
  111.0 7.9 %collective-permute-start.20 = (bf16[272,128]{1,0:T(8,128)(2,1)S(1)}, bf16[272,128]{1,0:T(8,128)(2,1)S(1)}, u32[]{:S(2)}, u32[]{:S(2)}) collective-permute-start(bf16[272,128]{1,0:T(8,128)(2,1)S(1)} %get-tuple-element.92), channel_id=1, source_target_pairs={{0,16},{4,20},{8,24},{12,28},{16,0},{20,4},{24,8},{28,12},{32,48},... | collective-permute-start | bytes 208904 | tf_op jit(solution)/shard_map/ppermute | solution.py:735
  112.0 8.2 %collective-permute-start.21 = (bf16[272,128]{1,0:T(8,128)(2,1)S(1)}, bf16[272,128]{1,0:T(8,128)(2,1)S(1)}, u32[]{:S(2)}, u32[]{:S(2)}) collective-permute-start(bf16[272,128]{1,0:T(8,128)(2,1)S(1)} %get-tuple-element.93), channel_id=1, source_target_pairs={{0,8},{4,12},{8,16},{12,20},{16,24},{20,28},{24,0},{28,4},{32,40},... | collective-permute-start | bytes 208904 | tf_op jit(solution)/shard_map/ppermute | solution.py:735
  120.9 9.6 %collective-permute-start.24 = (bf16[272,128]{1,0:T(8,128)(2,1)S(1)}, bf16[272,128]{1,0:T(8,128)(2,1)S(1)}, u32[]{:S(2)}, u32[]{:S(2)}) collective-permute-start(bf16[272,128]{1,0:T(8,128)(2,1)S(1)} %get-tuple-element.95.refs_8_), channel_id=1, source_target_pairs={{96,0},{100,4},{104,8},{108,12},{112,16},{116,20},{120,24},{124,28... | collective-permute-start | bytes 208904 | tf_op jit(solution)/shard_map/ppermute | solution.py:735
  122.2 8.3 %collective-permute-start.23 = (bf16[272,128]{1,0:T(8,128)(2,1)S(1)}, bf16[272,128]{1,0:T(8,128)(2,1)S(1)}, u32[]{:S(2)}, u32[]{:S(2)}) collective-permute-start(bf16[272,128]{1,0:T(8,128)(2,1)S(1)} %get-tuple-element.95.refs_8_), channel_id=1, source_target_pairs={{64,0},{68,4},{72,8},{76,12},{80,16},{84,20},{88,24},{92,28},{96,3... | collective-permute-start | bytes 208904 | tf_op jit(solution)/shard_map/ppermute | solution.py:735
  123.5 7.0 %collective-permute-start.22 = (bf16[272,128]{1,0:T(8,128)(2,1)S(1)}, bf16[272,128]{1,0:T(8,128)(2,1)S(1)}, u32[]{:S(2)}, u32[]{:S(2)}) collective-permute-start(bf16[272,128]{1,0:T(8,128)(2,1)S(1)} %get-tuple-element.95.refs_8_), channel_id=1, source_target_pairs={{32,0},{36,4},{40,8},{44,12},{48,16},{52,20},{56,24},{60,28},{64,3... | collective-permute-start | bytes 208904 | tf_op jit(solution)/shard_map/ppermute | solution.py:735
  158.6 6.7 %collective-permute-start.35 = (f32[1,2176]{1,0:T(1,128)S(1)}, f32[1,2176]{1,0:T(1,128)S(1)}, u32[]{:S(2)}, u32[]{:S(2)}) collective-permute-start(f32[1,2176]{1,0:T(1,128)S(1)} %add_add_fusion.1), channel_id=1, source_target_pairs={{0,96},{4,100},{8,104},{12,108},{16,112},{20,116},{24,120},{28,124... | collective-permute-start | bytes 26120 | tf_op jit(solution)/shard_map/ppermute | solution.py:735
  (38 other events, 180.3 us)
Sparse Core Ops, SparseCore 0:
  13.4 33.2 all-gather.1
  58.2 94.4 reduce-scatter.1
